TPU v7x, 32 devices: a whole 2x2x4 slice. The times are simulated.
32 devices in a mesh: dp: 4 (over z), expert: 4 (over x, core), tensor: 2 (over y).
Axes of the slice: x: 2, y: 2, z: 4, core: 2. Of those that a mesh axis runs over, the one named last changes fastest.
Arguments:
- tokens: bfloat16 [2048, 2048], P(('dp', 'expert')), may hold values from -6 to 6
- cotangent: bfloat16 [2048, 2048], P(('dp', 'expert')), may hold values from -6 to 6
- scores: float32 [2048, 8], P(('dp', 'expert')), may hold values from 0.05 to 1
- routes: int32 [2048, 1], P(('dp', 'expert')), may hold values from 0 to 7; in each aligned block of 128 rows (0 to 127, 128 to 255, ...) at most 32 rows name the same one
- w_gate: bfloat16 [8, 2048, 768], P('expert', 'dp', 'tensor'), may hold values from -0.125 to 0.125
- w_up: bfloat16 [8, 2048, 768], P('expert', 'dp', 'tensor'), may hold values from -0.125 to 0.125
- w_down: bfloat16 [8, 768, 2048], P('expert', 'tensor', 'dp'), may hold values from -0.21875 to 0.21875
Outputs:
- output: bfloat16 [2048, 2048], P(('dp', 'expert'), 'tensor')
- grad_tokens: bfloat16 [2048, 2048], P(('dp', 'expert'), 'tensor')
- grad_gate: float32 [8, 2048, 768], P('expert', 'dp', 'tensor')
- grad_up: float32 [8, 2048, 768], P('expert', 'dp', 'tensor')
- grad_down: float32 [8, 768, 2048], P('expert', 'tensor', 'dp')
Inputs may be any that keep to these rules, and one draw needn't show every extreme that they name: `routes`: each row names 1 different experts. Among the rows of one token block no expert is named more than 32 times, and 32 is reached.
All inputs are finite; a program needn't handle non-finite values.
Results may differ from a plain program's by a relative error of at most 0.019.
Values may be sent and summed in bfloat16 or wider, within the bound.
No kernel may reach another device: no remote copies, remote signals or barrier semaphores. Data moves between devices by JAX's collectives and lax.ppermute only.
A program may use at most 64 MiB of HBM per device.

v0:
```python
import jax
import jax.numpy as jnp
from jax import lax
from jax.sharding import PartitionSpec as P


def slot_onehot(route_block, expert_count, capacity):
    flat = route_block.reshape(-1)
    member = (flat[:, None] == jnp.arange(expert_count, dtype=jnp.int32)[None, :]).astype(jnp.int32)
    before = jnp.cumsum(member, axis=0) - member
    place = jnp.sum(before * member, axis=1)
    slot_ids = flat * capacity + place
    return slot_ids[:, None] == jnp.arange(expert_count * capacity, dtype=jnp.int32)[None, :]


def on_device(tokens, cotangent, scores, routes, w_gate, w_up, w_down):
    highest = lax.Precision.HIGHEST
    tok_count = tokens.shape[0]
    model_width = tokens.shape[1]
    flight_count = routes.shape[1]
    owners = lax.axis_size("expert")
    local_count = w_gate.shape[0]
    expert_count = local_count * owners
    capacity = min(tok_count, 2 * tok_count * flight_count // expert_count)
    slot_total = expert_count * capacity
    table = slot_onehot(routes, expert_count, capacity)
    picker = table.astype(jnp.bfloat16)
    mix = (scores / jnp.sum(scores, axis=1, keepdims=True))[:, :flight_count]
    rep_x = jnp.repeat(tokens, flight_count, axis=0)
    rep_d = (mix[:, :, None] * cotangent.astype(jnp.float32)[:, None, :]).astype(jnp.bfloat16)
    rep_d = rep_d.reshape(tok_count * flight_count, model_width)
    send_x = jnp.einsum("rs,rd->sd", picker, rep_x, preferred_element_type=jnp.float32).astype(
        jnp.bfloat16
    )
    send_d = jnp.einsum("rs,rd->sd", picker, rep_d, preferred_element_type=jnp.float32).astype(
        jnp.bfloat16
    )
    full_gate, full_up, full_down = (
        lax.all_gather(w_gate, "dp", axis=1, tiled=True),
        lax.all_gather(w_up, "dp", axis=1, tiled=True),
        lax.all_gather(w_down, "dp", axis=2, tiled=True),
    )
    got_x, got_d = (
        lax.all_to_all(send_x, "expert", split_axis=0, concat_axis=0, tiled=True),
        lax.all_to_all(send_d, "expert", split_axis=0, concat_axis=0, tiled=True),
    )
    rows_x = got_x.reshape(owners, local_count, capacity, model_width)
    rows_d = got_d.reshape(owners, local_count, capacity, model_width)
    gate_act = jnp.einsum("oecd,edf->oecf", rows_x, full_gate, preferred_element_type=jnp.float32)
    up_act = jnp.einsum("oecd,edf->oecf", rows_x, full_up, preferred_element_type=jnp.float32)
    sigma = jax.nn.sigmoid(gate_act)
    silu_act = gate_act * sigma
    hidden = (silu_act * up_act).astype(jnp.bfloat16)
    part_out = jnp.einsum("oecf,efd->oecd", hidden, full_down, preferred_element_type=jnp.float32)
    back_grad = jnp.einsum("oecd,efd->oecf", rows_d, full_down, preferred_element_type=jnp.float32)
    grad_act_gate = (back_grad * up_act * sigma * (1.0 + gate_act * (1.0 - sigma))).astype(
        jnp.bfloat16
    )
    grad_act_up = (back_grad * silu_act).astype(jnp.bfloat16)
    part_in = jnp.einsum(
        "oecf,edf->oecd", grad_act_gate, full_gate, preferred_element_type=jnp.float32
    )
    part_in = part_in + jnp.einsum(
        "oecf,edf->oecd", grad_act_up, full_up, preferred_element_type=jnp.float32
    )
    spread = table.reshape(tok_count, flight_count, slot_total).astype(jnp.float32)
    weighted = jnp.einsum("tks,tk->ts", spread, mix, precision=highest)
    plain = jnp.sum(spread, axis=1)
    summed_out, summed_in = (
        lax.psum_scatter(
            part_out.astype(jnp.bfloat16), "tensor", scatter_dimension=3, tiled=True
        ).astype(jnp.float32),
        lax.psum_scatter(
            part_in.astype(jnp.bfloat16), "tensor", scatter_dimension=3, tiled=True
        ).astype(jnp.float32),
    )
    back_out, back_in = (
        lax.all_to_all(
            summed_out.astype(jnp.bfloat16), "expert", split_axis=0, concat_axis=0, tiled=True
        ).astype(summed_out.dtype),
        lax.all_to_all(
            summed_in.astype(jnp.bfloat16), "expert", split_axis=0, concat_axis=0, tiled=True
        ).astype(summed_in.dtype),
    )
    flat_out = back_out.reshape(slot_total, back_out.shape[3])
    flat_in = back_in.reshape(slot_total, back_in.shape[3])
    output = jnp.dot(weighted, flat_out, precision=highest).astype(jnp.bfloat16)
    grad_tokens = jnp.dot(plain, flat_in, precision=highest).astype(jnp.bfloat16)
    term_gate = jnp.einsum(
        "oecd,oecf->edf", rows_x, grad_act_gate, preferred_element_type=jnp.float32
    )
    term_up = jnp.einsum("oecd,oecf->edf", rows_x, grad_act_up, preferred_element_type=jnp.float32)
    term_down = jnp.einsum("oecf,oecd->efd", hidden, rows_d, preferred_element_type=jnp.float32)
    grad_gate, grad_up, grad_down = (
        lax.psum_scatter(
            term_gate.astype(jnp.bfloat16), "dp", scatter_dimension=1, tiled=True
        ).astype(jnp.float32),
        lax.psum_scatter(
            term_up.astype(jnp.bfloat16), "dp", scatter_dimension=1, tiled=True
        ).astype(jnp.float32),
        lax.psum_scatter(
            term_down.astype(jnp.bfloat16), "dp", scatter_dimension=2, tiled=True
        ).astype(jnp.float32),
    )
    return (output, grad_tokens, grad_gate, grad_up, grad_down)


def solution(mesh):
    in_specs = (
        P(("dp", "expert"), None),
        P(("dp", "expert"), None),
        P(("dp", "expert"), None),
        P(("dp", "expert"), None),
        P("expert", "dp", "tensor"),
        P("expert", "dp", "tensor"),
        P("expert", "tensor", "dp"),
    )
    out_specs = (
        P(("dp", "expert"), "tensor"),
        P(("dp", "expert"), "tensor"),
        P("expert", "dp", "tensor"),
        P("expert", "dp", "tensor"),
        P("expert", "tensor", "dp"),
    )
    return jax.shard_map(
        on_device, mesh=mesh, in_specs=in_specs, out_specs=out_specs, check_vma=False
    )
```

profile of v0, /device:TPU:0, one launch (start us, length us, event | category | flops | bytes accessed | tf_op | source)
XLA Modules:
  0.0 450.2 jit_solution(3163455656501832368)
XLA Ops:
  13.2 2.6 convolution_convert_fusion
  15.8 4.2 all-to-all-start.2
  21.5 12.9 %all-to-all-done.2 = bf16[4,64,2048]{2,1,0:T(8,128)(2,1)S(1)} async-done(((bf16[4,64,2048]{2,1,0:T(8,128)(2,1)}), bf16[4,64,2048]{2,1,0:T(8,128)(2,1)S(1)}, u32[]{:S(2)}, u32[]{:S(2)}) %all-to-all-start.2) | async-done | bytes 1048608 | tf_op jit(solution)/shard_map/all_to_all | solution.py:45
  34.5 3.5 all-to-all-start
  38.0 37.7 %all-gather.8.cloned.1.call-done = bf16[2,384,2048]{2,1,0:T(8,128)(2,1)} async-done(((bf16[2,384,512]{2,1,0:T(8,128)(2,1)}), bf16[2,384,2048]{2,1,0:T(8,128)(2,1)}) %all-gather.8.cloned.1.call-update) | async-done | bytes 3145744 | tf_op jit(solution)/shard_map/all_gather | solution.py:41
  75.8 2.9 fusion.27
  78.7 60.8 %all-gather.6.cloned.1.call-done = bf16[2,2048,384]{2,1,0:T(8,128)(2,1)} async-done(((bf16[2,512,384]{2,1,0:T(8,128)(2,1)}), bf16[2,2048,384]{2,1,0:T(8,128)(2,1)}) %all-gather.6.cloned.1.call-update) | async-done | bytes 3145744 | tf_op jit(solution)/shard_map/all_gather | solution.py:40
  139.6 2.6 fusion.33
  142.2 61.2 %all-gather.4.cloned.1.call-done = bf16[2,2048,384]{2,1,0:T(8,128)(2,1)} async-done(((bf16[2,512,384]{2,1,0:T(8,128)(2,1)}), bf16[2,2048,384]{2,1,0:T(8,128)(2,1)}) %all-gather.4.cloned.1.call-update) | async-done | bytes 3145744 | tf_op jit(solution)/shard_map/all_gather | solution.py:39
  203.3 3.6 multiply_convert_fusion.3
  211.1 3.6 fusion.21
  214.8 2.7 bitcast_convert_fusion
  218.4 2.7 bitcast_convert_fusion.2
  222.0 2.7 bitcast_convert_fusion.1
  224.7 5.5 %reduce-scatter.8.cloned.1.call-done = bf16[4,2,32,1024]{3,2,0,1:T(8,128)(2,1)} async-done(((bf16[4,2,32,2048]{3,2,0,1:T(8,128)(2,1)}), bf16[4,2,32,1024]{3,2,0,1:T(8,128)(2,1)}) %reduce-scatter.8.cloned.1.call-update) | async-done | bytes 524304 | tf_op jit(solution)/shard_map/reduce_scatter | solution.py:73
  232.1 3.5 all-to-all-start.3
  235.6 17.8 %reduce-scatter.6.cloned.1.call-done = bf16[4,2,32,1024]{3,2,0,1:T(8,128)(2,1)} async-done(((bf16[4,2,32,2048]{3,2,0,1:T(8,128)(2,1)}), bf16[4,2,32,1024]{3,2,0,1:T(8,128)(2,1)}) %reduce-scatter.6.cloned.1.call-update) | async-done | bytes 524304 | tf_op jit(solution)/shard_map/reduce_scatter | solution.py:70
  255.2 3.5 all-to-all-start.1
  259.6 7.8 %all-to-all-done.1 = bf16[4,2,32,1024]{3,2,1,0:T(8,128)(2,1)S(1)} async-done(((bf16[4,2,32,1024]{3,2,1,0:T(8,128)(2,1)}), bf16[4,2,32,1024]{3,2,1,0:T(8,128)(2,1)S(1)}, u32[]{:S(2)}, u32[]{:S(2)}) %all-to-all-start.1) | async-done | bytes 524320 | tf_op jit(solution)/shard_map/all_to_all | solution.py:78
  268.6 47.2 %reduce-scatter.14.cloned.1.call-done = bf16[2,384,512]{2,1,0:T(8,128)(2,1)} async-done(((bf16[2,384,2048]{2,1,0:T(8,128)(2,1)}), bf16[2,384,512]{2,1,0:T(8,128)(2,1)}) %reduce-scatter.14.cloned.1.call-update) | async-done | bytes 786448 | tf_op jit(solution)/shard_map/reduce_scatter | solution.py:101
  315.8 2.5 convert_element_type.88
  318.2 60.1 %reduce-scatter.10.cloned.1.call-done = bf16[2,512,384]{2,1,0:T(8,128)(2,1)} async-done(((bf16[2,2048,384]{2,1,0:T(8,128)(2,1)}), bf16[2,512,384]{2,1,0:T(8,128)(2,1)}) %reduce-scatter.10.cloned.1.call-update) | async-done | bytes 786448 | tf_op jit(solution)/shard_map/reduce_scatter | solution.py:95
  378.4 2.4 convert_element_type.84
  380.7 60.2 %reduce-scatter.12.cloned.1.call-done = bf16[2,512,384]{2,1,0:T(8,128)(2,1)} async-done(((bf16[2,2048,384]{2,1,0:T(8,128)(2,1)}), bf16[2,512,384]{2,1,0:T(8,128)(2,1)}) %reduce-scatter.12.cloned.1.call-update) | async-done | bytes 786448 | tf_op jit(solution)/shard_map/reduce_scatter | solution.py:98
  (49 shorter events, 21.8 us)
Async XLA Ops:
  7.2 12.8 %copy-start = (bf16[128,2048]{1,0:T(8,128)(2,1)S(1)}, bf16[128,2048]{1,0:T(8,128)(2,1)}, u32[]{:S(2)}) copy-start(bf16[128,2048]{1,0:T(8,128)(2,1)} %param.7) | copy-start | bytes 1572868
  7.2 68.6 %all-gather.8.cloned.1.call-start = ((), (), s32[]{:S(2)}) async-start(), calls=%async_computation.11 | async-start | bytes 3932160 | tf_op jit(solution)/shard_map/all_gather | solution.py:41
  7.9 131.7 %all-gather.6.cloned.1.call-start = ((), (), s32[]{:S(2)}) async-start(), calls=%async_computation.10 | async-start | bytes 3932160 | tf_op jit(solution)/shard_map/all_gather | solution.py:40
  8.7 194.7 %all-gather.4.cloned.1.call-start = ((), (), s32[]{:S(2)}) async-start(), calls=%async_computation.9 | async-start | bytes 3932160 | tf_op jit(solution)/shard_map/all_gather | solution.py:39
  15.8 18.7 %all-to-all-start.2 = ((bf16[4,64,2048]{2,1,0:T(8,128)(2,1)}), bf16[4,64,2048]{2,1,0:T(8,128)(2,1)S(1)}, u32[]{:S(2)}, u32[]{:S(2)}) async-start(bf16[4,64,2048]{2,1,0:T(8,128)(2,1)} %bitcast.17), calls=%async_computation.3 | async-start | bytes 2097152 | tf_op jit(solution)/shard_map/all_to_all | solution.py:45
  34.5 44.3 %all-to-all-start = ((bf16[4,64,2048]{2,1,0:T(8,128)(2,1)}), bf16[4,64,2048]{2,1,0:T(8,128)(2,1)S(1)}, u32[]{:S(2)}, u32[]{:S(2)}) async-start(bf16[4,64,2048]{2,1,0:T(8,128)(2,1)} %bitcast.4), calls=%async_computation | async-start | bytes 2097152 | tf_op jit(solution)/shard_map/all_to_all | solution.py:44
  38.0 192.2 %reduce-scatter.8.cloned.1.call-start = ((), (), s32[]{:S(2)}) async-start(), calls=%async_computation.13 | async-start | bytes 1572864 | tf_op jit(solution)/shard_map/reduce_scatter | solution.py:73
  203.3 3.6 copy-start.1
  206.9 1.1 copy-start.6
  206.9 1.1 copy-start.3
  206.9 2.0 copy-start.2
  208.9 2.1 copy-start.5
  211.0 42.3 %reduce-scatter.6.cloned.1.call-start = ((), (), s32[]{:S(2)}) async-start(), calls=%async_computation.12 | async-start | bytes 1572864 | tf_op jit(solution)/shard_map/reduce_scatter | solution.py:70
  214.7 101.0 %reduce-scatter.14.cloned.1.call-start = ((), (), s32[]{:S(2)}) async-start(), calls=%async_computation.16 | async-start | bytes 3932160 | tf_op jit(solution)/shard_map/reduce_scatter | solution.py:101
  217.5 0.9 copy-start.4
  217.5 160.9 %reduce-scatter.10.cloned.1.call-start = ((), (), s32[]{:S(2)}) async-start(), calls=%async_computation.14 | async-start | bytes 3932160 | tf_op jit(solution)/shard_map/reduce_scatter | solution.py:95
  221.1 0.9 copy-start.7
  221.1 219.9 %reduce-scatter.12.cloned.1.call-start = ((), (), s32[]{:S(2)}) async-start(), calls=%async_computation.15 | async-start | bytes 3932160 | tf_op jit(solution)/shard_map/reduce_scatter | solution.py:98
  232.1 23.1 %all-to-all-start.3 = ((bf16[4,2,32,1024]{3,2,1,0:T(8,128)(2,1)}), bf16[4,2,32,1024]{3,2,1,0:T(8,128)(2,1)S(1)}, u32[]{:S(2)}, u32[]{:S(2)}) async-start(bf16[4,2,32,1024]{3,2,1,0:T(8,128)(2,1)} %copy.24), calls=%async_computation.5 | async-start | bytes 1048576 | tf_op jit(solution)/shard_map/all_to_all | solution.py:81
  255.2 12.3 %all-to-all-start.1 = ((bf16[4,2,32,1024]{3,2,1,0:T(8,128)(2,1)}), bf16[4,2,32,1024]{3,2,1,0:T(8,128)(2,1)S(1)}, u32[]{:S(2)}, u32[]{:S(2)}) async-start(bf16[4,2,32,1024]{3,2,1,0:T(8,128)(2,1)} %copy.22), calls=%async_computation.2 | async-start | bytes 1048576 | tf_op jit(solution)/shard_map/all_to_all | solution.py:78
Sparse Core Ops, SparseCore 0:
  9.6 66.1 all-gather.7
  77.3 62.1 all-gather.5
  141.2 62.1 all-gather.3
  211.2 18.9 reduce-scatter.7
  233.0 20.3 reduce-scatter.5
  255.5 60.2 reduce-scatter.13
  318.1 60.2 reduce-scatter.9
  380.7 60.2 reduce-scatter.11
where the time goes:
time: 451 us; the launch traced here: 450 us
  waiting for transfers between devices  373 us (83%)
  matrix products  30.2 us (7%)
  starting transfers between devices  15 us (3%)
  between operations  14.2 us (3%)
  other arithmetic  11 us (2%)
  local copies, waits for them, and re-layouts  6.36 us (1%)
    all_gather x1, waiting for transfers between devices, on_device(): lax.all_gather(w_gate, 'dp', axis=1, tiled=True)  61.2 us
    all_gather x1, waiting for transfers between devices, on_device(): lax.all_gather(w_up, 'dp', axis=1, tiled=True)  60.8 us
    reduce_scatter x1, waiting for transfers between devices, on_device(): lax.psum_scatter(term_up.astype(jnp.bfloat16), 'dp', scatter_dimension=1,...  60.2 us
    reduce_scatter x1, waiting for transfers between devices, on_device(): lax.psum_scatter(term_gate.astype(jnp.bfloat16), 'dp', scatter_dimension=...  60.1 us
    reduce_scatter x1, waiting for transfers between devices, on_device(): lax.psum_scatter(term_down.astype(jnp.bfloat16), 'dp', scatter_dimension=...  47.2 us
    all_gather x1, waiting for transfers between devices, on_device(): lax.all_gather(w_down, 'dp', axis=2, tiled=True)  37.7 us
    reduce_scatter x1, waiting for transfers between devices, on_device(): lax.psum_scatter(part_out.astype(jnp.bfloat16), 'tensor', scatter_dimensi...  17.8 us
    all_to_all x1, waiting for transfers between devices, on_device(): lax.all_to_all(send_d, 'expert', split_axis=0, concat_axis=0, tiled=True)  12.9 us
  transfers between devices with their start and end apart: 12, of which 10 were waited for; matrix products, arithmetic and copies ran while one was open for 8% of the time, Pallas kernels for 0%

commit v1 on v0

v1 whole, which is shorter than its diff:
```python
import jax
import jax.numpy as jnp
from jax import lax
from jax.sharding import PartitionSpec as P

F32 = jnp.float32
BF16 = jnp.bfloat16


def slots_of(route_block, expert_count, capacity):
    flat = route_block.reshape(-1)
    member = (flat[:, None] == jnp.arange(expert_count, dtype=jnp.int32)[None, :]).astype(jnp.int32)
    before = jnp.cumsum(member, axis=0) - member
    place = jnp.sum(before * member, axis=1)
    return flat * capacity + place


def on_device(tokens, cotangent, scores, routes, w_gate, w_up, w_down):
    tok_count = tokens.shape[0]
    owners = lax.axis_size("expert")
    local_count = w_gate.shape[0]
    expert_count = local_count * owners
    capacity = min(tok_count, 2 * tok_count // expert_count)
    slot_total = expert_count * capacity
    slot_ids = slots_of(routes, expert_count, capacity)
    groups_slots = lax.all_gather(slot_ids, "dp", axis=0, tiled=False)
    mix = scores[:, :1] / jnp.sum(scores, axis=1, keepdims=True)
    x_chunk = lax.all_to_all(tokens, "dp", split_axis=1, concat_axis=0, tiled=True)
    weighted = (mix * cotangent.astype(F32)).astype(BF16)
    d_chunk = lax.all_to_all(weighted, "dp", split_axis=1, concat_axis=0, tiled=True)
    groups = groups_slots.shape[0]
    width = x_chunk.shape[1]
    picker = (
        groups_slots[:, None, :] == jnp.arange(slot_total, dtype=jnp.int32)[None, :, None]
    ).astype(BF16)
    pick_send = picker.reshape(groups, owners, local_count * capacity, tok_count)

    def dispatch(chunk):
        rows = chunk.reshape(groups, tok_count, width)
        send = jnp.einsum("gesr,grk->egsk", pick_send, rows, preferred_element_type=F32).astype(BF16)
        got = lax.all_to_all(send, "expert", split_axis=0, concat_axis=0, tiled=True)
        return got.reshape(owners, groups, local_count, capacity, width)

    rows_x = dispatch(x_chunk)
    rows_d = dispatch(d_chunk)

    def scattered(partial):
        return lax.psum_scatter(
            partial.astype(BF16).reshape(-1, partial.shape[4]), "dp", scatter_dimension=0, tiled=True
        ).astype(F32)

    gate_act = scattered(
        jnp.einsum("sgick,ikf->giscf", rows_x, w_gate, preferred_element_type=F32)
    )
    up_act = scattered(jnp.einsum("sgick,ikf->giscf", rows_x, w_up, preferred_element_type=F32))
    back_grad = scattered(
        jnp.einsum("sgick,ifk->giscf", rows_d, w_down, preferred_element_type=F32)
    )
    sigma = jax.nn.sigmoid(gate_act)
    silu_act = gate_act * sigma
    hidden = (silu_act * up_act).astype(BF16)
    grad_act_gate = (back_grad * up_act * sigma * (1.0 + gate_act * (1.0 - sigma))).astype(BF16)
    grad_act_up = (back_grad * silu_act).astype(BF16)

    def gathered(act):
        whole = lax.all_gather(act, "dp", axis=0, tiled=True)
        return whole.reshape(groups, local_count, owners, capacity, act.shape[1])

    hidden = gathered(hidden)
    grad_act_gate = gathered(grad_act_gate)
    grad_act_up = gathered(grad_act_up)
    part_out = jnp.einsum("giscf,ifk->sgick", hidden, w_down, preferred_element_type=F32)
    part_in = jnp.einsum("giscf,ikf->sgick", grad_act_gate, w_gate, preferred_element_type=F32)
    part_in = part_in + jnp.einsum(
        "giscf,ikf->sgick", grad_act_up, w_up, preferred_element_type=F32
    )

    pick_back = picker.reshape(groups, owners, local_count, capacity, tok_count)

    def combine(part):
        back = lax.all_to_all(part.astype(BF16), "expert", split_axis=0, concat_axis=0, tiled=True)
        rows = jnp.einsum("geicr,egick->grk", pick_back, back, preferred_element_type=F32)
        whole = lax.all_to_all(rows.astype(BF16), "dp", split_axis=0, concat_axis=2, tiled=True)
        whole = whole.reshape(tok_count, groups * width)
        return lax.psum_scatter(whole, "tensor", scatter_dimension=1, tiled=True).astype(F32)

    output = (mix * combine(part_out)).astype(BF16)
    grad_tokens = combine(part_in).astype(BF16)
    grad_gate = jnp.einsum("sgick,giscf->ikf", rows_x, grad_act_gate, preferred_element_type=F32)
    grad_up = jnp.einsum("sgick,giscf->ikf", rows_x, grad_act_up, preferred_element_type=F32)
    grad_down = jnp.einsum("giscf,sgick->ifk", hidden, rows_d, preferred_element_type=F32)
    return (output, grad_tokens, grad_gate, grad_up, grad_down)


def solution(mesh):
    in_specs = (
        P(("dp", "expert"), None),
        P(("dp", "expert"), None),
        P(("dp", "expert"), None),
        P(("dp", "expert"), None),
        P("expert", "dp", "tensor"),
        P("expert", "dp", "tensor"),
        P("expert", "tensor", "dp"),
    )
    out_specs = (
        P(("dp", "expert"), "tensor"),
        P(("dp", "expert"), "tensor"),
        P("expert", "dp", "tensor"),
        P("expert", "dp", "tensor"),
        P("expert", "tensor", "dp"),
    )
    return jax.shard_map(
        on_device, mesh=mesh, in_specs=in_specs, out_specs=out_specs, check_vma=False
    )
```

time: 451 us -> 275 us (0.61)
  waiting for transfers between devices: 373 us -> 84.8 us
  blocking collectives: 0 us -> 111 us
  matrix products: 30.2 us -> 18.2 us
  starting transfers between devices: 15 us -> 26 us
  local copies, waits for them, and re-layouts: 6.36 us -> 16.4 us
  other arithmetic: 11 us -> 2.94 us
    all_gather x3 -> x0, waiting for transfers between devices: 160 us -> none  [the longest x1 61.2 us: on_device(): lax.all_gather(w_gate, 'dp', axis=1, tiled=True)]
    reduce_scatter x5, waiting for transfers between devices: 191 us -> 37.5 us  [the longest x3 31.5 us: scattered(): lax.psum_scatter(partial.astype(BF16).reshape(-1, partial.shape[4]), 'dp'...]
    all_gather x0 -> x4, blocking collectives: none -> 77.3 us  [the longest x3 63.3 us: gathered(): whole = lax.all_gather(act, 'dp', axis=0, tiled=True)]
    all_to_all x0 -> x2, blocking collectives: none -> 34 us  [dispatch(): lax.all_to_all(send, 'expert', split_axis=0, concat_axis=0, tiled=True)]
    all_to_all x4 -> x6, waiting for transfers between devices: 20.8 us -> 47.2 us  [the longest x1 23.6 us: on_device(): lax.all_to_all(weighted, 'dp', split_axis=1, concat_axis=0, tiled=True)]
    dot_general x13, matrix products: 30.2 us -> 18.2 us  [the longest x1 3.26 us: on_device(): jnp.einsum('sgick,giscf->ikf', rows_x, grad_act_gate, preferred_element_t...]
    all_to_all x4 -> x6, starting transfers between devices: 14.7 us -> 25.9 us  [the longest x2 7.75 us: combine(): lax.all_to_all(rows.astype(BF16), 'dp', split_axis=0, concat_axis=2, tile...]
    convert_element_type x4, other arithmetic: 7.98 us -> 2.55 us  [the longest x1 1.36 us: on_device(): grad_act_up = (back_grad * silu_act).astype(BF16)]
  transfers between devices with their start and end apart: 12 -> 11, of which waited for: 10 -> 6; matrix products, arithmetic and copies ran while one was open for 8% -> 9% of each run, Pallas kernels for 0% -> 0%
where the time goes in v1:
time: 275 us; the launch traced here: 274 us
  blocking collectives  111 us (40%)
  waiting for transfers between devices  84.8 us (31%)
  starting transfers between devices  26 us (9%)
  matrix products  18.2 us (7%)
  local copies, waits for them, and re-layouts  16.4 us (6%)
  between operations  14 us (5%)
  other arithmetic  2.94 us (1%)
    all_gather x3, blocking collectives, gathered(): whole = lax.all_gather(act, 'dp', axis=0, tiled=True)  63.3 us
    all_to_all x2, blocking collectives, dispatch(): lax.all_to_all(send, 'expert', split_axis=0, concat_axis=0, tiled=True)  34 us
    reduce_scatter x3, waiting for transfers between devices, scattered(): lax.psum_scatter(partial.astype(BF16).reshape(-1, partial.shape[4]), 'dp'...  31.5 us
    all_to_all x1, waiting for transfers between devices, on_device(): lax.all_to_all(weighted, 'dp', split_axis=1, concat_axis=0, tiled=True)  23.6 us
    all_gather x1, blocking collectives, on_device(): groups_slots = lax.all_gather(slot_ids, 'dp', axis=0, tiled=False)  14 us
    all_to_all x2, waiting for transfers between devices, combine(): lax.all_to_all(part.astype(BF16), 'expert', split_axis=0, concat_axis=0,...  12.3 us
    all_to_all x2, waiting for transfers between devices, combine(): lax.all_to_all(rows.astype(BF16), 'dp', split_axis=0, concat_axis=2, tile...  11.3 us
    all_to_all x2, starting transfers between devices, combine(): lax.all_to_all(rows.astype(BF16), 'dp', split_axis=0, concat_axis=2, tile...  7.75 us
  transfers between devices with their start and end apart: 11, of which 6 were waited for; matrix products, arithmetic and copies ran while one was open for 9% of the time, Pallas kernels for 0%

profile of v1, /device:TPU:0, one launch (start us, length us, event | category | flops | bytes accessed | tf_op | source)
XLA Modules:
  0.0 273.7 jit_solution(3721309420768128933)
XLA Ops:
  9.6 6.3 %all-to-all-start = ((bf16[128,4,512]{2,0,1:T(8,128)(2,1)}), bf16[128,4,512]{2,0,1:T(8,128)(2,1)S(1)}, u32[]{:S(2)}, u32[]{:S(2)}) async-start(bf16[128,4,512]{2,0,1:T(8,128)(2,1)} %copy.62), calls=%async_computation | async-start | bytes 1048576 | tf_op jit(solution)/shard_map/all_to_all | solution.py:28
  16.4 14.0 %all-gather = s32[4,1,128]{2,1,0:T(1,128)S(1)} all-gather(s32[1,1,128]{2,1,0:T(1,128)S(1)} %fusion.51), channel_id=1, replica_groups=mesh['dp'=4,'expert'=4,'tensor'=2] {'dp'}, dimensions={0}, use_global_device_ids=true | all-gather | bytes 2560 | tf_op jit(solution)/shard_map/all_gather | solution.py:26
  31.0 17.2 %all_to_all.82 = bf16[4,4,64,512]{3,2,1,0:T(8,128)(2,1)S(1)} all-to-all(bf16[4,4,64,512]{3,2,1,0:T(8,128)(2,1)S(1)} %copy.63), channel_id=1, replica_groups=mesh['dp'=4,'expert'=4,'tensor'=2] {'expert'}, dimensions={0} | all-to-all | bytes 2097152 | tf_op jit(solution)/shard_map/all_to_all | solution.py:41
  51.4 4.8 %all-to-all-start.4 = ((bf16[128,4,512]{2,0,1:T(8,128)(2,1)}), bf16[128,4,512]{2,0,1:T(8,128)(2,1)S(1)}, u32[]{:S(2)}, u32[]{:S(2)}) async-start(bf16[128,4,512]{2,0,1:T(8,128)(2,1)} %copy.72), calls=%async_computation.7 | async-start | bytes 1048576 | tf_op jit(solution)/shard_map/all_to_all | solution.py:30
  56.2 1.8 fusion.7
  59.1 23.6 %all-to-all-done.4 = bf16[128,4,512]{2,0,1:T(8,128)(2,1)S(1)} async-done(((bf16[128,4,512]{2,0,1:T(8,128)(2,1)}), bf16[128,4,512]{2,0,1:T(8,128)(2,1)S(1)}, u32[]{:S(2)}, u32[]{:S(2)}) %all-to-all-start.4) | async-done | bytes 524320 | tf_op jit(solution)/shard_map/all_to_all | solution.py:30
  83.3 16.9 %all_to_all.83 = bf16[4,4,64,512]{3,2,1,0:T(8,128)(2,1)S(1)} all-to-all(bf16[4,4,64,512]{3,2,1,0:T(8,128)(2,1)S(1)} %copy.73), channel_id=1, replica_groups=mesh['dp'=4,'expert'=4,'tensor'=2] {'expert'}, dimensions={0} | all-to-all | bytes 2097152 | tf_op jit(solution)/shard_map/all_to_all | solution.py:41
  101.9 6.0 %reduce-scatter.8.cloned.1.call-done = bf16[256,384]{1,0:T(8,128)(2,1)} async-done(((bf16[1024,384]{1,0:T(8,128)(2,1)}), bf16[256,384]{1,0:T(8,128)(2,1)}) %reduce-scatter.8.cloned.1.call-update) | async-done | bytes 196624 | tf_op jit(solution)/shard_map/reduce_scatter | solution.py:48
  107.9 25.5 %reduce-scatter.12.cloned.1.call-done = bf16[256,384]{1,0:T(8,128)(2,1)} async-done(((bf16[1024,384]{1,0:T(8,128)(2,1)}), bf16[256,384]{1,0:T(8,128)(2,1)}) %reduce-scatter.12.cloned.1.call-update) | async-done | bytes 196624 | tf_op jit(solution)/shard_map/reduce_scatter | solution.py:48
  134.8 18.0 %all_gather.14 = bf16[1024,384]{1,0:T(8,128)(2,1)S(1)} all-gather(bf16[256,384]{1,0:T(8,128)(2,1)S(1)} %get-tuple-element.22), channel_id=1, replica_groups=mesh['dp'=4,'expert'=4,'tensor'=2] {'dp'}, dimensions={0}, use_global_device_ids=true | all-gather | bytes 983040 | tf_op jit(solution)/shard_map/all_gather | solution.py:66
  155.4 3.5 %all-to-all-start.2 = ((bf16[4,4,2,32,512]{4,3,2,1,0:T(8,128)(2,1)}), bf16[4,4,2,32,512]{4,3,2,1,0:T(8,128)(2,1)S(1)}, u32[]{:S(2)}, u32[]{:S(2)}) async-start(bf16[4,4,2,32,512]{4,3,2,1,0:T(8,128)(2,1)} %copy.69), calls=%async_computation.4 | async-start | bytes 2097152 | tf_op jit(solution)/shard_map/all_to_all | solution.py:81
  158.9 18.0 %all_gather.15 = bf16[1024,384]{1,0:T(8,128)(2,1)S(1)} all-gather(bf16[256,384]{1,0:T(8,128)(2,1)S(1)} %get-tuple-element.21), channel_id=1, replica_groups=mesh['dp'=4,'expert'=4,'tensor'=2] {'dp'}, dimensions={0}, use_global_device_ids=true | all-gather | bytes 983040 | tf_op jit(solution)/shard_map/all_gather | solution.py:66
  178.1 3.5 %all-to-all-start.3 = ((bf16[4,128,512]{2,1,0:T(8,128)(2,1)}), bf16[4,128,512]{2,1,0:T(8,128)(2,1)S(1)}, u32[]{:S(2)}, u32[]{:S(2)}) async-start(bf16[4,128,512]{2,1,0:T(8,128)(2,1)} %fusion.4), calls=%async_computation.5 | async-start | bytes 1048576 | tf_op jit(solution)/shard_map/all_to_all | solution.py:83
  181.6 27.4 %all_gather.16 = bf16[1024,384]{1,0:T(8,128)(2,1)S(1)} all-gather(bf16[256,384]{1,0:T(8,128)(2,1)S(1)} %get-tuple-element.20), channel_id=1, replica_groups=mesh['dp'=4,'expert'=4,'tensor'=2] {'dp'}, dimensions={0}, use_global_device_ids=true | all-gather | bytes 983040 | tf_op jit(solution)/shard_map/all_gather | solution.py:66
  209.0 1.9 fusion.16
  213.6 3.5 %all-to-all-start.6 = ((bf16[4,4,2,32,512]{4,3,2,1,0:T(8,128)(2,1)}), bf16[4,4,2,32,512]{4,3,2,1,0:T(8,128)(2,1)S(1)}, u32[]{:S(2)}, u32[]{:S(2)}) async-start(bf16[4,4,2,32,512]{4,3,2,1,0:T(8,128)(2,1)} %copy.78), calls=%async_computation.10 | async-start | bytes 2097152 | tf_op jit(solution)/shard_map/all_to_all | solution.py:81
  217.1 2.0 copy.70
  219.2 12.3 %all-to-all-done.6 = bf16[4,4,2,32,512]{4,3,2,1,0:T(8,128)(2,1)S(1)} async-done(((bf16[4,4,2,32,512]{4,3,2,1,0:T(8,128)(2,1)}), bf16[4,4,2,32,512]{4,3,2,1,0:T(8,128)(2,1)S(1)}, u32[]{:S(2)}, u32[]{:S(2)}) %all-to-all-start.6) | async-done | bytes 1048608 | tf_op jit(solution)/shard_map/all_to_all | solution.py:81
  232.7 4.3 %all-to-all-start.7 = ((bf16[4,128,512]{2,1,0:T(8,128)(2,1)}), bf16[4,128,512]{2,1,0:T(8,128)(2,1)S(1)}, u32[]{:S(2)}, u32[]{:S(2)}) async-start(bf16[4,128,512]{2,1,0:T(8,128)(2,1)} %fusion.5), calls=%async_computation.11 | async-start | bytes 1048576 | tf_op jit(solution)/shard_map/all_to_all | solution.py:83
  237.0 3.1 %convolution_bitcast_fusion.1 = f32[2,512,384]{2,1,0:T(8,128)} fusion(bf16[4,4,2,32,512]{4,3,2,1,0:T(8,128)(2,1)} %bitcast.131, bf16[4,2,4,32,384]{4,3,2,1,0:T(8,128)(2,1)S(1)} %bitcast.117), kind=kOutput, calls=%fused_computation.2 | convolution fusion | flops 402653184 | bytes 3407872 | tf_op jit(solution)/shard_map/sgick,giscf->ikf/dot_general | solution.py:90
  240.1 11.3 %all-to-all-done.7 = bf16[4,128,512]{2,1,0:T(8,128)(2,1)S(1)} async-done(((bf16[4,128,512]{2,1,0:T(8,128)(2,1)}), bf16[4,128,512]{2,1,0:T(8,128)(2,1)S(1)}, u32[]{:S(2)}, u32[]{:S(2)}) %all-to-all-start.7) | async-done | bytes 524320 | tf_op jit(solution)/shard_map/all_to_all | solution.py:83
  252.5 3.3 %convolution_bitcast_fusion.2 = f32[2,512,384]{2,1,0:T(8,128)} fusion(bf16[4,4,2,32,512]{4,3,2,1,0:T(8,128)(2,1)} %bitcast.132, bf16[4,2,4,32,384]{4,3,2,1,0:T(8,128)(2,1)S(1)} %bitcast.119), kind=kOutput, calls=%fused_computation.3 | convolution fusion | flops 402653184 | bytes 3407872 | tf_op jit(solution)/shard_map/sgick,giscf->ikf/dot_general | solution.py:89
  259.4 6.0 %reduce-scatter.14.cloned.1.call-done = bf16[128,1024]{0,1:T(8,128)(2,1)} async-done(((bf16[128,2048]{0,1:T(8,128)(2,1)}), bf16[128,1024]{0,1:T(8,128)(2,1)}) %reduce-scatter.14.cloned.1.call-update) | async-done | bytes 262160 | tf_op jit(solution)/shard_map/reduce_scatter | solution.py:85
  265.3 1.8 copy.86
  (72 shorter events, 23.8 us)
Async XLA Ops:
  7.2 93.0 %copy-start = (bf16[2,384,512]{2,1,0:T(8,128)(2,1)S(1)}, bf16[2,384,512]{2,1,0:T(8,128)(2,1)}, u32[]{:S(2)}) copy-start(bf16[2,384,512]{2,1,0:T(8,128)(2,1)} %param.13) | copy-start | bytes 2359300
  7.2 8.7 %copy-start.11 = (s32[128,1]{0,1:T(1,128)S(1)}, s32[128,1]{0,1:T(1,128)}, u32[]{:S(2)}) copy-start(s32[128,1]{0,1:T(1,128)} %param.10) | copy-start | bytes 1540
  9.6 20.8 %all-to-all-start = ((bf16[128,4,512]{2,0,1:T(8,128)(2,1)}), bf16[128,4,512]{2,0,1:T(8,128)(2,1)S(1)}, u32[]{:S(2)}, u32[]{:S(2)}) async-start(bf16[128,4,512]{2,0,1:T(8,128)(2,1)} %copy.62), calls=%async_computation | async-start | bytes 1048576 | tf_op jit(solution)/shard_map/all_to_all | solution.py:28
  15.9 86.0 %reduce-scatter.6.cloned.1.call-start = ((), (), s32[]{:S(2)}) async-start(), calls=%async_computation.13 | async-start | bytes 983040 | tf_op jit(solution)/shard_map/reduce_scatter | solution.py:48
  31.0 17.2 %copy-start.5 = (bf16[2,512,384]{2,1,0:T(8,128)(2,1)S(1)}, bf16[2,512,384]{2,1,0:T(8,128)(2,1)}, u32[]{:S(2)}) copy-start(bf16[2,512,384]{2,1,0:T(8,128)(2,1)} %param.11) | copy-start | bytes 2359300
  48.2 8.0 %copy-start.2 = (bf16[4,4,64,512]{3,2,1,0:T(8,128)(2,1)}, bf16[4,4,64,512]{3,2,1,0:T(8,128)(2,1)S(1)}, u32[]{:S(2)}) copy-start(bf16[4,4,64,512]{3,2,1,0:T(8,128)(2,1)S(1)} %all_to_all.82) | copy-start | bytes 3145732
  48.9 1.1 copy-start.9
  48.9 1.3 copy-start.10
  51.4 31.3 %all-to-all-start.4 = ((bf16[128,4,512]{2,0,1:T(8,128)(2,1)}), bf16[128,4,512]{2,0,1:T(8,128)(2,1)S(1)}, u32[]{:S(2)}, u32[]{:S(2)}) async-start(bf16[128,4,512]{2,0,1:T(8,128)(2,1)} %copy.72), calls=%async_computation.7 | async-start | bytes 1048576 | tf_op jit(solution)/shard_map/all_to_all | solution.py:30
  56.2 51.7 %reduce-scatter.8.cloned.1.call-start = ((), (), s32[]{:S(2)}) async-start(), calls=%async_computation.14 | async-start | bytes 983040 | tf_op jit(solution)/shard_map/reduce_scatter | solution.py:48
  59.1 74.3 %reduce-scatter.12.cloned.1.call-start = ((), (), s32[]{:S(2)}) async-start(), calls=%async_computation.16 | async-start | bytes 983040 | tf_op jit(solution)/shard_map/reduce_scatter | solution.py:48
  100.1 1.7 copy-start.3
  152.7 0.9 copy-start.7
  155.4 21.5 %all-to-all-start.2 = ((bf16[4,4,2,32,512]{4,3,2,1,0:T(8,128)(2,1)}), bf16[4,4,2,32,512]{4,3,2,1,0:T(8,128)(2,1)S(1)}, u32[]{:S(2)}, u32[]{:S(2)}) async-start(bf16[4,4,2,32,512]{4,3,2,1,0:T(8,128)(2,1)} %copy.69), calls=%async_computation.4 | async-start | bytes 2097152 | tf_op jit(solution)/shard_map/all_to_all | solution.py:81
  178.1 34.7 %all-to-all-start.3 = ((bf16[4,128,512]{2,1,0:T(8,128)(2,1)}), bf16[4,128,512]{2,1,0:T(8,128)(2,1)S(1)}, u32[]{:S(2)}, u32[]{:S(2)}) async-start(bf16[4,128,512]{2,1,0:T(8,128)(2,1)} %fusion.4), calls=%async_computation.5 | async-start | bytes 1048576 | tf_op jit(solution)/shard_map/all_to_all | solution.py:83
  209.0 1.9 copy-start.6
  212.8 0.8 copy-start.1
  213.6 18.0 %all-to-all-start.6 = ((bf16[4,4,2,32,512]{4,3,2,1,0:T(8,128)(2,1)}), bf16[4,4,2,32,512]{4,3,2,1,0:T(8,128)(2,1)S(1)}, u32[]{:S(2)}, u32[]{:S(2)}) async-start(bf16[4,4,2,32,512]{4,3,2,1,0:T(8,128)(2,1)} %copy.78), calls=%async_computation.10 | async-start | bytes 2097152 | tf_op jit(solution)/shard_map/all_to_all | solution.py:81
  217.1 40.4 %reduce-scatter.10.cloned.1.call-start = ((), (), s32[]{:S(2)}) async-start(), calls=%async_computation.15 | async-start | bytes 786432 | tf_op jit(solution)/shard_map/reduce_scatter | solution.py:85
  232.7 18.7 %all-to-all-start.7 = ((bf16[4,128,512]{2,1,0:T(8,128)(2,1)}), bf16[4,128,512]{2,1,0:T(8,128)(2,1)S(1)}, u32[]{:S(2)}, u32[]{:S(2)}) async-start(bf16[4,128,512]{2,1,0:T(8,128)(2,1)} %fusion.5), calls=%async_computation.11 | async-start | bytes 1048576 | tf_op jit(solution)/shard_map/all_to_all | solution.py:83
  237.0 28.3 %reduce-scatter.14.cloned.1.call-start = ((), (), s32[]{:S(2)}) async-start(), calls=%async_computation.17 | async-start | bytes 786432 | tf_op jit(solution)/shard_map/reduce_scatter | solution.py:85
  252.5 3.3 %copy-start.4 = (bf16[4,4,64,512]{3,2,1,0:T(8,128)(2,1)S(1)}, bf16[4,4,64,512]{3,2,1,0:T(8,128)(2,1)}, u32[]{:S(2)}) copy-start(bf16[4,4,64,512]{3,2,1,0:T(8,128)(2,1)} %copy-done.3) | copy-start | bytes 3145732
  252.5 3.3 %copy-start.8 = (bf16[1024,384]{1,0:T(8,128)(2,1)S(1)}, bf16[1024,384]{1,0:T(8,128)(2,1)}, u32[]{:S(2)}) copy-start(bf16[1024,384]{1,0:T(8,128)(2,1)} %copy-done.7) | copy-start | bytes 2359300
Sparse Core Ops, SparseCore 0:
  50.1 31.9 reduce-scatter.5
  85.0 22.9 reduce-scatter.7
  110.8 22.5 reduce-scatter.11
  219.9 15.6 reduce-scatter.9
  252.6 12.7 reduce-scatter.13

commit v2 on v1

v2 whole, which is shorter than its diff:
```python
import jax
import jax.numpy as jnp
from jax import lax
from jax.sharding import PartitionSpec as P

F32 = jnp.float32
BF16 = jnp.bfloat16


def dot(eq, a, b):
    return jnp.einsum(eq, a, b, preferred_element_type=F32)


def on_device(tokens, cotangent, scores, routes, w_gate, w_up, w_down):
    tok_count, model_width = tokens.shape
    owners = lax.axis_size("expert")
    groups = lax.axis_size("dp")
    sharers = lax.axis_size("tensor")
    local_count = w_gate.shape[0]
    expert_count = local_count * owners
    capacity = min(tok_count, 2 * tok_count // expert_count)
    held = local_count * capacity
    width = model_width // groups
    my_group = lax.axis_index("dp")
    my_owner = lax.axis_index("expert")
    my_part = lax.axis_index("tensor")

    def shift(value, step):
        if step % groups == 0:
            return value
        return lax.ppermute(value, "dp", [(j, (j + step) % groups) for j in range(groups)])

    def swap(value, bits):
        if bits == 0:
            return value
        return lax.ppermute(value, "expert", [(j, j ^ bits) for j in range(owners)])

    def chunks_out(rows):
        parts = []
        for step in range(groups):
            start = lax.rem(my_group + step, groups) * width
            parts.append(shift(lax.dynamic_slice(rows, (0, start), (tok_count, width)), step))
        return parts

    def picked(stack, index):
        return lax.dynamic_index_in_dim(stack, lax.rem(index + groups, groups), 0, keepdims=False)

    def by_group(parts):
        stack = jnp.stack(parts)
        return jnp.stack([picked(stack, my_group - g) for g in range(groups)])

    routes_all = by_group([shift(routes[:, 0], step) for step in range(groups)])
    x_chunk = by_group(chunks_out(tokens))
    mix = scores[:, :1] / jnp.sum(scores, axis=1, keepdims=True)
    weighted = (mix * cotangent.astype(F32)).astype(BF16)
    d_chunk = by_group(chunks_out(weighted))

    member = (routes_all[:, :, None] == jnp.arange(expert_count, dtype=jnp.int32)).astype(F32)
    earlier = jnp.tril(jnp.ones((tok_count, tok_count), BF16), -1)
    before = dot("ab,gbe->gae", earlier, member.astype(BF16))
    place = jnp.sum(before * member, axis=2).astype(jnp.int32)
    slot_ids = routes_all * capacity + place

    def picker(bits):
        base = (my_owner ^ bits) * held
        wanted = base + jnp.arange(held, dtype=jnp.int32).reshape(local_count, 1, capacity, 1)
        return (slot_ids[None, :, None, :] == wanted).astype(BF16)

    pickers = [picker(bits) for bits in range(owners)]

    def dispatch(chunk):
        got = []
        for bits in range(owners):
            send = dot("igct,gtk->igck", pickers[bits], chunk).astype(BF16)
            got.append(swap(send.reshape(local_count, groups * capacity, width), bits))
        return [jnp.concatenate([g[i] for g in got], axis=0) for i in range(local_count)]

    rows_x = dispatch(x_chunk)
    rows_d = dispatch(d_chunk)

    def line_sum(part):
        part = part.astype(BF16)
        if groups != 4:
            return lax.psum(part, "dp").astype(F32)
        near = lax.ppermute(part, "dp", [(0, 1), (3, 2)])
        pair = part.astype(F32) + near.astype(F32)
        far = lax.ppermute(pair.astype(BF16), "dp", [(1, 2), (2, 1)])
        total = (pair + far.astype(F32)).astype(BF16)
        back = lax.ppermute(total, "dp", [(1, 0), (2, 3)])
        at_end = (my_group == 0) | (my_group == groups - 1)
        return jnp.where(at_end, back, total).astype(F32)

    experts = range(local_count)
    gate_act, up_act, back_grad = {}, {}, {}
    for i in experts:
        gate_act[i] = line_sum(dot("rk,kf->rf", rows_x[i], w_gate[i]))
        up_act[i] = line_sum(dot("rk,kf->rf", rows_x[i], w_up[i]))
    for i in experts:
        back_grad[i] = line_sum(dot("rk,fk->rf", rows_d[i], w_down[i]))

    part_out, part_in, grad_gate, grad_up, grad_down = [], [], [], [], []
    for i in experts:
        sigma = jax.nn.sigmoid(gate_act[i])
        silu_act = gate_act[i] * sigma
        hidden = (silu_act * up_act[i]).astype(BF16)
        act_gate = (
            back_grad[i] * up_act[i] * sigma * (1.0 + gate_act[i] * (1.0 - sigma))
        ).astype(BF16)
        act_up = (back_grad[i] * silu_act).astype(BF16)
        part_out.append(dot("rf,fk->rk", hidden, w_down[i]).astype(BF16))
        into = dot("rf,kf->rk", act_gate, w_gate[i]) + dot("rf,kf->rk", act_up, w_up[i])
        part_in.append(into.astype(BF16))
        grad_gate.append(dot("rk,rf->kf", rows_x[i], act_gate))
        grad_up.append(dot("rk,rf->kf", rows_x[i], act_up))
        grad_down.append(dot("rf,rk->fk", hidden, rows_d[i]))

    pick_all = jnp.stack(pickers)

    def combine(parts):
        rows = jnp.stack(parts).reshape(local_count, owners, groups, capacity, width)
        back = jnp.stack([swap(rows[:, bits], bits) for bits in range(owners)])
        sums = dot("bigct,bigck->gtk", pick_all, back).astype(BF16)
        mine = jnp.stack(
            [shift(picked(sums, my_group - step), -step) for step in range(groups)]
        )
        whole = jnp.concatenate([picked(mine, c - my_group) for c in range(groups)], axis=1)
        if sharers != 2:
            return lax.psum_scatter(whole, "tensor", scatter_dimension=1, tiled=True).astype(F32)
        half = model_width // 2
        give = lax.dynamic_slice(whole, (0, (1 - my_part) * half), (tok_count, half))
        keep = lax.dynamic_slice(whole, (0, my_part * half), (tok_count, half))
        return keep.astype(F32) + lax.ppermute(give, "tensor", [(0, 1), (1, 0)]).astype(F32)

    output = (mix * combine(part_out)).astype(BF16)
    grad_tokens = combine(part_in).astype(BF16)
    return (output, grad_tokens, jnp.stack(grad_gate), jnp.stack(grad_up), jnp.stack(grad_down))


def solution(mesh):
    in_specs = (
        P(("dp", "expert"), None),
        P(("dp", "expert"), None),
        P(("dp", "expert"), None),
        P(("dp", "expert"), None),
        P("expert", "dp", "tensor"),
        P("expert", "dp", "tensor"),
        P("expert", "tensor", "dp"),
    )
    out_specs = (
        P(("dp", "expert"), "tensor"),
        P(("dp", "expert"), "tensor"),
        P("expert", "dp", "tensor"),
        P("expert", "dp", "tensor"),
        P("expert", "tensor", "dp"),
    )
    return jax.shard_map(
        on_device, mesh=mesh, in_specs=in_specs, out_specs=out_specs, check_vma=False
    )
```

time: 275 us -> 219 us (0.80)
  blocking collectives: 111 us -> 0 us
  waiting for transfers between devices: 84.8 us -> 131 us
  starting transfers between devices: 26 us -> 61.6 us
  local copies, waits for them, and re-layouts: 16.4 us -> 0.71 us
  between operations: 14 us -> 1.58 us
  other arithmetic: 2.94 us -> 11.9 us
  matrix products: 18.2 us -> 11.2 us
    ppermute x0 -> x47, waiting for transfers between devices: none -> 131 us  [the longest x6 47.9 us: line_sum(): back = lax.ppermute(total, 'dp', [(1, 0), (2, 3)])]
    all_gather x4 -> x0, blocking collectives: 77.3 us -> none  [the longest x3 63.3 us: gathered(): whole = lax.all_gather(act, 'dp', axis=0, tiled=True)]
    ppermute x0 -> x47, starting transfers between devices: none -> 61.6 us  [the longest x15 30 us: shift(): lax.ppermute(value, 'dp', [(j, (j + step) % groups) for j in range(groups)])]
    all_to_all x6 -> x0, waiting for transfers between devices: 47.2 us -> none  [the longest x1 23.6 us: on_device(): lax.all_to_all(weighted, 'dp', split_axis=1, concat_axis=0, tiled=True)]
    reduce_scatter x5 -> x0, waiting for transfers between devices: 37.5 us -> none  [the longest x3 31.5 us: scattered(): lax.psum_scatter(partial.astype(BF16).reshape(-1, partial.shape[4]), 'dp'...]
    all_to_all x2 -> x0, blocking collectives: 34 us -> none  [dispatch(): lax.all_to_all(send, 'expert', split_axis=0, concat_axis=0, tiled=True)]
    all_to_all x6 -> x0, starting transfers between devices: 25.9 us -> none  [the longest x2 7.75 us: combine(): lax.all_to_all(rows.astype(BF16), 'dp', split_axis=0, concat_axis=2, tile...]
    dot_general x13 -> x29, matrix products: 18.2 us -> 11.2 us  [dot(): return jnp.einsum(eq, a, b, preferred_element_type=F32)]
  transfers between devices with their start and end apart: 11 -> 47, of which waited for: 6 -> 22; matrix products, arithmetic and copies ran while one was open for 9% -> 8% of each run, Pallas kernels for 0% -> 0%
where the time goes in v2:
time: 219 us; the launch traced here: 218 us
  waiting for transfers between devices  131 us (60%)
  starting transfers between devices  61.6 us (28%)
  other arithmetic  11.9 us (5%)
  matrix products  11.2 us (5%)
    ppermute x6, waiting for transfers between devices, line_sum(): back = lax.ppermute(total, 'dp', [(1, 0), (2, 3)])  47.9 us
    ppermute x6, waiting for transfers between devices, line_sum(): near = lax.ppermute(part, 'dp', [(0, 1), (3, 2)])  32 us
    ppermute x15, starting transfers between devices, shift(): lax.ppermute(value, 'dp', [(j, (j + step) % groups) for j in range(groups)])  30 us
    ppermute x12, waiting for transfers between devices, swap(): return lax.ppermute(value, 'expert', [(j, j ^ bits) for j in range(owners)])  29.2 us
    ppermute x15, waiting for transfers between devices, shift(): lax.ppermute(value, 'dp', [(j, (j + step) % groups) for j in range(groups)])  18.4 us
    dot_general x29, matrix products, dot(): return jnp.einsum(eq, a, b, preferred_element_type=F32)  11.2 us
    ppermute x6, starting transfers between devices, line_sum(): near = lax.ppermute(part, 'dp', [(0, 1), (3, 2)])  8.21 us
    ppermute x12, starting transfers between devices, swap(): return lax.ppermute(value, 'expert', [(j, j ^ bits) for j in range(owners)])  8.13 us
  transfers between devices with their start and end apart: 47, of which 22 were waited for; matrix products, arithmetic and copies ran while one was open for 8% of the time, Pallas kernels for 0%

profile of v2, /device:TPU:0, one launch (start us, length us, event | category | flops | bytes accessed | tf_op | source)
XLA Modules:
  0.0 217.8 jit_solution(8034954605124037160)
XLA Ops:
  0.6 5.1 %collective-permute-start.2 = (s32[128]{0:T(128)}, s32[128]{0:T(128)S(1)}, u32[]{:S(2)}, u32[]{:S(2)}) collective-permute-start(s32[128]{0:T(128)} %bitcast.276), channel_id=1, source_target_pairs={{0,24},{8,0},{16,8},{24,16},{1,25},{9,1},{17,9},{25,17},{2,26},{10... | collective-permute-start | bytes 1544 | tf_op jit(solution)/shard_map/ppermute | solution.py:31
  9.4 2.9 %collective-permute-start.30 = (bf16[128,512]{1,0:T(8,128)(2,1)S(1)}, bf16[128,512]{1,0:T(8,128)(2,1)S(1)}, u32[]{:S(2)}, u32[]{:S(2)}) collective-permute-start(bf16[128,512]{1,0:T(8,128)(2,1)S(1)} %get-tuple-element.50), channel_id=1, source_target_pairs={{0,24},{8,0},{16,8},{24,16},{1,25},{9,1},{17,9},{25,17},{2,26},{10... | collective-permute-start | bytes 393224 | tf_op jit(solution)/shard_map/ppermute | solution.py:31
  13.7 3.8 %collective-permute-start.5 = (bf16[128,512]{1,0:T(8,128)(2,1)S(1)}, bf16[128,512]{1,0:T(8,128)(2,1)S(1)}, u32[]{:S(2)}, u32[]{:S(2)}) collective-permute-start(bf16[128,512]{1,0:T(8,128)(2,1)S(1)} %get-tuple-element.43), channel_id=1, source_target_pairs={{0,24},{8,0},{16,8},{24,16},{1,25},{9,1},{17,9},{25,17},{2,26},{10... | collective-permute-start | bytes 393224 | tf_op jit(solution)/shard_map/ppermute | solution.py:31
  17.8 6.3 %collective-permute-start.3 = (bf16[128,512]{1,0:T(8,128)(2,1)S(1)}, bf16[128,512]{1,0:T(8,128)(2,1)S(1)}, u32[]{:S(2)}, u32[]{:S(2)}) collective-permute-start(bf16[128,512]{1,0:T(8,128)(2,1)S(1)} %get-tuple-element.42), channel_id=1, source_target_pairs={{0,8},{8,16},{16,24},{24,0},{1,9},{9,17},{17,25},{25,1},{2,10},{10... | collective-permute-start | bytes 393224 | tf_op jit(solution)/shard_map/ppermute | solution.py:31
  24.2 7.1 %collective-permute-done.29 = bf16[128,512]{1,0:T(8,128)(2,1)S(1)} collective-permute-done((bf16[128,512]{1,0:T(8,128)(2,1)S(1)}, bf16[128,512]{1,0:T(8,128)(2,1)S(1)}, u32[]{:S(2)}, u32[]{:S(2)}) %collective-permute-start.29) | collective-permute-done | bytes 131104 | tf_op jit(solution)/shard_map/ppermute | solution.py:31
  31.4 4.1 %collective-permute-done.4 = bf16[128,512]{1,0:T(8,128)(2,1)S(1)} collective-permute-done((bf16[128,512]{1,0:T(8,128)(2,1)S(1)}, bf16[128,512]{1,0:T(8,128)(2,1)S(1)}, u32[]{:S(2)}, u32[]{:S(2)}) %collective-permute-start.4) | collective-permute-done | bytes 131104 | tf_op jit(solution)/shard_map/ppermute | solution.py:31
  42.0 4.2 %collective-permute-done.33 = bf16[2,128,512]{2,1,0:T(8,128)(2,1)S(1)} collective-permute-done((bf16[2,128,512]{2,1,0:T(8,128)(2,1)S(1)}, bf16[2,128,512]{2,1,0:T(8,128)(2,1)S(1)}, u32[]{:S(2)}, u32[]{:S(2)}) %collective-permute-start.33) | collective-permute-done | bytes 262176 | tf_op jit(solution)/shard_map/ppermute | solution.py:36
  46.4 5.6 %collective-permute-done.32 = bf16[2,128,512]{2,1,0:T(8,128)(2,1)S(1)} collective-permute-done((bf16[2,128,512]{2,1,0:T(8,128)(2,1)S(1)}, bf16[2,128,512]{2,1,0:T(8,128)(2,1)S(1)}, u32[]{:S(2)}, u32[]{:S(2)}) %collective-permute-start.32) | collective-permute-done | bytes 262176 | tf_op jit(solution)/shard_map/ppermute | solution.py:36
  54.0 3.5 %collective-permute-done.8 = bf16[2,128,512]{2,1,0:T(8,128)(2,1)S(1)} collective-permute-done((bf16[2,128,512]{2,1,0:T(8,128)(2,1)S(1)}, bf16[2,128,512]{2,1,0:T(8,128)(2,1)S(1)}, u32[]{:S(2)}, u32[]{:S(2)}) %collective-permute-start.8) | collective-permute-done | bytes 262176 | tf_op jit(solution)/shard_map/ppermute | solution.py:36
  57.5 5.6 %collective-permute-done.7 = bf16[2,128,512]{2,1,0:T(8,128)(2,1)S(1)} collective-permute-done((bf16[2,128,512]{2,1,0:T(8,128)(2,1)S(1)}, bf16[2,128,512]{2,1,0:T(8,128)(2,1)S(1)}, u32[]{:S(2)}, u32[]{:S(2)}) %collective-permute-start.7) | collective-permute-done | bytes 262176 | tf_op jit(solution)/shard_map/ppermute | solution.py:36
  75.4 7.6 %collective-permute-done.12 = bf16[512,384]{1,0:T(8,128)(2,1)S(1)} collective-permute-done((bf16[512,384]{1,0:T(8,128)(2,1)S(1)}, bf16[512,384]{1,0:T(8,128)(2,1)S(1)}, u32[]{:S(2)}, u32[]{:S(2)}) %collective-permute-start.12) | collective-permute-done | bytes 393248 | tf_op jit(solution)/shard_map/ppermute | solution.py:85
  83.8 7.6 %collective-permute-done.37 = bf16[512,384]{1,0:T(8,128)(2,1)S(1)} collective-permute-done((bf16[512,384]{1,0:T(8,128)(2,1)S(1)}, bf16[512,384]{1,0:T(8,128)(2,1)S(1)}, u32[]{:S(2)}, u32[]{:S(2)}) %collective-permute-start.37) | collective-permute-done | bytes 393248 | tf_op jit(solution)/shard_map/ppermute | solution.py:85
  92.2 7.6 %collective-permute-done.15 = bf16[512,384]{1,0:T(8,128)(2,1)S(1)} collective-permute-done((bf16[512,384]{1,0:T(8,128)(2,1)S(1)}, bf16[512,384]{1,0:T(8,128)(2,1)S(1)}, u32[]{:S(2)}, u32[]{:S(2)}) %collective-permute-start.15) | collective-permute-done | bytes 393248 | tf_op jit(solution)/shard_map/ppermute | solution.py:85
  100.7 6.9 %collective-permute-done.18 = bf16[512,384]{1,0:T(8,128)(2,1)S(1)} collective-permute-done((bf16[512,384]{1,0:T(8,128)(2,1)S(1)}, bf16[512,384]{1,0:T(8,128)(2,1)S(1)}, u32[]{:S(2)}, u32[]{:S(2)}) %collective-permute-start.18) | collective-permute-done | bytes 393248 | tf_op jit(solution)/shard_map/ppermute | solution.py:85
  116.5 28.1 %collective-permute-done.39 = bf16[512,384]{1,0:T(8,128)(2,1)S(1)} collective-permute-done((bf16[512,384]{1,0:T(8,128)(2,1)S(1)}, bf16[512,384]{1,0:T(8,128)(2,1)S(1)}, u32[]{:S(2)}, u32[]{:S(2)}) %collective-permute-start.39) | collective-permute-done | bytes 393248 | tf_op jit(solution)/shard_map/ppermute | solution.py:89
  146.1 7.0 %collective-permute-done.17 = bf16[512,384]{1,0:T(8,128)(2,1)S(1)} collective-permute-done((bf16[512,384]{1,0:T(8,128)(2,1)S(1)}, bf16[512,384]{1,0:T(8,128)(2,1)S(1)}, u32[]{:S(2)}, u32[]{:S(2)}) %collective-permute-start.17) | collective-permute-done | bytes 393248 | tf_op jit(solution)/shard_map/ppermute | solution.py:89
  153.4 8.1 %collective-permute-done.20 = bf16[512,384]{1,0:T(8,128)(2,1)S(1)} collective-permute-done((bf16[512,384]{1,0:T(8,128)(2,1)S(1)}, bf16[512,384]{1,0:T(8,128)(2,1)S(1)}, u32[]{:S(2)}, u32[]{:S(2)}) %collective-permute-start.20) | collective-permute-done | bytes 393248 | tf_op jit(solution)/shard_map/ppermute | solution.py:89
  163.4 4.8 %collective-permute-done.14 = bf16[512,384]{1,0:T(8,128)(2,1)S(1)} collective-permute-done((bf16[512,384]{1,0:T(8,128)(2,1)S(1)}, bf16[512,384]{1,0:T(8,128)(2,1)S(1)}, u32[]{:S(2)}, u32[]{:S(2)}) %collective-permute-start.14) | collective-permute-done | bytes 393248 | tf_op jit(solution)/shard_map/ppermute | solution.py:89
  180.9 4.5 %collective-permute-done.22 = bf16[2,4,32,512]{3,2,0,1:T(8,128)(2,1)S(1)} collective-permute-done((bf16[2,4,32,512]{3,2,0,1:T(8,128)(2,1)S(1)}, bf16[2,4,32,512]{3,2,0,1:T(8,128)(2,1)S(1)}, u32[]{:S(2)}, u32[]{:S(2)}) %collective-permute-start.22) | collective-permute-done | bytes 262176 | tf_op jit(solution)/shard_map/ppermute | solution.py:36
  185.9 3.2 %collective-permute-start.25 = (bf16[128,512]{1,0:T(8,128)(2,1)S(1)}, bf16[128,512]{1,0:T(8,128)(2,1)S(1)}, u32[]{:S(2)}, u32[]{:S(2)}) collective-permute-start(bf16[128,512]{1,0:T(8,128)(2,1)S(1)} %get-tuple-element.35), channel_id=1, source_target_pairs={{0,16},{8,24},{16,0},{24,8},{1,17},{9,25},{17,1},{25,9},{2,18},{10... | collective-permute-start | bytes 393224 | tf_op jit(solution)/shard_map/ppermute | solution.py:31
  193.4 3.1 %collective-permute-done.41 = bf16[2,4,32,512]{3,2,0,1:T(8,128)(2,1)S(1)} collective-permute-done((bf16[2,4,32,512]{3,2,0,1:T(8,128)(2,1)S(1)}, bf16[2,4,32,512]{3,2,0,1:T(8,128)(2,1)S(1)}, u32[]{:S(2)}, u32[]{:S(2)}) %collective-permute-start.41) | collective-permute-done | bytes 262176 | tf_op jit(solution)/shard_map/ppermute | solution.py:36
  197.0 3.2 %collective-permute-start.44 = (bf16[128,512]{1,0:T(8,128)(2,1)S(1)}, bf16[128,512]{1,0:T(8,128)(2,1)S(1)}, u32[]{:S(2)}, u32[]{:S(2)}) collective-permute-start(bf16[128,512]{1,0:T(8,128)(2,1)S(1)} %get-tuple-element.27), channel_id=1, source_target_pairs={{0,16},{8,24},{16,0},{24,8},{1,17},{9,25},{17,1},{25,9},{2,18},{10... | collective-permute-start | bytes 393224 | tf_op jit(solution)/shard_map/ppermute | solution.py:31
  205.2 4.6 %collective-permute-done.44 = bf16[128,512]{1,0:T(8,128)(2,1)S(1)} collective-permute-done((bf16[128,512]{1,0:T(8,128)(2,1)S(1)}, bf16[128,512]{1,0:T(8,128)(2,1)S(1)}, u32[]{:S(2)}, u32[]{:S(2)}) %collective-permute-start.44) | collective-permute-done | bytes 131104 | tf_op jit(solution)/shard_map/ppermute | solution.py:31
  213.8 3.3 %collective-permute-done.46 = bf16[128,1024]{1,0:T(8,128)(2,1)S(1)} collective-permute-done((bf16[128,1024]{1,0:T(8,128)(2,1)S(1)}, bf16[128,1024]{1,0:T(8,128)(2,1)S(1)}, u32[]{:S(2)}, u32[]{:S(2)}) %collective-permute-start.46) | collective-permute-done | bytes 262176 | tf_op jit(solution)/shard_map/ppermute | solution.py:132
  (172 shorter events, 68.4 us)
Async XLA Ops:
  12.3 19.0 %collective-permute-start.29 = (bf16[128,512]{1,0:T(8,128)(2,1)S(1)}, bf16[128,512]{1,0:T(8,128)(2,1)S(1)}, u32[]{:S(2)}, u32[]{:S(2)}) collective-permute-start(bf16[128,512]{1,0:T(8,128)(2,1)S(1)} %get-tuple-element.51), channel_id=1, source_target_pairs={{0,16},{8,24},{16,0},{24,8},{1,17},{9,25},{17,1},{25,9},{2,18},{10... | collective-permute-start | bytes 393224 | tf_op jit(solution)/shard_map/ppermute | solution.py:31
  13.6 17.7 %collective-permute-start.28 = (bf16[128,512]{1,0:T(8,128)(2,1)S(1)}, bf16[128,512]{1,0:T(8,128)(2,1)S(1)}, u32[]{:S(2)}, u32[]{:S(2)}) collective-permute-start(bf16[128,512]{1,0:T(8,128)(2,1)S(1)} %get-tuple-element.52), channel_id=1, source_target_pairs={{0,8},{8,16},{16,24},{24,0},{1,9},{9,17},{17,25},{25,1},{2,10},{10... | collective-permute-start | bytes 393224 | tf_op jit(solution)/shard_map/ppermute | solution.py:31
  13.7 17.7 %collective-permute-start.5 = (bf16[128,512]{1,0:T(8,128)(2,1)S(1)}, bf16[128,512]{1,0:T(8,128)(2,1)S(1)}, u32[]{:S(2)}, u32[]{:S(2)}) collective-permute-start(bf16[128,512]{1,0:T(8,128)(2,1)S(1)} %get-tuple-element.43), channel_id=1, source_target_pairs={{0,24},{8,0},{16,8},{24,16},{1,25},{9,1},{17,9},{25,17},{2,26},{10... | collective-permute-start | bytes 393224 | tf_op jit(solution)/shard_map/ppermute | solution.py:31
  17.5 18.0 %collective-permute-start.4 = (bf16[128,512]{1,0:T(8,128)(2,1)S(1)}, bf16[128,512]{1,0:T(8,128)(2,1)S(1)}, u32[]{:S(2)}, u32[]{:S(2)}) collective-permute-start(bf16[128,512]{1,0:T(8,128)(2,1)S(1)} %get-tuple-element.44), channel_id=1, source_target_pairs={{0,16},{8,24},{16,0},{24,8},{1,17},{9,25},{17,1},{25,9},{2,18},{10... | collective-permute-start | bytes 393224 | tf_op jit(solution)/shard_map/ppermute | solution.py:31
  17.8 17.7 %collective-permute-start.3 = (bf16[128,512]{1,0:T(8,128)(2,1)S(1)}, bf16[128,512]{1,0:T(8,128)(2,1)S(1)}, u32[]{:S(2)}, u32[]{:S(2)}) collective-permute-start(bf16[128,512]{1,0:T(8,128)(2,1)S(1)} %get-tuple-element.42), channel_id=1, source_target_pairs={{0,8},{8,16},{16,24},{24,0},{1,9},{9,17},{17,25},{25,1},{2,10},{10... | collective-permute-start | bytes 393224 | tf_op jit(solution)/shard_map/ppermute | solution.py:31
  39.8 17.7 %collective-permute-start.8 = (bf16[2,128,512]{2,1,0:T(8,128)(2,1)S(1)}, bf16[2,128,512]{2,1,0:T(8,128)(2,1)S(1)}, u32[]{:S(2)}, u32[]{:S(2)}) collective-permute-start(bf16[2,128,512]{2,1,0:T(8,128)(2,1)S(1)} %bitcast.247), channel_id=1, source_target_pairs={{0,6},{2,4},{4,2},{6,0},{1,7},{3,5},{5,3},{7,1},{8,14},{10,12},{12... | collective-permute-start | bytes 786440 | tf_op jit(solution)/shard_map/ppermute | solution.py:36
  41.0 22.2 %collective-permute-start.7 = (bf16[2,128,512]{2,1,0:T(8,128)(2,1)S(1)}, bf16[2,128,512]{2,1,0:T(8,128)(2,1)S(1)}, u32[]{:S(2)}, u32[]{:S(2)}) collective-permute-start(bf16[2,128,512]{2,1,0:T(8,128)(2,1)S(1)} %bitcast.246), channel_id=1, source_target_pairs={{0,4},{2,6},{4,0},{6,2},{1,5},{3,7},{5,1},{7,3},{8,12},{10,14},{12... | collective-permute-start | bytes 786440 | tf_op jit(solution)/shard_map/ppermute | solution.py:36
  46.2 16.9 %collective-permute-start.6 = (bf16[2,128,512]{2,1,0:T(8,128)(2,1)S(1)}, bf16[2,128,512]{2,1,0:T(8,128)(2,1)S(1)}, u32[]{:S(2)}, u32[]{:S(2)}) collective-permute-start(bf16[2,128,512]{2,1,0:T(8,128)(2,1)S(1)} %bitcast.250), channel_id=1, source_target_pairs={{0,2},{2,0},{4,6},{6,4},{1,3},{3,1},{5,7},{7,5},{8,10},{10,8},{12,... | collective-permute-start | bytes 786440 | tf_op jit(solution)/shard_map/ppermute | solution.py:36
  52.5 18.4 %collective-permute-start.34 = (bf16[512,384]{1,0:T(8,128)(2,1)S(1)}, bf16[512,384]{1,0:T(8,128)(2,1)S(1)}, u32[]{:S(2)}, u32[]{:S(2)}) collective-permute-start(bf16[512,384]{1,0:T(8,128)(2,1)S(1)} %convolution_convert_fusion.3), channel_id=1, source_target_pairs={{0,8},{24,16},{1,9},{25,17},{2,10},{26,18},{3,11},{27,19},{4,12},{... | collective-permute-start | bytes 1179656 | tf_op jit(solution)/shard_map/ppermute | solution.py:85
  65.6 17.4 %collective-permute-start.12 = (bf16[512,384]{1,0:T(8,128)(2,1)S(1)}, bf16[512,384]{1,0:T(8,128)(2,1)S(1)}, u32[]{:S(2)}, u32[]{:S(2)}) collective-permute-start(bf16[512,384]{1,0:T(8,128)(2,1)S(1)} %convolution_convert_fusion.6), channel_id=1, source_target_pairs={{0,8},{24,16},{1,9},{25,17},{2,10},{26,18},{3,11},{27,19},{4,12},{... | collective-permute-start | bytes 1179656 | tf_op jit(solution)/shard_map/ppermute | solution.py:85
  67.4 24.0 %collective-permute-start.37 = (bf16[512,384]{1,0:T(8,128)(2,1)S(1)}, bf16[512,384]{1,0:T(8,128)(2,1)S(1)}, u32[]{:S(2)}, u32[]{:S(2)}) collective-permute-start(bf16[512,384]{1,0:T(8,128)(2,1)S(1)} %convolution_convert_fusion.2), channel_id=1, source_target_pairs={{0,8},{24,16},{1,9},{25,17},{2,10},{26,18},{3,11},{27,19},{4,12},{... | collective-permute-start | bytes 1179656 | tf_op jit(solution)/shard_map/ppermute | solution.py:85
  69.2 30.7 %collective-permute-start.15 = (bf16[512,384]{1,0:T(8,128)(2,1)S(1)}, bf16[512,384]{1,0:T(8,128)(2,1)S(1)}, u32[]{:S(2)}, u32[]{:S(2)}) collective-permute-start(bf16[512,384]{1,0:T(8,128)(2,1)S(1)} %convolution_convert_fusion.5), channel_id=1, source_target_pairs={{0,8},{24,16},{1,9},{25,17},{2,10},{26,18},{3,11},{27,19},{4,12},{... | collective-permute-start | bytes 1179656 | tf_op jit(solution)/shard_map/ppermute | solution.py:85
  70.9 36.6 %collective-permute-start.18 = (bf16[512,384]{1,0:T(8,128)(2,1)S(1)}, bf16[512,384]{1,0:T(8,128)(2,1)S(1)}, u32[]{:S(2)}, u32[]{:S(2)}) collective-permute-start(bf16[512,384]{1,0:T(8,128)(2,1)S(1)} %convolution_convert_fusion.4), channel_id=1, source_target_pairs={{0,8},{24,16},{1,9},{25,17},{2,10},{26,18},{3,11},{27,19},{4,12},{... | collective-permute-start | bytes 1179656 | tf_op jit(solution)/shard_map/ppermute | solution.py:85
  74.6 33.8 %collective-permute-start.35 = (bf16[512,384]{1,0:T(8,128)(2,1)S(1)}, bf16[512,384]{1,0:T(8,128)(2,1)S(1)}, u32[]{:S(2)}, u32[]{:S(2)}) collective-permute-start(bf16[512,384]{1,0:T(8,128)(2,1)S(1)} %fusion.38), channel_id=1, source_target_pairs={{8,16},{16,8},{9,17},{17,9},{10,18},{18,10},{11,19},{19,11},{12,20... | collective-permute-start | bytes 1179656 | tf_op jit(solution)/shard_map/ppermute | solution.py:87
  83.0 26.2 %collective-permute-start.10 = (bf16[512,384]{1,0:T(8,128)(2,1)S(1)}, bf16[512,384]{1,0:T(8,128)(2,1)S(1)}, u32[]{:S(2)}, u32[]{:S(2)}) collective-permute-start(bf16[512,384]{1,0:T(8,128)(2,1)S(1)} %fusion.34), channel_id=1, source_target_pairs={{8,16},{16,8},{9,17},{17,9},{10,18},{18,10},{11,19},{19,11},{12,20... | collective-permute-start | bytes 1179656 | tf_op jit(solution)/shard_map/ppermute | solution.py:87
  91.4 23.6 %collective-permute-start.13 = (bf16[512,384]{1,0:T(8,128)(2,1)S(1)}, bf16[512,384]{1,0:T(8,128)(2,1)S(1)}, u32[]{:S(2)}, u32[]{:S(2)}) collective-permute-start(bf16[512,384]{1,0:T(8,128)(2,1)S(1)} %fusion.35), channel_id=1, source_target_pairs={{8,16},{16,8},{9,17},{17,9},{10,18},{18,10},{11,19},{19,11},{12,20... | collective-permute-start | bytes 1179656 | tf_op jit(solution)/shard_map/ppermute | solution.py:87
  109.2 53.8 %collective-permute-start.36 = (bf16[512,384]{1,0:T(8,128)(2,1)S(1)}, bf16[512,384]{1,0:T(8,128)(2,1)S(1)}, u32[]{:S(2)}, u32[]{:S(2)}) collective-permute-start(bf16[512,384]{1,0:T(8,128)(2,1)S(1)} %add_convert_fusion.1), channel_id=1, source_target_pairs={{8,0},{16,24},{9,1},{17,25},{10,2},{18,26},{11,3},{19,27},{12,4},{... | collective-permute-start | bytes 1179656 | tf_op jit(solution)/shard_map/ppermute | solution.py:89
  110.7 52.3 %collective-permute-start.11 = (bf16[512,384]{1,0:T(8,128)(2,1)S(1)}, bf16[512,384]{1,0:T(8,128)(2,1)S(1)}, u32[]{:S(2)}, u32[]{:S(2)}) collective-permute-start(bf16[512,384]{1,0:T(8,128)(2,1)S(1)} %add_convert_fusion.5), channel_id=1, source_target_pairs={{8,0},{16,24},{9,1},{17,25},{10,2},{18,26},{11,3},{19,27},{12,4},{... | collective-permute-start | bytes 1179656 | tf_op jit(solution)/shard_map/ppermute | solution.py:89
  112.1 32.5 %collective-permute-start.39 = (bf16[512,384]{1,0:T(8,128)(2,1)S(1)}, bf16[512,384]{1,0:T(8,128)(2,1)S(1)}, u32[]{:S(2)}, u32[]{:S(2)}) collective-permute-start(bf16[512,384]{1,0:T(8,128)(2,1)S(1)} %add_convert_fusion), channel_id=1, source_target_pairs={{8,0},{16,24},{9,1},{17,25},{10,2},{18,26},{11,3},{19,27},{12,4},{... | collective-permute-start | bytes 1179656 | tf_op jit(solution)/shard_map/ppermute | solution.py:89
  113.6 39.5 %collective-permute-start.17 = (bf16[512,384]{1,0:T(8,128)(2,1)S(1)}, bf16[512,384]{1,0:T(8,128)(2,1)S(1)}, u32[]{:S(2)}, u32[]{:S(2)}) collective-permute-start(bf16[512,384]{1,0:T(8,128)(2,1)S(1)} %add_convert_fusion.3), channel_id=1, source_target_pairs={{8,0},{16,24},{9,1},{17,25},{10,2},{18,26},{11,3},{19,27},{12,4},{... | collective-permute-start | bytes 1179656 | tf_op jit(solution)/shard_map/ppermute | solution.py:89
  115.1 46.4 %collective-permute-start.20 = (bf16[512,384]{1,0:T(8,128)(2,1)S(1)}, bf16[512,384]{1,0:T(8,128)(2,1)S(1)}, u32[]{:S(2)}, u32[]{:S(2)}) collective-permute-start(bf16[512,384]{1,0:T(8,128)(2,1)S(1)} %add_convert_fusion.2), channel_id=1, source_target_pairs={{8,0},{16,24},{9,1},{17,25},{10,2},{18,26},{11,3},{19,27},{12,4},{... | collective-permute-start | bytes 1179656 | tf_op jit(solution)/shard_map/ppermute | solution.py:89
  144.7 23.5 %collective-permute-start.14 = (bf16[512,384]{1,0:T(8,128)(2,1)S(1)}, bf16[512,384]{1,0:T(8,128)(2,1)S(1)}, u32[]{:S(2)}, u32[]{:S(2)}) collective-permute-start(bf16[512,384]{1,0:T(8,128)(2,1)S(1)} %add_convert_fusion.4), channel_id=1, source_target_pairs={{8,0},{16,24},{9,1},{17,25},{10,2},{18,26},{11,3},{19,27},{12,4},{... | collective-permute-start | bytes 1179656 | tf_op jit(solution)/shard_map/ppermute | solution.py:89
  176.2 20.3 %collective-permute-start.41 = (bf16[2,4,32,512]{3,2,0,1:T(8,128)(2,1)S(1)}, bf16[2,4,32,512]{3,2,0,1:T(8,128)(2,1)S(1)}, u32[]{:S(2)}, u32[]{:S(2)}) collective-permute-start(bf16[2,4,32,512]{3,2,0,1:T(8,128)(2,1)S(1)} %get-tuple-element.16), channel_id=1, source_target_pairs={{0,4},{2,6},{4,0},{6,2},{1,5},{3,7},{5,1},{7,3},{8,12},{10,14},{12... | collective-permute-start | bytes 786440 | tf_op jit(solution)/shard_map/ppermute | solution.py:36
  179.5 17.0 %collective-permute-start.40 = (bf16[2,4,32,512]{3,2,0,1:T(8,128)(2,1)S(1)}, bf16[2,4,32,512]{3,2,0,1:T(8,128)(2,1)S(1)}, u32[]{:S(2)}, u32[]{:S(2)}) collective-permute-start(bf16[2,4,32,512]{3,2,0,1:T(8,128)(2,1)S(1)} %get-tuple-element.14), channel_id=1, source_target_pairs={{0,2},{2,0},{4,6},{6,4},{1,3},{3,1},{5,7},{7,5},{8,10},{10,8},{12,... | collective-permute-start | bytes 786440 | tf_op jit(solution)/shard_map/ppermute | solution.py:36
  (28 other events, 293.9 us)

commit v3 on v2

--- a/solution.py
+++ b/solution.py
@@ -1,6 +1,8 @@
 import jax
 import jax.numpy as jnp
 from jax import lax
+from jax.experimental import pallas as pl
+from jax.experimental.pallas import tpu as pltpu
 from jax.sharding import PartitionSpec as P
 
 F32 = jnp.float32
@@ -11,7 +13,7 @@
     return jnp.einsum(eq, a, b, preferred_element_type=F32)
 
 
-def on_device(tokens, cotangent, scores, routes, w_gate, w_up, w_down):
+def plain_form(tokens, cotangent, scores, routes, w_gate, w_up, w_down):
     tok_count, model_width = tokens.shape
     owners = lax.axis_size("expert")
     groups = lax.axis_size("dp")
@@ -136,6 +138,430 @@
     return (output, grad_tokens, jnp.stack(grad_gate), jnp.stack(grad_up), jnp.stack(grad_down))
 
 
+VMEM_LIMIT = 48 * 1024 * 1024
+
+
+def call(body, outs, ins, scratch=(), flops=0, specs=None):
+    moved = sum(a.size * a.dtype.itemsize for a in ins)
+    moved += sum(o.size * o.dtype.itemsize for o in outs)
+    many = pl.BlockSpec(memory_space=pltpu.VMEM)
+    return pl.pallas_call(
+        body,
+        out_shape=outs,
+        grid=() if specs is None else (1,),
+        in_specs=[many] * len(ins) if specs is None else specs,
+        out_specs=[many] * len(outs),
+        scratch_shapes=list(scratch),
+        compiler_params=pltpu.CompilerParams(vmem_limit_bytes=VMEM_LIMIT),
+        cost_estimate=pl.CostEstimate(flops=flops, bytes_accessed=moved, transcendentals=0),
+    )(*ins)
+
+
+def arr(shape, dtype=BF16):
+    return jax.ShapeDtypeStruct(shape, dtype)
+
+
+def mm(a, b):
+    return jnp.dot(a, b, preferred_element_type=F32)
+
+
+def mm_nt(a, b):
+    return lax.dot_general(a, b, (((1,), (1,)), ((), ())), preferred_element_type=F32)
+
+
+def mm_tn(a, b):
+    return lax.dot_general(a, b, (((0,), (0,)), ((), ())), preferred_element_type=F32)
+
+
+def kernel_form(tokens, cotangent, scores, routes, w_gate, w_up, w_down):
+    toks, model_width = tokens.shape
+    owners, groups = lax.axis_size("expert"), lax.axis_size("dp")
+    local, width, units = w_gate.shape
+    expert_count = local * owners
+    cap = min(toks, 2 * toks // expert_count)
+    held = local * cap
+    slot_total = expert_count * cap
+    pair_rows = groups // 2 * cap
+    half_rows = local * owners * pair_rows
+    block = owners * pair_rows
+    extra = 16
+
+    def shift(value, step):
+        return lax.ppermute(value, "dp", [(j, (j + step) % groups) for j in range(groups)])
+
+    def swap(value, bits):
+        return lax.ppermute(value, "expert", [(j, j ^ bits) for j in range(owners)])
+
+    def near_hop(value):
+        return lax.ppermute(value, "dp", [(0, 1), (3, 2)])
+
+    def far_hop(value):
+        return lax.ppermute(value, "dp", [(1, 2), (2, 1)])
+
+    def back_hop(value):
+        return lax.ppermute(value, "dp", [(1, 0), (2, 3)])
+
+    def group_at(step):
+        return lax.rem(lax.axis_index("dp") + step + groups, groups)
+
+    def columns_at(step):
+        return pl.ds(pl.multiple_of(group_at(step) * width, width), width)
+
+    def pack_body(tok_ref, route_ref, *out_refs):
+        row = lax.broadcasted_iota(jnp.int32, (extra, toks), 0)
+        line = jnp.broadcast_to(route_ref[...].astype(F32), (extra, toks))
+        line = jnp.where(row == 0, line, 0.0).astype(BF16)
+        for step in range(groups):
+            out = out_refs[step]
+            out[0:toks, :] = tok_ref[:, columns_at(step)]
+            out[toks : toks + extra, :] = jnp.zeros((extra, width), BF16)
+            out[toks : toks + extra, 0:toks] = line
+
+    x_pack = call(
+        pack_body, [arr((toks + extra, width))] * groups, [tokens, routes.reshape(1, toks)]
+    )
+    x_got = [x_pack[0]] + [shift(x_pack[step], step) for step in range(1, groups)]
+
+    def slots_row(line):
+        first = lax.broadcasted_iota(jnp.int32, (toks, toks), 0)
+        second = lax.broadcasted_iota(jnp.int32, (toks, toks), 1)
+        whole = jnp.broadcast_to(line, (toks, toks))
+        column = jnp.sum(jnp.where(first == second, whole, 0.0), axis=1, keepdims=True)
+        same = (column == whole) & (first < second)
+        place = jnp.sum(jnp.where(same, 1.0, 0.0), axis=0, keepdims=True)
+        slot = (line * float(cap) + place).astype(jnp.int32)
+        return slot ^ (lax.axis_index("expert") * held)
+
+    def picker(slot):
+        row = lax.broadcasted_iota(jnp.int32, (slot_total, toks), 0)
+        return jnp.where(row == jnp.broadcast_to(slot, (slot_total, toks)), 1.0, 0.0).astype(BF16)
+
+    def send_rows(pick, rows, group, out_refs):
+        sent = mm(pick, rows).astype(BF16)
+        parity, place = lax.rem(group, 2), lax.div(group, 2)
+        rows_at = pl.ds(pl.multiple_of(place * cap, cap), cap)
+        for bits in range(owners):
+            for i in range(local):
+                at = bits * held + i * cap
+                out_refs[bits][parity, i, rows_at, :] = sent[at : at + cap]
+
+    message = arr((2, local, pair_rows, width))
+
+    def dispatch_x_body(*refs):
+        x_refs, cot_ref, score_ref = refs[:groups], refs[groups], refs[groups + 1]
+        outs = refs[groups + 2 :]
+        send_refs, d_refs = outs[:owners], outs[owners : owners + groups]
+        slot_ref, mix_ref, weighted_ref = outs[owners + groups :]
+        for step in range(groups):
+            group = group_at(-step)
+            slot = slots_row(x_refs[step][toks : toks + extra, 0:toks][0:1].astype(F32))
+            slot_ref[pl.ds(group * 8, 8), :] = jnp.broadcast_to(slot, (8, toks))
+            send_rows(picker(slot), x_refs[step][0:toks, :], group, send_refs)
+        score = score_ref[...]
+        mix = score[:, 0:1] / jnp.sum(score, axis=1, keepdims=True)
+        mix_ref[...] = jnp.broadcast_to(mix, mix_ref.shape)
+        weighted_ref[...] = (mix * cot_ref[...].astype(F32)).astype(BF16)
+        for step in range(groups):
+            d_refs[step][...] = weighted_ref[:, columns_at(step)]
+
+    got = call(
+        dispatch_x_body,
+        [message] * owners
+        + [arr((toks, width))] * groups
+        + [arr((groups * 8, toks), jnp.int32), arr((toks, 128), F32)],
+        [*x_got, cotangent, scores],
+        scratch=[pltpu.VMEM((toks, model_width), BF16)],
+        flops=2 * groups * slot_total * toks * width,
+    )
+    x_send, d_pack = got[:owners], got[owners : owners + groups]
+    slots, mix_wide = got[owners + groups :]
+    rows_x = [x_send[0]] + [swap(x_send[bits], bits) for bits in range(1, owners)]
+    d_got = [d_pack[0]] + [shift(d_pack[step], step) for step in range(1, groups)]
+
+    def half_specs(half):
+        return [pl.BlockSpec((1, local, pair_rows, width), lambda *_: (half, 0, 0, 0))] * owners
+
+    full = pl.BlockSpec(memory_space=pltpu.VMEM)
+
+    def expert_rows(refs, i):
+        return jnp.concatenate([r[0, i] for r in refs], axis=0)
+
+    piece = arr((half_rows, units))
+    piece_flops = 2 * half_rows * units * width
+
+    def part_into(out_ref, row_refs, w_ref, product):
+        for i in range(local):
+            out_ref[i * block : (i + 1) * block, :] = product(
+                expert_rows(row_refs, i), w_ref[i]
+            ).astype(BF16)
+
+    def first_body(*refs):
+        rows, gate_ref, up_ref = refs[:owners], refs[owners], refs[owners + 1]
+        part_into(refs[-2], rows, gate_ref, mm)
+        part_into(refs[-1], rows, up_ref, mm)
+
+    part = {}
+    part["g0"], part["u0"] = call(
+        first_body,
+        [piece, piece],
+        [*rows_x, w_gate, w_up],
+        specs=half_specs(0) + [full, full],
+        flops=2 * piece_flops,
+    )
+
+    order = ["g0", "u0", "g1", "u1", "b0", "b1"]
+    near, far, back, pair, total = {}, {}, {}, {}, {}
+    near["g0"], near["u0"] = near_hop(part["g0"]), near_hop(part["u0"])
+
+    def slot_call(number, rows=None, half=0, weight=None, product=None):
+        take = order[number] if number < len(order) else None
+        last = order[number - 1] if number > 0 else None
+        ins, outs = [], []
+        if take:
+            ins += [part[take], near[take]]
+            outs.append(piece)
+        if last:
+            ins += [pair[last], far[last]]
+            outs.append(piece)
+        specs = [full] * len(ins)
+        if rows is not None:
+            ins += [*rows, weight]
+            specs += half_specs(half) + [full]
+            outs.append(piece)
+        count = len(ins)
+
+        def body(*refs):
+            at, to = 0, count
+            for _ in range(bool(take) + bool(last)):
+                refs[to][...] = (refs[at][...].astype(F32) + refs[at + 1][...].astype(F32)).astype(
+                    BF16
+                )
+                at, to = at + 2, to + 1
+            if rows is not None:
+                part_into(refs[to], refs[at : at + owners], refs[at + owners], product)
+
+        got = list(
+            call(body, outs, ins, specs=specs, flops=piece_flops if rows is not None else 0)
+        )
+        if take:
+            pair[take] = got.pop(0)
+            far[take] = far_hop(pair[take])
+        if last:
+            total[last] = got.pop(0)
+            back[last] = back_hop(total[last])
+        if rows is not None:
+            name = order[number + 2]
+            part[name] = got.pop(0)
+            near[name] = near_hop(part[name])
+
+    slot_call(0, rows_x, 1, w_gate, mm)
+
+    def dispatch_d_body(*refs):
+        d_refs, slot_ref, out_refs = refs[:groups], refs[groups], refs[groups + 1 :]
+        for step in range(groups):
+            group = group_at(-step)
+            slot = slot_ref[pl.ds(group * 8, 8), :][0:1]
+            send_rows(picker(slot), d_refs[step][...], group, out_refs)
+
+    d_send = call(
+        dispatch_d_body,
+        [message] * owners,
+        [*d_got, slots],
+        flops=2 * groups * slot_total * toks * width,
+    )
+    rows_d = [d_send[0]] + [swap(d_send[bits], bits) for bits in range(1, owners)]
+
+    slot_call(1, rows_x, 1, w_up, mm)
+    slot_call(2, rows_d, 0, w_down, mm_nt)
+    slot_call(3, rows_d, 1, w_down, mm_nt)
+    slot_call(4)
+    slot_call(5)
+
+    def summed(total_ref, back_ref):
+        place = lax.axis_index("dp")
+        at_end = (place == 0) | (place == groups - 1)
+        return jnp.where(at_end, back_ref[...], total_ref[...]).astype(F32)
+
+    def both(name):
+        return [total[name], back[name]]
+
+    def spread(refs, half, i, value):
+        for bits in range(owners):
+            rows = value[bits * pair_rows : (bits + 1) * pair_rows]
+            if half is None:
+                refs[bits][i] = rows
+            else:
+                refs[bits][half, i] = rows
+
+    def out_body(*refs):
+        w_ref, outs = refs[8], refs[9:]
+        hidden_refs, out_refs = outs[:2], outs[2:]
+        for half in range(2):
+            t = refs[4 * half : 4 * half + 4]
+            gate, up = summed(t[0], t[1]), summed(t[2], t[3])
+            hidden_refs[half][...] = (gate * jax.nn.sigmoid(gate) * up).astype(BF16)
+            for i in range(local):
+                rows = hidden_refs[half][i * block : (i + 1) * block, :]
+                spread(out_refs, half, i, mm(rows, w_ref[i]).astype(BF16))
+
+    got = call(
+        out_body,
+        [piece, piece] + [message] * owners,
+        [*both("g0"), *both("u0"), *both("g1"), *both("u1"), w_down],
+        flops=2 * piece_flops,
+    )
+    hidden, out_send = got[:2], got[2:]
+    out_got = [out_send[0]] + [swap(out_send[bits], bits) for bits in range(1, owners)]
+
+    slot_call(6)
+
+    half_message = arr((local, pair_rows, width))
+
+    def combine(slot_ref, block_of, out_refs, sum_ref):
+        for group in range(groups):
+            place = group // 2 * cap
+            rows = [
+                block_of(bits, group % 2, i, slice(place, place + cap))
+                for bits in range(owners)
+                for i in range(local)
+            ]
+            pick = picker(slot_ref[group * 8 : group * 8 + 1, :])
+            sum_ref[group] = mm_tn(pick, jnp.concatenate(rows, axis=0)).astype(BF16)
+        for step in range(groups):
+            out_refs[step][...] = sum_ref[group_at(-step)]
+
+    def in_call(half, with_out):
+        names = [f"g{half}", f"u{half}", f"b{half}"]
+        ins = [a for n in names for a in both(n)] + [w_gate, w_up]
+        outs = [piece, piece] + [half_message] * owners
+        scratch = []
+        if with_out:
+            ins += [*out_got, slots]
+            outs += [arr((toks, width))] * groups
+            scratch = [pltpu.VMEM((groups, toks, width), BF16)]
+        count = len(ins)
+
+        def body(*refs):
+            gate, up, grad = (summed(refs[2 * n], refs[2 * n + 1]) for n in range(3))
+            gate_w, up_w = refs[6], refs[7]
+            act_refs, in_refs = refs[count : count + 2], refs[count + 2 : count + 2 + owners]
+            sigma = jax.nn.sigmoid(gate)
+            act_refs[0][...] = (grad * up * sigma * (1.0 + gate * (1.0 - sigma))).astype(BF16)
+            act_refs[1][...] = (grad * (gate * sigma)).astype(BF16)
+            for i in range(local):
+                rows = slice(i * block, (i + 1) * block)
+                into = mm_nt(act_refs[0][rows, :], gate_w[i]) + mm_nt(
+                    act_refs[1][rows, :], up_w[i]
+                )
+                spread(in_refs, None, i, into.astype(BF16))
+            if with_out:
+                got_refs, slot_ref = refs[8 : 8 + owners], refs[8 + owners]
+                combine(
+                    slot_ref,
+                    lambda bits, parity, i, rows: got_refs[bits][parity, i, rows, :],
+                    refs[count + 2 + owners : count + 2 + owners + groups],
+                    refs[-1],
+                )
+
+        return call(body, outs, ins, scratch=scratch, flops=2 * piece_flops)
+
+    got0 = in_call(0, False)
+    in_got0 = [got0[2]] + [swap(got0[2 + bits], bits) for bits in range(1, owners)]
+    got1 = in_call(1, True)
+    in_got1 = [got1[2]] + [swap(got1[2 + bits], bits) for bits in range(1, owners)]
+    out_tok = got1[2 + owners :]
+    out_chunk = [out_tok[0]] + [shift(out_tok[step], -step) for step in range(1, groups)]
+
+    def in_tokens_body(*refs):
+        halves = (refs[:owners], refs[owners : 2 * owners])
+        combine(
+            refs[2 * owners],
+            lambda bits, parity, i, rows: halves[parity][bits][i, rows, :],
+            refs[2 * owners + 1 : 2 * owners + 1 + groups],
+            refs[-1],
+        )
+
+    in_tok = call(
+        in_tokens_body,
+        [arr((toks, width))] * groups,
+        [*in_got0, *in_got1, slots],
+        scratch=[pltpu.VMEM((groups, toks, width), BF16)],
+        flops=2 * groups * slot_total * toks * width,
+    )
+    in_chunk = [in_tok[0]] + [shift(in_tok[step], -step) for step in range(1, groups)]
+
+    per_part = groups // 2
+    part_width = per_part * width
+
+    def assemble_body(*refs):
+        chunk_refs, give_ref, keep_ref, whole_ref = refs[:groups], *refs[groups:]
+        for step in range(groups):
+            whole_ref[group_at(step)] = chunk_refs[step][...]
+        mine = lax.axis_index("tensor")
+        for j in range(per_part):
+            at = slice(j * width, (j + 1) * width)
+            give_ref[:, at] = whole_ref[(1 - mine) * per_part + j]
+            keep_ref[:, at] = whole_ref[mine * per_part + j]
+
+    def assemble(chunks):
+        give, keep = call(
+            assemble_body,
+            [arr((toks, part_width))] * 2,
+            chunks,
+            scratch=[pltpu.VMEM((groups, toks, width), BF16)],
+        )
+        other = lax.ppermute(give, "tensor", [(0, 1), (1, 0)])
+        return keep.astype(F32) + other.astype(F32)
+
+    output = (mix_wide[:, 0:1] * assemble(out_chunk)).astype(BF16)
+    grad_tokens = assemble(in_chunk).astype(BF16)
+
+    def weight_grad(left_body, ins, shape):
+        def body(*refs):
+            for i in range(local):
+                left, right = left_body(refs, i)
+                refs[-1][i] = mm_tn(left, right)
+
+        return call(body, [arr(shape, F32)], ins, flops=2 * piece_flops)[0]
+
+    def all_rows(refs, i):
+        return jnp.concatenate([r[half, i] for half in range(2) for r in refs], axis=0)
+
+    def all_units(refs, i):
+        return jnp.concatenate([r[i * block : (i + 1) * block, :] for r in refs], axis=0)
+
+    def by_rows(refs, i):
+        return all_rows(refs[:owners], i), all_units(refs[owners : owners + 2], i)
+
+    def by_units(refs, i):
+        right, left = by_rows(refs, i)
+        return left, right
+
+    grad_gate = weight_grad(by_rows, [*rows_x, got0[0], got1[0]], w_gate.shape)
+    grad_up = weight_grad(by_rows, [*rows_x, got0[1], got1[1]], w_up.shape)
+    grad_down = weight_grad(by_units, [*rows_d, *hidden], w_down.shape)
+    return (output, grad_tokens, grad_gate, grad_up, grad_down)
+
+
+def on_device(tokens, cotangent, scores, routes, w_gate, w_up, w_down):
+    owners = lax.axis_size("expert")
+    toks = tokens.shape[0]
+    cap = min(toks, 2 * toks // (w_gate.shape[0] * owners))
+    held = w_gate.shape[0] * cap
+    fits = (
+        lax.axis_size("dp") == 4
+        and lax.axis_size("tensor") == 2
+        and owners == 4
+        and cap % 16 == 0
+        and held & (held - 1) == 0
+        and toks == 128
+        and w_gate.shape[1] % 128 == 0
+        and w_gate.shape[2] % 128 == 0
+    )
+    form = kernel_form if fits else plain_form
+    return form(tokens, cotangent, scores, routes, w_gate, w_up, w_down)
+
+
 def solution(mesh):
     in_specs = (
         P(("dp", "expert"), None),

time: 219 us -> 232 us (1.059)
  starting transfers between devices: 61.6 us -> 80.1 us
  Pallas kernels: 0 us -> 14.5 us
  matrix products: 11.2 us -> 0 us
  other arithmetic: 11.9 us -> 1.57 us
  local copies, waits for them, and re-layouts: 0.71 us -> 3.75 us
    ppermute x20, starting transfers between devices: 23.4 us -> 50.3 us  [the longest x6 35.3 us: near_hop(): return lax.ppermute(value, 'dp', [(0, 1), (3, 2)])]
    ppermute x15 -> x12, waiting for transfers between devices: 18.4 us -> 34.6 us  [shift(): lax.ppermute(value, 'dp', [(j, (j + step) % groups) for j in range(groups)])]
    ppermute x20, waiting for transfers between devices: 83.3 us -> 67.8 us  [the longest x6 48.7 us: back_hop(): return lax.ppermute(value, 'dp', [(1, 0), (2, 3)])]
    pallas_call x0 -> x20, Pallas kernels: none -> 14.5 us  [call(): pl.pallas_call(body, out_shape=outs, grid=() if specs is None else (1,),...]
    dot_general x29 -> x0, matrix products: 11.2 us -> none  [dot(): return jnp.einsum(eq, a, b, preferred_element_type=F32)]
    ppermute x15 -> x12, starting transfers between devices: 30 us -> 20.9 us  [shift(): lax.ppermute(value, 'dp', [(j, (j + step) % groups) for j in range(groups)])]
    convert_element_type x19 -> x2, other arithmetic: 6.03 us -> 1.57 us  [the longest x1 0.8 us: kernel_form(): output = (mix_wide[:, 0:1] * assemble(out_chunk)).astype(BF16)]
    another operation x11 -> x0, other arithmetic: 4.24 us -> none  [the longest x1 1.26 us: on_device(): jnp.stack(grad_down)]
  transfers between devices with their start and end apart: 47 -> 47, of which waited for: 22 -> 23; matrix products, arithmetic and copies ran while one was open for 8% -> 1% of each run, Pallas kernels for 0% -> 6%
where the time goes in v3:
time: 232 us
  waiting for transfers between devices  131 us (56%)
  starting transfers between devices  80.1 us (35%)
  Pallas kernels  14.5 us (6%)
  local copies, waits for them, and re-layouts  3.75 us (2%)
    ppermute x6, waiting for transfers between devices, back_hop(): return lax.ppermute(value, 'dp', [(1, 0), (2, 3)])  48.7 us
    ppermute x6, starting transfers between devices, near_hop(): return lax.ppermute(value, 'dp', [(0, 1), (3, 2)])  35.3 us
    ppermute x12, waiting for transfers between devices, shift(): lax.ppermute(value, 'dp', [(j, (j + step) % groups) for j in range(groups)])  34.6 us
    ppermute x15, waiting for transfers between devices, swap(): return lax.ppermute(value, 'expert', [(j, j ^ bits) for j in range(owners)])  28.2 us
    ppermute x12, starting transfers between devices, shift(): lax.ppermute(value, 'dp', [(j, (j + step) % groups) for j in range(groups)])  20.9 us
    ppermute x6, waiting for transfers between devices, near_hop(): return lax.ppermute(value, 'dp', [(0, 1), (3, 2)])  15.4 us
    pallas_call x20, Pallas kernels, call(): pl.pallas_call(body, out_shape=outs, grid=() if specs is None else (1,),...  14.5 us
    ppermute x15, starting transfers between devices, swap(): return lax.ppermute(value, 'expert', [(j, j ^ bits) for j in range(owners)])  8.9 us
  transfers between devices with their start and end apart: 47, of which 23 were waited for; matrix products, arithmetic and copies ran while one was open for 1% of the time, Pallas kernels for 6%

profile of v3, /device:TPU:0, one launch (start us, length us, event | category | flops | bytes accessed | tf_op | source)
XLA Modules:
  0.0 231.5 jit_solution(853409376846540671)
XLA Ops:
  2.5 3.1 %collective-permute-start = (bf16[144,512]{1,0:T(8,128)(2,1)S(1)}, bf16[144,512]{1,0:T(8,128)(2,1)S(1)}, u32[]{:S(2)}, u32[]{:S(2)}) collective-permute-start(bf16[144,512]{1,0:T(8,128)(2,1)S(1)} %get-tuple-element.71), channel_id=1, source_target_pairs={{0,8},{8,16},{16,24},{24,0},{1,9},{9,17},{17,25},{25,1},{2,10},{10... | collective-permute-start | bytes 442376 | tf_op jit(solution)/shard_map/ppermute | solution.py:190
  12.4 5.5 %collective-permute-done.1.refs_2_ = bf16[144,512]{1,0:T(8,128)(2,1)S(1)} collective-permute-done((bf16[144,512]{1,0:T(8,128)(2,1)S(1)}, bf16[144,512]{1,0:T(8,128)(2,1)S(1)}, u32[]{:S(2)}, u32[]{:S(2)}) %collective-permute-start.1) | collective-permute-done | bytes 147488 | tf_op jit(solution)/shard_map/ppermute | solution.py:190
  21.5 7.3 %collective-permute-done.4.refs_2_.refs_4_.refs_6_ = bf16[2,2,64,512]{3,2,1,0:T(8,128)(2,1)S(1)} collective-permute-done((bf16[2,2,64,512]{3,2,1,0:T(8,128)(2,1)S(1)}, bf16[2,2,64,512]{3,2,1,0:T(8,128)(2,1)S(1)}, u32[]{:S(2)}, u32[]{:S(2)}) %collective-permute-start.4) | collective-permute-done | bytes 262176 | tf_op jit(solution)/shard_map/ppermute | solution.py:193
  28.8 4.7 %collective-permute-done.5.refs_3_.refs_5_.refs_7_ = bf16[2,2,64,512]{3,2,1,0:T(8,128)(2,1)S(1)} collective-permute-done((bf16[2,2,64,512]{3,2,1,0:T(8,128)(2,1)S(1)}, bf16[2,2,64,512]{3,2,1,0:T(8,128)(2,1)S(1)}, u32[]{:S(2)}, u32[]{:S(2)}) %collective-permute-start.5) | collective-permute-done | bytes 262176 | tf_op jit(solution)/shard_map/ppermute | solution.py:193
  34.2 5.5 %collective-permute-start.7 = (bf16[512,384]{1,0:T(8,128)(2,1)S(1)}, bf16[512,384]{1,0:T(8,128)(2,1)S(1)}, u32[]{:S(2)}, u32[]{:S(2)}) collective-permute-start(bf16[512,384]{1,0:T(8,128)(2,1)S(1)} %get-tuple-element.80.refs_0_), channel_id=1, source_target_pairs={{0,8},{24,16},{1,9},{25,17},{2,10},{26,18},{3,11},{27,19},{4,12},{... | collective-permute-start | bytes 1179656 | tf_op jit(solution)/shard_map/ppermute | solution.py:196
  41.1 8.1 %collective-permute-done.7.refs_1_ = bf16[512,384]{1,0:T(8,128)(2,1)S(1)} collective-permute-done((bf16[512,384]{1,0:T(8,128)(2,1)S(1)}, bf16[512,384]{1,0:T(8,128)(2,1)S(1)}, u32[]{:S(2)}, u32[]{:S(2)}) %collective-permute-start.7) | collective-permute-done | bytes 393248 | tf_op jit(solution)/shard_map/ppermute | solution.py:196
  50.4 3.8 %collective-permute-start.12 = (bf16[128,512]{1,0:T(8,128)(2,1)S(1)}, bf16[128,512]{1,0:T(8,128)(2,1)S(1)}, u32[]{:S(2)}, u32[]{:S(2)}) collective-permute-start(bf16[128,512]{1,0:T(8,128)(2,1)S(1)} %get-tuple-element.86), channel_id=1, source_target_pairs={{0,8},{8,16},{16,24},{24,0},{1,9},{9,17},{17,25},{25,1},{2,10},{10... | collective-permute-start | bytes 393224 | tf_op jit(solution)/shard_map/ppermute | solution.py:190
  55.7 2.8 %collective-permute-start.14 = (bf16[128,512]{1,0:T(8,128)(2,1)S(1)}, bf16[128,512]{1,0:T(8,128)(2,1)S(1)}, u32[]{:S(2)}, u32[]{:S(2)}) collective-permute-start(bf16[128,512]{1,0:T(8,128)(2,1)S(1)} %get-tuple-element.88), channel_id=1, source_target_pairs={{0,24},{8,0},{16,8},{24,16},{1,25},{9,1},{17,9},{25,17},{2,26},{10... | collective-permute-start | bytes 393224 | tf_op jit(solution)/shard_map/ppermute | solution.py:190
  58.6 3.6 %collective-permute-start.10 = (bf16[512,384]{1,0:T(8,128)(2,1)S(1)}, bf16[512,384]{1,0:T(8,128)(2,1)S(1)}, u32[]{:S(2)}, u32[]{:S(2)}) collective-permute-start(bf16[512,384]{1,0:T(8,128)(2,1)S(1)} %get-tuple-element.83.refs_0_), channel_id=1, source_target_pairs={{0,8},{24,16},{1,9},{25,17},{2,10},{26,18},{3,11},{27,19},{4,12},{... | collective-permute-start | bytes 1179656 | tf_op jit(solution)/shard_map/ppermute | solution.py:196
  63.5 10.5 %collective-permute-done.13.refs_2_ = bf16[128,512]{1,0:T(8,128)(2,1)S(1)} collective-permute-done((bf16[128,512]{1,0:T(8,128)(2,1)S(1)}, bf16[128,512]{1,0:T(8,128)(2,1)S(1)}, u32[]{:S(2)}, u32[]{:S(2)}) %collective-permute-start.13) | collective-permute-done | bytes 131104 | tf_op jit(solution)/shard_map/ppermute | solution.py:190
  76.4 5.3 %collective-permute-start.9 = (bf16[512,384]{1,0:T(8,128)(2,1)S(1)}, bf16[512,384]{1,0:T(8,128)(2,1)S(1)}, u32[]{:S(2)}, u32[]{:S(2)}) collective-permute-start(bf16[512,384]{1,0:T(8,128)(2,1)S(1)} %get-tuple-element.82.refs_0_), channel_id=1, source_target_pairs={{0,8},{24,16},{1,9},{25,17},{2,10},{26,18},{3,11},{27,19},{4,12},{... | collective-permute-start | bytes 1179656 | tf_op jit(solution)/shard_map/ppermute | solution.py:196
  83.7 4.7 %collective-permute-done.17.refs_7_.refs_3_ = bf16[2,2,64,512]{3,2,1,0:T(8,128)(2,1)S(1)} collective-permute-done((bf16[2,2,64,512]{3,2,1,0:T(8,128)(2,1)S(1)}, bf16[2,2,64,512]{3,2,1,0:T(8,128)(2,1)S(1)}, u32[]{:S(2)}, u32[]{:S(2)}) %collective-permute-start.17) | collective-permute-done | bytes 262176 | tf_op jit(solution)/shard_map/ppermute | solution.py:193
  89.8 6.5 %collective-permute-start.20 = (bf16[512,384]{1,0:T(8,128)(2,1)S(1)}, bf16[512,384]{1,0:T(8,128)(2,1)S(1)}, u32[]{:S(2)}, u32[]{:S(2)}) collective-permute-start(bf16[512,384]{1,0:T(8,128)(2,1)S(1)} %get-tuple-element.96.refs_0_), channel_id=1, source_target_pairs={{0,8},{24,16},{1,9},{25,17},{2,10},{26,18},{3,11},{27,19},{4,12},{... | collective-permute-start | bytes 1179656 | tf_op jit(solution)/shard_map/ppermute | solution.py:196
  97.7 13.0 %collective-permute-start.23 = (bf16[512,384]{1,0:T(8,128)(2,1)S(1)}, bf16[512,384]{1,0:T(8,128)(2,1)S(1)}, u32[]{:S(2)}, u32[]{:S(2)}) collective-permute-start(bf16[512,384]{1,0:T(8,128)(2,1)S(1)} %get-tuple-element.99.refs_0_), channel_id=1, source_target_pairs={{0,8},{24,16},{1,9},{25,17},{2,10},{26,18},{3,11},{27,19},{4,12},{... | collective-permute-start | bytes 1179656 | tf_op jit(solution)/shard_map/ppermute | solution.py:196
  111.7 7.3 %collective-permute-done.23.refs_1_ = bf16[512,384]{1,0:T(8,128)(2,1)S(1)} collective-permute-done((bf16[512,384]{1,0:T(8,128)(2,1)S(1)}, bf16[512,384]{1,0:T(8,128)(2,1)S(1)}, u32[]{:S(2)}, u32[]{:S(2)}) %collective-permute-start.23) | collective-permute-done | bytes 393248 | tf_op jit(solution)/shard_map/ppermute | solution.py:196
  126.5 19.0 %collective-permute-done.27.refs_1_ = bf16[512,384]{1,0:T(8,128)(2,1)S(1)} collective-permute-done((bf16[512,384]{1,0:T(8,128)(2,1)S(1)}, bf16[512,384]{1,0:T(8,128)(2,1)S(1)}, u32[]{:S(2)}, u32[]{:S(2)}) %collective-permute-start.27) | collective-permute-done | bytes 393248 | tf_op jit(solution)/shard_map/ppermute | solution.py:202
  146.8 7.1 %collective-permute-done.28.refs_3_ = bf16[512,384]{1,0:T(8,128)(2,1)S(1)} collective-permute-done((bf16[512,384]{1,0:T(8,128)(2,1)S(1)}, bf16[512,384]{1,0:T(8,128)(2,1)S(1)}, u32[]{:S(2)}, u32[]{:S(2)}) %collective-permute-start.28) | collective-permute-done | bytes 393248 | tf_op jit(solution)/shard_map/ppermute | solution.py:202
  153.9 8.4 %collective-permute-done.19.refs_5_.refs_1_ = bf16[512,384]{1,0:T(8,128)(2,1)S(1)} collective-permute-done((bf16[512,384]{1,0:T(8,128)(2,1)S(1)}, bf16[512,384]{1,0:T(8,128)(2,1)S(1)}, u32[]{:S(2)}, u32[]{:S(2)}) %collective-permute-start.19) | collective-permute-done | bytes 393248 | tf_op jit(solution)/shard_map/ppermute | solution.py:202
  162.3 8.4 %collective-permute-done.22.refs_7_.refs_3_ = bf16[512,384]{1,0:T(8,128)(2,1)S(1)} collective-permute-done((bf16[512,384]{1,0:T(8,128)(2,1)S(1)}, bf16[512,384]{1,0:T(8,128)(2,1)S(1)}, u32[]{:S(2)}, u32[]{:S(2)}) %collective-permute-start.22) | collective-permute-done | bytes 393248 | tf_op jit(solution)/shard_map/ppermute | solution.py:202
  173.5 5.7 %collective-permute-done.36.refs_5_ = bf16[512,384]{1,0:T(8,128)(2,1)S(1)} collective-permute-done((bf16[512,384]{1,0:T(8,128)(2,1)S(1)}, bf16[512,384]{1,0:T(8,128)(2,1)S(1)}, u32[]{:S(2)}, u32[]{:S(2)}) %collective-permute-start.36) | collective-permute-done | bytes 393248 | tf_op jit(solution)/shard_map/ppermute | solution.py:202
  180.8 4.7 %collective-permute-done.31.refs_11_ = bf16[2,2,64,512]{3,2,1,0:T(8,128)(2,1)S(1)} collective-permute-done((bf16[2,2,64,512]{3,2,1,0:T(8,128)(2,1)S(1)}, bf16[2,2,64,512]{3,2,1,0:T(8,128)(2,1)S(1)}, u32[]{:S(2)}, u32[]{:S(2)}) %collective-permute-start.31) | collective-permute-done | bytes 262176 | tf_op jit(solution)/shard_map/ppermute | solution.py:193
  193.8 8.0 %collective-permute-done.33.refs_2_ = bf16[128,512]{1,0:T(8,128)(2,1)S(1)} collective-permute-done((bf16[128,512]{1,0:T(8,128)(2,1)S(1)}, bf16[128,512]{1,0:T(8,128)(2,1)S(1)}, u32[]{:S(2)}, u32[]{:S(2)}) %collective-permute-start.33) | collective-permute-done | bytes 131104 | tf_op jit(solution)/shard_map/ppermute | solution.py:190
  216.5 6.3 %collective-permute-done.44.refs_2_ = bf16[128,512]{1,0:T(8,128)(2,1)S(1)} collective-permute-done((bf16[128,512]{1,0:T(8,128)(2,1)S(1)}, bf16[128,512]{1,0:T(8,128)(2,1)S(1)}, u32[]{:S(2)}, u32[]{:S(2)}) %collective-permute-start.44) | collective-permute-done | bytes 131104 | tf_op jit(solution)/shard_map/ppermute | solution.py:190
  227.2 3.6 %collective-permute-done.46 = bf16[128,1024]{1,0:T(8,128)(2,1)S(1)} collective-permute-done((bf16[128,1024]{1,0:T(8,128)(2,1)S(1)}, bf16[128,1024]{1,0:T(8,128)(2,1)S(1)}, u32[]{:S(2)}, u32[]{:S(2)}) %collective-permute-start.46) | collective-permute-done | bytes 262176 | tf_op jit(solution)/shard_map/ppermute | solution.py:513
  (106 shorter events, 67.4 us)
Async XLA Ops:
  21.1 12.3 %collective-permute-start.5 = (bf16[2,2,64,512]{3,2,1,0:T(8,128)(2,1)S(1)}, bf16[2,2,64,512]{3,2,1,0:T(8,128)(2,1)S(1)}, u32[]{:S(2)}, u32[]{:S(2)}) collective-permute-start(bf16[2,2,64,512]{3,2,1,0:T(8,128)(2,1)S(1)} %get-tuple-element.78), channel_id=1, source_target_pairs={{0,6},{2,4},{4,2},{6,0},{1,7},{3,5},{5,3},{7,1},{8,14},{10,12},{12... | collective-permute-start | bytes 786440 | tf_op jit(solution)/shard_map/ppermute | solution.py:193
  34.2 15.0 %collective-permute-start.7 = (bf16[512,384]{1,0:T(8,128)(2,1)S(1)}, bf16[512,384]{1,0:T(8,128)(2,1)S(1)}, u32[]{:S(2)}, u32[]{:S(2)}) collective-permute-start(bf16[512,384]{1,0:T(8,128)(2,1)S(1)} %get-tuple-element.80.refs_0_), channel_id=1, source_target_pairs={{0,8},{24,16},{1,9},{25,17},{2,10},{26,18},{3,11},{27,19},{4,12},{... | collective-permute-start | bytes 1179656 | tf_op jit(solution)/shard_map/ppermute | solution.py:196
  39.8 18.8 %collective-permute-start.6 = (bf16[512,384]{1,0:T(8,128)(2,1)S(1)}, bf16[512,384]{1,0:T(8,128)(2,1)S(1)}, u32[]{:S(2)}, u32[]{:S(2)}) collective-permute-start(bf16[512,384]{1,0:T(8,128)(2,1)S(1)} %get-tuple-element.79.refs_0_), channel_id=1, source_target_pairs={{0,8},{24,16},{1,9},{25,17},{2,10},{26,18},{3,11},{27,19},{4,12},{... | collective-permute-start | bytes 1179656 | tf_op jit(solution)/shard_map/ppermute | solution.py:196
  49.7 12.4 %collective-permute-start.8 = (bf16[512,384]{1,0:T(8,128)(2,1)S(1)}, bf16[512,384]{1,0:T(8,128)(2,1)S(1)}, u32[]{:S(2)}, u32[]{:S(2)}) collective-permute-start(bf16[512,384]{1,0:T(8,128)(2,1)S(1)} %get-tuple-element.81.refs_2_), channel_id=1, source_target_pairs={{8,16},{16,8},{9,17},{17,9},{10,18},{18,10},{11,19},{19,11},{12,20... | collective-permute-start | bytes 1179656 | tf_op jit(solution)/shard_map/ppermute | solution.py:199
  50.4 13.1 %collective-permute-start.12 = (bf16[128,512]{1,0:T(8,128)(2,1)S(1)}, bf16[128,512]{1,0:T(8,128)(2,1)S(1)}, u32[]{:S(2)}, u32[]{:S(2)}) collective-permute-start(bf16[128,512]{1,0:T(8,128)(2,1)S(1)} %get-tuple-element.86), channel_id=1, source_target_pairs={{0,8},{8,16},{16,24},{24,0},{1,9},{9,17},{17,25},{25,1},{2,10},{10... | collective-permute-start | bytes 393224 | tf_op jit(solution)/shard_map/ppermute | solution.py:190
  54.2 19.8 %collective-permute-start.13 = (bf16[128,512]{1,0:T(8,128)(2,1)S(1)}, bf16[128,512]{1,0:T(8,128)(2,1)S(1)}, u32[]{:S(2)}, u32[]{:S(2)}) collective-permute-start(bf16[128,512]{1,0:T(8,128)(2,1)S(1)} %get-tuple-element.87), channel_id=1, source_target_pairs={{0,16},{8,24},{16,0},{24,8},{1,17},{9,25},{17,1},{25,9},{2,18},{10... | collective-permute-start | bytes 393224 | tf_op jit(solution)/shard_map/ppermute | solution.py:190
  55.7 18.3 %collective-permute-start.14 = (bf16[128,512]{1,0:T(8,128)(2,1)S(1)}, bf16[128,512]{1,0:T(8,128)(2,1)S(1)}, u32[]{:S(2)}, u32[]{:S(2)}) collective-permute-start(bf16[128,512]{1,0:T(8,128)(2,1)S(1)} %get-tuple-element.88), channel_id=1, source_target_pairs={{0,24},{8,0},{16,8},{24,16},{1,25},{9,1},{17,9},{25,17},{2,26},{10... | collective-permute-start | bytes 393224 | tf_op jit(solution)/shard_map/ppermute | solution.py:190
  58.6 29.8 %collective-permute-start.10 = (bf16[512,384]{1,0:T(8,128)(2,1)S(1)}, bf16[512,384]{1,0:T(8,128)(2,1)S(1)}, u32[]{:S(2)}, u32[]{:S(2)}) collective-permute-start(bf16[512,384]{1,0:T(8,128)(2,1)S(1)} %get-tuple-element.83.refs_0_), channel_id=1, source_target_pairs={{0,8},{24,16},{1,9},{25,17},{2,10},{26,18},{3,11},{27,19},{4,12},{... | collective-permute-start | bytes 1179656 | tf_op jit(solution)/shard_map/ppermute | solution.py:196
  62.8 25.6 %collective-permute-start.11 = (bf16[512,384]{1,0:T(8,128)(2,1)S(1)}, bf16[512,384]{1,0:T(8,128)(2,1)S(1)}, u32[]{:S(2)}, u32[]{:S(2)}) collective-permute-start(bf16[512,384]{1,0:T(8,128)(2,1)S(1)} %get-tuple-element.84.refs_2_), channel_id=1, source_target_pairs={{8,16},{16,8},{9,17},{17,9},{10,18},{18,10},{11,19},{19,11},{12,20... | collective-permute-start | bytes 1179656 | tf_op jit(solution)/shard_map/ppermute | solution.py:199
  76.1 12.3 %collective-permute-start.17 = (bf16[2,2,64,512]{3,2,1,0:T(8,128)(2,1)S(1)}, bf16[2,2,64,512]{3,2,1,0:T(8,128)(2,1)S(1)}, u32[]{:S(2)}, u32[]{:S(2)}) collective-permute-start(bf16[2,2,64,512]{3,2,1,0:T(8,128)(2,1)S(1)} %get-tuple-element.93), channel_id=1, source_target_pairs={{0,6},{2,4},{4,2},{6,0},{1,7},{3,5},{5,3},{7,1},{8,14},{10,12},{12... | collective-permute-start | bytes 786440 | tf_op jit(solution)/shard_map/ppermute | solution.py:193
  76.4 19.9 %collective-permute-start.9 = (bf16[512,384]{1,0:T(8,128)(2,1)S(1)}, bf16[512,384]{1,0:T(8,128)(2,1)S(1)}, u32[]{:S(2)}, u32[]{:S(2)}) collective-permute-start(bf16[512,384]{1,0:T(8,128)(2,1)S(1)} %get-tuple-element.82.refs_0_), channel_id=1, source_target_pairs={{0,8},{24,16},{1,9},{25,17},{2,10},{26,18},{3,11},{27,19},{4,12},{... | collective-permute-start | bytes 1179656 | tf_op jit(solution)/shard_map/ppermute | solution.py:196
  89.8 21.0 %collective-permute-start.20 = (bf16[512,384]{1,0:T(8,128)(2,1)S(1)}, bf16[512,384]{1,0:T(8,128)(2,1)S(1)}, u32[]{:S(2)}, u32[]{:S(2)}) collective-permute-start(bf16[512,384]{1,0:T(8,128)(2,1)S(1)} %get-tuple-element.96.refs_0_), channel_id=1, source_target_pairs={{0,8},{24,16},{1,9},{25,17},{2,10},{26,18},{3,11},{27,19},{4,12},{... | collective-permute-start | bytes 1179656 | tf_op jit(solution)/shard_map/ppermute | solution.py:196
  97.0 13.8 %collective-permute-start.21 = (bf16[512,384]{1,0:T(8,128)(2,1)S(1)}, bf16[512,384]{1,0:T(8,128)(2,1)S(1)}, u32[]{:S(2)}, u32[]{:S(2)}) collective-permute-start(bf16[512,384]{1,0:T(8,128)(2,1)S(1)} %get-tuple-element.97.refs_2_), channel_id=1, source_target_pairs={{8,16},{16,8},{9,17},{17,9},{10,18},{18,10},{11,19},{19,11},{12,20... | collective-permute-start | bytes 1179656 | tf_op jit(solution)/shard_map/ppermute | solution.py:199
  97.7 21.3 %collective-permute-start.23 = (bf16[512,384]{1,0:T(8,128)(2,1)S(1)}, bf16[512,384]{1,0:T(8,128)(2,1)S(1)}, u32[]{:S(2)}, u32[]{:S(2)}) collective-permute-start(bf16[512,384]{1,0:T(8,128)(2,1)S(1)} %get-tuple-element.99.refs_0_), channel_id=1, source_target_pairs={{0,8},{24,16},{1,9},{25,17},{2,10},{26,18},{3,11},{27,19},{4,12},{... | collective-permute-start | bytes 1179656 | tf_op jit(solution)/shard_map/ppermute | solution.py:196
  119.9 25.6 %collective-permute-start.27 = (bf16[512,384]{1,0:T(8,128)(2,1)S(1)}, bf16[512,384]{1,0:T(8,128)(2,1)S(1)}, u32[]{:S(2)}, u32[]{:S(2)}) collective-permute-start(bf16[512,384]{1,0:T(8,128)(2,1)S(1)} %get-tuple-element.102.refs_0_), channel_id=1, source_target_pairs={{8,0},{16,24},{9,1},{17,25},{10,2},{18,26},{11,3},{19,27},{12,4},{... | collective-permute-start | bytes 1179656 | tf_op jit(solution)/shard_map/ppermute | solution.py:202
  121.2 32.7 %collective-permute-start.28 = (bf16[512,384]{1,0:T(8,128)(2,1)S(1)}, bf16[512,384]{1,0:T(8,128)(2,1)S(1)}, u32[]{:S(2)}, u32[]{:S(2)}) collective-permute-start(bf16[512,384]{1,0:T(8,128)(2,1)S(1)} %get-tuple-element.103.refs_2_), channel_id=1, source_target_pairs={{8,0},{16,24},{9,1},{17,25},{10,2},{18,26},{11,3},{19,27},{12,4},{... | collective-permute-start | bytes 1179656 | tf_op jit(solution)/shard_map/ppermute | solution.py:202
  122.5 39.9 %collective-permute-start.19 = (bf16[512,384]{1,0:T(8,128)(2,1)S(1)}, bf16[512,384]{1,0:T(8,128)(2,1)S(1)}, u32[]{:S(2)}, u32[]{:S(2)}) collective-permute-start(bf16[512,384]{1,0:T(8,128)(2,1)S(1)} %get-tuple-element.95.refs_4_.refs_0_), channel_id=1, source_target_pairs={{8,0},{16,24},{9,1},{17,25},{10,2},{18,26},{11,3},{19,27},{12,4},{... | collective-permute-start | bytes 1179656 | tf_op jit(solution)/shard_map/ppermute | solution.py:202
  123.8 47.0 %collective-permute-start.22 = (bf16[512,384]{1,0:T(8,128)(2,1)S(1)}, bf16[512,384]{1,0:T(8,128)(2,1)S(1)}, u32[]{:S(2)}, u32[]{:S(2)}) collective-permute-start(bf16[512,384]{1,0:T(8,128)(2,1)S(1)} %get-tuple-element.98.refs_6_.refs_2_), channel_id=1, source_target_pairs={{8,0},{16,24},{9,1},{17,25},{10,2},{18,26},{11,3},{19,27},{12,4},{... | collective-permute-start | bytes 1179656 | tf_op jit(solution)/shard_map/ppermute | solution.py:202
  125.1 54.1 %collective-permute-start.36 = (bf16[512,384]{1,0:T(8,128)(2,1)S(1)}, bf16[512,384]{1,0:T(8,128)(2,1)S(1)}, u32[]{:S(2)}, u32[]{:S(2)}) collective-permute-start(bf16[512,384]{1,0:T(8,128)(2,1)S(1)} %get-tuple-element.114.refs_4_), channel_id=1, source_target_pairs={{8,0},{16,24},{9,1},{17,25},{10,2},{18,26},{11,3},{19,27},{12,4},{... | collective-permute-start | bytes 1179656 | tf_op jit(solution)/shard_map/ppermute | solution.py:202
  145.5 40.0 %collective-permute-start.26 = (bf16[512,384]{1,0:T(8,128)(2,1)S(1)}, bf16[512,384]{1,0:T(8,128)(2,1)S(1)}, u32[]{:S(2)}, u32[]{:S(2)}) collective-permute-start(bf16[512,384]{1,0:T(8,128)(2,1)S(1)} %shard_map.120.refs_4_), channel_id=1, source_target_pairs={{8,0},{16,24},{9,1},{17,25},{10,2},{18,26},{11,3},{19,27},{12,4},{... | collective-permute-start | bytes 1179656 | tf_op jit(solution)/shard_map/ppermute | solution.py:202
  189.9 13.4 %collective-permute-start.34 = (bf16[128,512]{1,0:T(8,128)(2,1)S(1)}, bf16[128,512]{1,0:T(8,128)(2,1)S(1)}, u32[]{:S(2)}, u32[]{:S(2)}) collective-permute-start(bf16[128,512]{1,0:T(8,128)(2,1)S(1)} %get-tuple-element.111), channel_id=1, source_target_pairs={{0,8},{8,16},{16,24},{24,0},{1,9},{9,17},{17,25},{25,1},{2,10},{10... | collective-permute-start | bytes 393224 | tf_op jit(solution)/shard_map/ppermute | solution.py:190
  190.5 12.9 %collective-permute-start.38 = (bf16[2,64,512]{2,1,0:T(8,128)(2,1)S(1)}, bf16[2,64,512]{2,1,0:T(8,128)(2,1)S(1)}, u32[]{:S(2)}, u32[]{:S(2)}) collective-permute-start(bf16[2,64,512]{2,1,0:T(8,128)(2,1)S(1)} %get-tuple-element.117), channel_id=1, source_target_pairs={{0,4},{2,6},{4,0},{6,2},{1,5},{3,7},{5,1},{7,3},{8,12},{10,14},{12... | collective-permute-start | bytes 393224 | tf_op jit(solution)/shard_map/ppermute | solution.py:193
  192.0 12.9 %collective-permute-start.39 = (bf16[2,64,512]{2,1,0:T(8,128)(2,1)S(1)}, bf16[2,64,512]{2,1,0:T(8,128)(2,1)S(1)}, u32[]{:S(2)}, u32[]{:S(2)}) collective-permute-start(bf16[2,64,512]{2,1,0:T(8,128)(2,1)S(1)} %get-tuple-element.118), channel_id=1, source_target_pairs={{0,6},{2,4},{4,2},{6,0},{1,7},{3,5},{5,3},{7,1},{8,14},{10,12},{12... | collective-permute-start | bytes 393224 | tf_op jit(solution)/shard_map/ppermute | solution.py:193
  203.4 23.0 %collective-permute-start.35 = (bf16[128,1024]{1,0:T(8,128)(2,1)S(1)}, bf16[128,1024]{1,0:T(8,128)(2,1)S(1)}, u32[]{:S(2)}, u32[]{:S(2)}) collective-permute-start(bf16[128,1024]{1,0:T(8,128)(2,1)S(1)} %get-tuple-element.113), channel_id=1, source_target_pairs={{0,1},{1,0},{2,3},{3,2},{4,5},{5,4},{6,7},{7,6},{8,9},{9,8},{10,11... | collective-permute-start | bytes 786440 | tf_op jit(solution)/shard_map/ppermute | solution.py:513
  (29 other events, 295.6 us)

commit v4 on v3

--- a/solution.py
+++ b/solution.py
@@ -278,67 +278,93 @@
     rows_x = [x_send[0]] + [swap(x_send[bits], bits) for bits in range(1, owners)]
     d_got = [d_pack[0]] + [shift(d_pack[step], step) for step in range(1, groups)]
 
-    def half_specs(half):
-        return [pl.BlockSpec((1, local, pair_rows, width), lambda *_: (half, 0, 0, 0))] * owners
-
     full = pl.BlockSpec(memory_space=pltpu.VMEM)
-
-    def expert_rows(refs, i):
-        return jnp.concatenate([r[0, i] for r in refs], axis=0)
-
     piece = arr((half_rows, units))
     piece_flops = 2 * half_rows * units * width
-
-    def part_into(out_ref, row_refs, w_ref, product):
+    dispatch_flops = 2 * groups * slot_total * toks * width
+    packed = arr((2, local, block, width))
+    half_packed = pl.BlockSpec((1, local, block, width), lambda *_: (0, 0, 0, 0))
+    other_packed = pl.BlockSpec((1, local, block, width), lambda *_: (1, 0, 0, 0))
+
+    def pack_rows(out_ref, refs):
+        for half in range(2):
+            for i in range(local):
+                for bits in range(owners):
+                    at = slice(bits * pair_rows, (bits + 1) * pair_rows)
+                    out_ref[half, i, at, :] = refs[bits][half, i]
+
+    def part_into(out_ref, rows_ref, w_ref, product, half=0):
         for i in range(local):
-            out_ref[i * block : (i + 1) * block, :] = product(
-                expert_rows(row_refs, i), w_ref[i]
-            ).astype(BF16)
+            out_ref[i * block : (i + 1) * block, :] = product(rows_ref[half, i], w_ref[i]).astype(
+                BF16
+            )
 
     def first_body(*refs):
-        rows, gate_ref, up_ref = refs[:owners], refs[owners], refs[owners + 1]
-        part_into(refs[-2], rows, gate_ref, mm)
-        part_into(refs[-1], rows, up_ref, mm)
+        x_refs, gate_ref, up_ref = refs[:owners], refs[owners], refs[owners + 1]
+        d_refs, slot_ref = refs[owners + 2 : owners + 2 + groups], refs[owners + 2 + groups]
+        outs = refs[owners + 3 + groups :]
+        pack_rows(outs[2], x_refs)
+        part_into(outs[0], outs[2], gate_ref, mm)
+        part_into(outs[1], outs[2], up_ref, mm)
+        for step in range(groups):
+            group = group_at(-step)
+            slot = slot_ref[pl.ds(group * 8, 8), :][0:1]
+            send_rows(picker(slot), d_refs[step][...], group, outs[3:])
 
     part = {}
-    part["g0"], part["u0"] = call(
+    got = call(
         first_body,
-        [piece, piece],
-        [*rows_x, w_gate, w_up],
-        specs=half_specs(0) + [full, full],
-        flops=2 * piece_flops,
-    )
+        [piece, piece, packed] + [message] * owners,
+        [*rows_x, w_gate, w_up, *d_got, slots],
+        flops=2 * piece_flops + dispatch_flops,
+    )
+    part["g0"], part["u0"], packed_x = got[:3]
+    d_send = got[3:]
 
     order = ["g0", "u0", "g1", "u1", "b0", "b1"]
-    near, far, back, pair, total = {}, {}, {}, {}, {}
+    near, far, back, pair, total, final = {}, {}, {}, {}, {}, {}
     near["g0"], near["u0"] = near_hop(part["g0"]), near_hop(part["u0"])
-
-    def slot_call(number, rows=None, half=0, weight=None, product=None):
+    rows_d = [d_send[0]] + [swap(d_send[bits], bits) for bits in range(1, owners)]
+
+    def at_end():
+        place = lax.axis_index("dp")
+        return (place == 0) | (place == groups - 1)
+
+    def slot_call(number, rows=None, half=0, weight=None, product=None, unpacked=None):
         take = order[number] if number < len(order) else None
-        last = order[number - 1] if number > 0 else None
+        last = order[number - 1] if 0 < number <= len(order) else None
+        done = order[number - 2] if 1 < number else None
         ins, outs = [], []
-        if take:
-            ins += [part[take], near[take]]
-            outs.append(piece)
-        if last:
-            ins += [pair[last], far[last]]
-            outs.append(piece)
+        for name, left, right in ((take, part, near), (last, pair, far), (done, total, back)):
+            if name:
+                ins += [left[name], right[name]]
+                outs.append(piece)
         specs = [full] * len(ins)
         if rows is not None:
-            ins += [*rows, weight]
-            specs += half_specs(half) + [full]
+            ins += [rows, weight]
+            specs += [other_packed if half else half_packed, full]
             outs.append(piece)
+        if unpacked is not None:
+            ins += unpacked
+            specs += [full] * owners
+            outs.append(packed)
         count = len(ins)
 
         def body(*refs):
             at, to = 0, count
-            for _ in range(bool(take) + bool(last)):
-                refs[to][...] = (refs[at][...].astype(F32) + refs[at + 1][...].astype(F32)).astype(
-                    BF16
-                )
+            for name in (take, last):
+                if name:
+                    both = refs[at][...].astype(F32) + refs[at + 1][...].astype(F32)
+                    refs[to][...] = both.astype(BF16)
+                    at, to = at + 2, to + 1
+            if done:
+                refs[to][...] = jnp.where(at_end(), refs[at + 1][...], refs[at][...])
                 at, to = at + 2, to + 1
             if rows is not None:
-                part_into(refs[to], refs[at : at + owners], refs[at + owners], product)
+                part_into(refs[to], refs[at], refs[at + 1], product)
+                at, to = at + 2, to + 1
+            if unpacked is not None:
+                pack_rows(refs[to], refs[at : at + owners])
 
         got = list(
             call(body, outs, ins, specs=specs, flops=piece_flops if rows is not None else 0)
@@ -349,41 +375,20 @@
         if last:
             total[last] = got.pop(0)
             back[last] = back_hop(total[last])
+        if done:
+            final[done] = got.pop(0)
         if rows is not None:
             name = order[number + 2]
             part[name] = got.pop(0)
             near[name] = near_hop(part[name])
-
-    slot_call(0, rows_x, 1, w_gate, mm)
-
-    def dispatch_d_body(*refs):
-        d_refs, slot_ref, out_refs = refs[:groups], refs[groups], refs[groups + 1 :]
-        for step in range(groups):
-            group = group_at(-step)
-            slot = slot_ref[pl.ds(group * 8, 8), :][0:1]
-            send_rows(picker(slot), d_refs[step][...], group, out_refs)
-
-    d_send = call(
-        dispatch_d_body,
-        [message] * owners,
-        [*d_got, slots],
-        flops=2 * groups * slot_total * toks * width,
-    )
-    rows_d = [d_send[0]] + [swap(d_send[bits], bits) for bits in range(1, owners)]
-
-    slot_call(1, rows_x, 1, w_up, mm)
-    slot_call(2, rows_d, 0, w_down, mm_nt)
-    slot_call(3, rows_d, 1, w_down, mm_nt)
+        return got
+
+    (packed_d,) = slot_call(0, packed_x, 1, w_gate, mm, unpacked=rows_d)
+    slot_call(1, packed_x, 1, w_up, mm)
+    slot_call(2, packed_d, 0, w_down, mm_nt)
+    slot_call(3, packed_d, 1, w_down, mm_nt)
     slot_call(4)
     slot_call(5)
-
-    def summed(total_ref, back_ref):
-        place = lax.axis_index("dp")
-        at_end = (place == 0) | (place == groups - 1)
-        return jnp.where(at_end, back_ref[...], total_ref[...]).astype(F32)
-
-    def both(name):
-        return [total[name], back[name]]
 
     def spread(refs, half, i, value):
         for bits in range(owners):
@@ -394,11 +399,10 @@
                 refs[bits][half, i] = rows
 
     def out_body(*refs):
-        w_ref, outs = refs[8], refs[9:]
+        w_ref, outs = refs[4], refs[5:]
         hidden_refs, out_refs = outs[:2], outs[2:]
         for half in range(2):
-            t = refs[4 * half : 4 * half + 4]
-            gate, up = summed(t[0], t[1]), summed(t[2], t[3])
+            gate, up = (refs[2 * half + n][...].astype(F32) for n in range(2))
             hidden_refs[half][...] = (gate * jax.nn.sigmoid(gate) * up).astype(BF16)
             for i in range(local):
                 rows = hidden_refs[half][i * block : (i + 1) * block, :]
@@ -407,7 +411,7 @@
     got = call(
         out_body,
         [piece, piece] + [message] * owners,
-        [*both("g0"), *both("u0"), *both("g1"), *both("u1"), w_down],
+        [final["g0"], final["u0"], final["g1"], final["u1"], w_down],
         flops=2 * piece_flops,
     )
     hidden, out_send = got[:2], got[2:]
@@ -417,34 +421,30 @@
 
     half_message = arr((local, pair_rows, width))
 
-    def combine(slot_ref, block_of, out_refs, sum_ref):
-        for group in range(groups):
-            place = group // 2 * cap
-            rows = [
-                block_of(bits, group % 2, i, slice(place, place + cap))
-                for bits in range(owners)
-                for i in range(local)
-            ]
-            pick = picker(slot_ref[group * 8 : group * 8 + 1, :])
-            sum_ref[group] = mm_tn(pick, jnp.concatenate(rows, axis=0)).astype(BF16)
-        for step in range(groups):
-            out_refs[step][...] = sum_ref[group_at(-step)]
-
-    def in_call(half, with_out):
-        names = [f"g{half}", f"u{half}", f"b{half}"]
-        ins = [a for n in names for a in both(n)] + [w_gate, w_up]
-        outs = [piece, piece] + [half_message] * owners
-        scratch = []
-        if with_out:
-            ins += [*out_got, slots]
-            outs += [arr((toks, width))] * groups
-            scratch = [pltpu.VMEM((groups, toks, width), BF16)]
+    def combined(slot_ref, group, block_of):
+        place = group // 2 * cap
+        rows = [
+            block_of(bits, i, slice(place, place + cap))
+            for bits in range(owners)
+            for i in range(local)
+        ]
+        pick = picker(slot_ref[group * 8 : group * 8 + 1, :])
+        return mm_tn(pick, jnp.concatenate(rows, axis=0)).astype(BF16)
+
+    def in_call(half):
+        ins = [final[f"g{half}"], final[f"u{half}"]]
+        ins += [final["b0"]] if half == 0 else [total["b1"], back["b1"]]
+        ins += [w_gate, w_up]
         count = len(ins)
 
         def body(*refs):
-            gate, up, grad = (summed(refs[2 * n], refs[2 * n + 1]) for n in range(3))
-            gate_w, up_w = refs[6], refs[7]
-            act_refs, in_refs = refs[count : count + 2], refs[count + 2 : count + 2 + owners]
+            gate, up = refs[0][...].astype(F32), refs[1][...].astype(F32)
+            grad = refs[2][...]
+            if half == 1:
+                grad = jnp.where(at_end(), refs[3][...], grad)
+            grad = grad.astype(F32)
+            gate_w, up_w = refs[count - 2], refs[count - 1]
+            act_refs, in_refs = refs[count : count + 2], refs[count + 2 :]
             sigma = jax.nn.sigmoid(gate)
             act_refs[0][...] = (grad * up * sigma * (1.0 + gate * (1.0 - sigma))).astype(BF16)
             act_refs[1][...] = (grad * (gate * sigma)).astype(BF16)
@@ -454,39 +454,60 @@
                     act_refs[1][rows, :], up_w[i]
                 )
                 spread(in_refs, None, i, into.astype(BF16))
-            if with_out:
-                got_refs, slot_ref = refs[8 : 8 + owners], refs[8 + owners]
-                combine(
-                    slot_ref,
-                    lambda bits, parity, i, rows: got_refs[bits][parity, i, rows, :],
-                    refs[count + 2 + owners : count + 2 + owners + groups],
-                    refs[-1],
+
+        got = call(
+            body, [piece, piece] + [half_message] * owners, ins, flops=2 * piece_flops
+        )
+        sent = got[2:]
+        return got[:2], [sent[0]] + [swap(sent[bits], bits) for bits in range(1, owners)]
+
+    acts0, in_got0 = in_call(0)
+    acts1, in_got1 = in_call(1)
+
+    def tokens_body(*refs):
+        o_refs, i_refs, slot_ref = refs[:owners], refs[owners : 2 * owners], refs[2 * owners]
+        outs = refs[2 * owners + 2 :]
+        sum_ref = refs[-1]
+        for group in range(groups):
+            sum_ref[group] = combined(
+                slot_ref, group, lambda bits, i, rows: o_refs[bits][group % 2, i, rows, :]
+            )
+        for group in range(0, groups, 2):
+            outs[groups][group // 2] = combined(
+                slot_ref, group, lambda bits, i, rows: i_refs[bits][i, rows, :]
+            )
+        for step in range(groups):
+            outs[step][...] = sum_ref[group_at(-step)]
+
+    got = call(
+        tokens_body,
+        [arr((toks, width))] * groups + [arr((groups // 2, toks, width))],
+        [*out_got, *in_got0, slots, acts1[0]],
+        scratch=[pltpu.VMEM((groups, toks, width), BF16)],
+        flops=2 * dispatch_flops,
+    )
+    out_tok, in_even = got[:groups], got[groups]
+    out_chunk = [out_tok[0]] + [shift(out_tok[step], -step) for step in range(1, groups)]
+
+    def in_tokens_body(*refs):
+        i_refs, even_ref, slot_ref = refs[:owners], refs[owners], refs[owners + 1]
+        sum_ref = refs[-1]
+        for group in range(groups):
+            if group % 2 == 0:
+                sum_ref[group] = even_ref[group // 2]
+            else:
+                sum_ref[group] = combined(
+                    slot_ref, group, lambda bits, i, rows: i_refs[bits][i, rows, :]
                 )
-
-        return call(body, outs, ins, scratch=scratch, flops=2 * piece_flops)
-
-    got0 = in_call(0, False)
-    in_got0 = [got0[2]] + [swap(got0[2 + bits], bits) for bits in range(1, owners)]
-    got1 = in_call(1, True)
-    in_got1 = [got1[2]] + [swap(got1[2 + bits], bits) for bits in range(1, owners)]
-    out_tok = got1[2 + owners :]
-    out_chunk = [out_tok[0]] + [shift(out_tok[step], -step) for step in range(1, groups)]
-
-    def in_tokens_body(*refs):
-        halves = (refs[:owners], refs[owners : 2 * owners])
-        combine(
-            refs[2 * owners],
-            lambda bits, parity, i, rows: halves[parity][bits][i, rows, :],
-            refs[2 * owners + 1 : 2 * owners + 1 + groups],
-            refs[-1],
-        )
+        for step in range(groups):
+            refs[owners + 2 + step][...] = sum_ref[group_at(-step)]
 
     in_tok = call(
         in_tokens_body,
         [arr((toks, width))] * groups,
-        [*in_got0, *in_got1, slots],
+        [*in_got1, in_even, slots],
         scratch=[pltpu.VMEM((groups, toks, width), BF16)],
-        flops=2 * groups * slot_total * toks * width,
+        flops=dispatch_flops,
     )
     in_chunk = [in_tok[0]] + [shift(in_tok[step], -step) for step in range(1, groups)]
 
@@ -516,30 +537,23 @@
     output = (mix_wide[:, 0:1] * assemble(out_chunk)).astype(BF16)
     grad_tokens = assemble(in_chunk).astype(BF16)
 
-    def weight_grad(left_body, ins, shape):
+    def weight_grad(rows, acts, shape, rows_first):
         def body(*refs):
             for i in range(local):
-                left, right = left_body(refs, i)
-                refs[-1][i] = mm_tn(left, right)
-
-        return call(body, [arr(shape, F32)], ins, flops=2 * piece_flops)[0]
-
-    def all_rows(refs, i):
-        return jnp.concatenate([r[half, i] for half in range(2) for r in refs], axis=0)
-
-    def all_units(refs, i):
-        return jnp.concatenate([r[i * block : (i + 1) * block, :] for r in refs], axis=0)
-
-    def by_rows(refs, i):
-        return all_rows(refs[:owners], i), all_units(refs[owners : owners + 2], i)
-
-    def by_units(refs, i):
-        right, left = by_rows(refs, i)
-        return left, right
-
-    grad_gate = weight_grad(by_rows, [*rows_x, got0[0], got1[0]], w_gate.shape)
-    grad_up = weight_grad(by_rows, [*rows_x, got0[1], got1[1]], w_up.shape)
-    grad_down = weight_grad(by_units, [*rows_d, *hidden], w_down.shape)
+                part_sum = None
+                for half in range(2):
+                    left, right = refs[0][half, i], refs[1 + half][i * block : (i + 1) * block, :]
+                    if not rows_first:
+                        left, right = right, left
+                    term = mm_tn(left, right)
+                    part_sum = term if part_sum is None else part_sum + term
+                refs[-1][i] = part_sum
+
+        return call(body, [arr(shape, F32)], [rows, *acts], flops=2 * piece_flops)[0]
+
+    grad_gate = weight_grad(packed_x, [acts0[0], acts1[0]], w_gate.shape, True)
+    grad_up = weight_grad(packed_x, [acts0[1], acts1[1]], w_up.shape, True)
+    grad_down = weight_grad(packed_d, hidden, w_down.shape, False)
     return (output, grad_tokens, grad_gate, grad_up, grad_down)
 
 

time: 232 us -> 195 us (0.84)
  waiting for transfers between devices: 131 us -> 97.2 us
  starting transfers between devices: 80.1 us -> 77.7 us
    ppermute x6, waiting for transfers between devices: 15.4 us -> 0.02 us  [near_hop(): return lax.ppermute(value, 'dp', [(0, 1), (3, 2)])]
    ppermute x6, waiting for transfers between devices: 48.7 us -> 38.3 us  [back_hop(): return lax.ppermute(value, 'dp', [(1, 0), (2, 3)])]
    ppermute x6, starting transfers between devices: 35.3 us -> 29.9 us  [near_hop(): return lax.ppermute(value, 'dp', [(0, 1), (3, 2)])]
    ppermute x15, waiting for transfers between devices: 28.2 us -> 24.1 us  [swap(): return lax.ppermute(value, 'expert', [(j, j ^ bits) for j in range(owners)])]
    ppermute x12, waiting for transfers between devices: 34.6 us -> 31.4 us  [shift(): lax.ppermute(value, 'dp', [(j, (j + step) % groups) for j in range(groups)])]
  transfers between devices with their start and end apart: 47 -> 47, of which waited for: 23 -> 22; matrix products, arithmetic and copies ran while one was open for 1% -> 1% of each run, Pallas kernels for 6% -> 6%
where the time goes in v4:
time: 195 us
  waiting for transfers between devices  97.2 us (50%)
  starting transfers between devices  77.7 us (40%)
  Pallas kernels  13.5 us (7%)
  local copies, waits for them, and re-layouts  3.75 us (2%)
    ppermute x6, waiting for transfers between devices, back_hop(): return lax.ppermute(value, 'dp', [(1, 0), (2, 3)])  38.3 us
    ppermute x12, waiting for transfers between devices, shift(): lax.ppermute(value, 'dp', [(j, (j + step) % groups) for j in range(groups)])  31.4 us
    ppermute x6, starting transfers between devices, near_hop(): return lax.ppermute(value, 'dp', [(0, 1), (3, 2)])  29.9 us
    ppermute x15, waiting for transfers between devices, swap(): return lax.ppermute(value, 'expert', [(j, j ^ bits) for j in range(owners)])  24.1 us
    ppermute x12, starting transfers between devices, shift(): lax.ppermute(value, 'dp', [(j, (j + step) % groups) for j in range(groups)])  22.8 us
    pallas_call x20, Pallas kernels, call(): pl.pallas_call(body, out_shape=outs, grid=() if specs is None else (1,),...  13.5 us
    ppermute x15, starting transfers between devices, swap(): return lax.ppermute(value, 'expert', [(j, j ^ bits) for j in range(owners)])  9.93 us
    ppermute x6, starting transfers between devices, back_hop(): return lax.ppermute(value, 'dp', [(1, 0), (2, 3)])  7.75 us
  transfers between devices with their start and end apart: 47, of which 22 were waited for; matrix products, arithmetic and copies ran while one was open for 1% of the time, Pallas kernels for 6%

profile of v4, /device:TPU:0, one launch (start us, length us, event | category | flops | bytes accessed | tf_op | source)
XLA Modules:
  0.0 194.8 jit_solution(14460218307490653086)
XLA Ops:
  2.5 3.1 %collective-permute-start = (bf16[144,512]{1,0:T(8,128)(2,1)S(1)}, bf16[144,512]{1,0:T(8,128)(2,1)S(1)}, u32[]{:S(2)}, u32[]{:S(2)}) collective-permute-start(bf16[144,512]{1,0:T(8,128)(2,1)S(1)} %get-tuple-element.80), channel_id=1, source_target_pairs={{0,8},{8,16},{16,24},{24,0},{1,9},{9,17},{17,25},{25,1},{2,10},{10... | collective-permute-start | bytes 442376 | tf_op jit(solution)/shard_map/ppermute | solution.py:190
  5.6 2.6 %collective-permute-start.1 = (bf16[144,512]{1,0:T(8,128)(2,1)S(1)}, bf16[144,512]{1,0:T(8,128)(2,1)S(1)}, u32[]{:S(2)}, u32[]{:S(2)}) collective-permute-start(bf16[144,512]{1,0:T(8,128)(2,1)S(1)} %get-tuple-element.81), channel_id=1, source_target_pairs={{0,16},{8,24},{16,0},{24,8},{1,17},{9,25},{17,1},{25,9},{2,18},{10... | collective-permute-start | bytes 442376 | tf_op jit(solution)/shard_map/ppermute | solution.py:190
  12.4 5.5 %collective-permute-done.1.refs_2_ = bf16[144,512]{1,0:T(8,128)(2,1)S(1)} collective-permute-done((bf16[144,512]{1,0:T(8,128)(2,1)S(1)}, bf16[144,512]{1,0:T(8,128)(2,1)S(1)}, u32[]{:S(2)}, u32[]{:S(2)}) %collective-permute-start.1) | collective-permute-done | bytes 147488 | tf_op jit(solution)/shard_map/ppermute | solution.py:190
  19.5 3.7 %collective-permute-start.6 = (bf16[128,512]{1,0:T(8,128)(2,1)S(1)}, bf16[128,512]{1,0:T(8,128)(2,1)S(1)}, u32[]{:S(2)}, u32[]{:S(2)}) collective-permute-start(bf16[128,512]{1,0:T(8,128)(2,1)S(1)} %get-tuple-element.89), channel_id=1, source_target_pairs={{0,8},{8,16},{16,24},{24,0},{1,9},{9,17},{17,25},{25,1},{2,10},{10... | collective-permute-start | bytes 393224 | tf_op jit(solution)/shard_map/ppermute | solution.py:190
  29.2 4.9 %collective-permute-done.7.refs_8_ = bf16[128,512]{1,0:T(8,128)(2,1)S(1)} collective-permute-done((bf16[128,512]{1,0:T(8,128)(2,1)S(1)}, bf16[128,512]{1,0:T(8,128)(2,1)S(1)}, u32[]{:S(2)}, u32[]{:S(2)}) %collective-permute-start.7) | collective-permute-done | bytes 131104 | tf_op jit(solution)/shard_map/ppermute | solution.py:190
  43.7 6.0 %collective-permute-done.11.refs_6_ = bf16[2,2,64,512]{3,2,1,0:T(8,128)(2,1)S(1)} collective-permute-done((bf16[2,2,64,512]{3,2,1,0:T(8,128)(2,1)S(1)}, bf16[2,2,64,512]{3,2,1,0:T(8,128)(2,1)S(1)}, u32[]{:S(2)}, u32[]{:S(2)}) %collective-permute-start.11) | collective-permute-done | bytes 262176 | tf_op jit(solution)/shard_map/ppermute | solution.py:193
  49.7 4.7 %collective-permute-done.12.refs_7_ = bf16[2,2,64,512]{3,2,1,0:T(8,128)(2,1)S(1)} collective-permute-done((bf16[2,2,64,512]{3,2,1,0:T(8,128)(2,1)S(1)}, bf16[2,2,64,512]{3,2,1,0:T(8,128)(2,1)S(1)}, u32[]{:S(2)}, u32[]{:S(2)}) %collective-permute-start.12) | collective-permute-done | bytes 262176 | tf_op jit(solution)/shard_map/ppermute | solution.py:193
  55.6 4.3 %collective-permute-start.13 = (bf16[512,384]{1,0:T(8,128)(2,1)S(1)}, bf16[512,384]{1,0:T(8,128)(2,1)S(1)}, u32[]{:S(2)}, u32[]{:S(2)}) collective-permute-start(bf16[512,384]{1,0:T(8,128)(2,1)S(1)} %get-tuple-element.99.refs_0_), channel_id=1, source_target_pairs={{0,8},{24,16},{1,9},{25,17},{2,10},{26,18},{3,11},{27,19},{4,12},{... | collective-permute-start | bytes 1179656 | tf_op jit(solution)/shard_map/ppermute | solution.py:196
  62.6 12.8 %collective-permute-start.18 = (bf16[512,384]{1,0:T(8,128)(2,1)S(1)}, bf16[512,384]{1,0:T(8,128)(2,1)S(1)}, u32[]{:S(2)}, u32[]{:S(2)}) collective-permute-start(bf16[512,384]{1,0:T(8,128)(2,1)S(1)} %get-tuple-element.106.refs_0_), channel_id=1, source_target_pairs={{0,8},{24,16},{1,9},{25,17},{2,10},{26,18},{3,11},{27,19},{4,12},{... | collective-permute-start | bytes 1179656 | tf_op jit(solution)/shard_map/ppermute | solution.py:196
  75.5 6.9 %collective-permute-done.17.refs_5_ = bf16[512,384]{1,0:T(8,128)(2,1)S(1)} collective-permute-done((bf16[512,384]{1,0:T(8,128)(2,1)S(1)}, bf16[512,384]{1,0:T(8,128)(2,1)S(1)}, u32[]{:S(2)}, u32[]{:S(2)}) %collective-permute-start.17) | collective-permute-done | bytes 393248 | tf_op jit(solution)/shard_map/ppermute | solution.py:202
  85.1 4.6 %collective-permute-start.21 = (bf16[512,384]{1,0:T(8,128)(2,1)S(1)}, bf16[512,384]{1,0:T(8,128)(2,1)S(1)}, u32[]{:S(2)}, u32[]{:S(2)}) collective-permute-start(bf16[512,384]{1,0:T(8,128)(2,1)S(1)} %get-tuple-element.110.refs_0_), channel_id=1, source_target_pairs={{0,8},{24,16},{1,9},{25,17},{2,10},{26,18},{3,11},{27,19},{4,12},{... | collective-permute-start | bytes 1179656 | tf_op jit(solution)/shard_map/ppermute | solution.py:196
  89.7 6.0 %collective-permute-done.20.refs_5_ = bf16[512,384]{1,0:T(8,128)(2,1)S(1)} collective-permute-done((bf16[512,384]{1,0:T(8,128)(2,1)S(1)}, bf16[512,384]{1,0:T(8,128)(2,1)S(1)}, u32[]{:S(2)}, u32[]{:S(2)}) %collective-permute-start.20) | collective-permute-done | bytes 393248 | tf_op jit(solution)/shard_map/ppermute | solution.py:202
  98.4 4.6 %collective-permute-start.24 = (bf16[512,384]{1,0:T(8,128)(2,1)S(1)}, bf16[512,384]{1,0:T(8,128)(2,1)S(1)}, u32[]{:S(2)}, u32[]{:S(2)}) collective-permute-start(bf16[512,384]{1,0:T(8,128)(2,1)S(1)} %get-tuple-element.114.refs_0_), channel_id=1, source_target_pairs={{0,8},{24,16},{1,9},{25,17},{2,10},{26,18},{3,11},{27,19},{4,12},{... | collective-permute-start | bytes 1179656 | tf_op jit(solution)/shard_map/ppermute | solution.py:196
  103.1 5.1 %collective-permute-done.23.refs_5_ = bf16[512,384]{1,0:T(8,128)(2,1)S(1)} collective-permute-done((bf16[512,384]{1,0:T(8,128)(2,1)S(1)}, bf16[512,384]{1,0:T(8,128)(2,1)S(1)}, u32[]{:S(2)}, u32[]{:S(2)}) %collective-permute-start.23) | collective-permute-done | bytes 393248 | tf_op jit(solution)/shard_map/ppermute | solution.py:202
  110.4 8.8 %collective-permute-done.26.refs_5_ = bf16[512,384]{1,0:T(8,128)(2,1)S(1)} collective-permute-done((bf16[512,384]{1,0:T(8,128)(2,1)S(1)}, bf16[512,384]{1,0:T(8,128)(2,1)S(1)}, u32[]{:S(2)}, u32[]{:S(2)}) %collective-permute-start.26) | collective-permute-done | bytes 393248 | tf_op jit(solution)/shard_map/ppermute | solution.py:202
  121.4 8.6 %collective-permute-done.31.refs_3_ = bf16[512,384]{1,0:T(8,128)(2,1)S(1)} collective-permute-done((bf16[512,384]{1,0:T(8,128)(2,1)S(1)}, bf16[512,384]{1,0:T(8,128)(2,1)S(1)}, u32[]{:S(2)}, u32[]{:S(2)}) %collective-permute-start.31) | collective-permute-done | bytes 393248 | tf_op jit(solution)/shard_map/ppermute | solution.py:202
  136.8 3.0 %collective-permute-done.35.refs_3_ = bf16[512,384]{1,0:T(8,128)(2,1)S(1)} collective-permute-done((bf16[512,384]{1,0:T(8,128)(2,1)S(1)}, bf16[512,384]{1,0:T(8,128)(2,1)S(1)}, u32[]{:S(2)}, u32[]{:S(2)}) %collective-permute-start.35) | collective-permute-done | bytes 393248 | tf_op jit(solution)/shard_map/ppermute | solution.py:202
  141.4 4.7 %collective-permute-done.29.refs_3_ = bf16[2,2,64,512]{3,2,1,0:T(8,128)(2,1)S(1)} collective-permute-done((bf16[2,2,64,512]{3,2,1,0:T(8,128)(2,1)S(1)}, bf16[2,2,64,512]{3,2,1,0:T(8,128)(2,1)S(1)}, u32[]{:S(2)}, u32[]{:S(2)}) %collective-permute-start.29) | collective-permute-done | bytes 262176 | tf_op jit(solution)/shard_map/ppermute | solution.py:193
  146.1 3.7 %collective-permute-done.33.refs_6_ = bf16[2,64,512]{2,1,0:T(8,128)(2,1)S(1)} collective-permute-done((bf16[2,64,512]{2,1,0:T(8,128)(2,1)S(1)}, bf16[2,64,512]{2,1,0:T(8,128)(2,1)S(1)}, u32[]{:S(2)}, u32[]{:S(2)}) %collective-permute-start.33) | collective-permute-done | bytes 131104 | tf_op jit(solution)/shard_map/ppermute | solution.py:193
  153.4 2.9 %collective-permute-start.37 = (bf16[128,512]{1,0:T(8,128)(2,1)S(1)}, bf16[128,512]{1,0:T(8,128)(2,1)S(1)}, u32[]{:S(2)}, u32[]{:S(2)}) collective-permute-start(bf16[128,512]{1,0:T(8,128)(2,1)S(1)} %get-tuple-element.133), channel_id=1, source_target_pairs={{0,16},{8,24},{16,0},{24,8},{1,17},{9,25},{17,1},{25,9},{2,18},{10... | collective-permute-start | bytes 393224 | tf_op jit(solution)/shard_map/ppermute | solution.py:190
  159.6 8.7 %collective-permute-done.37.refs_2_ = bf16[128,512]{1,0:T(8,128)(2,1)S(1)} collective-permute-done((bf16[128,512]{1,0:T(8,128)(2,1)S(1)}, bf16[128,512]{1,0:T(8,128)(2,1)S(1)}, u32[]{:S(2)}, u32[]{:S(2)}) %collective-permute-start.37) | collective-permute-done | bytes 131104 | tf_op jit(solution)/shard_map/ppermute | solution.py:190
  170.4 3.9 %collective-permute-start.44 = (bf16[128,512]{1,0:T(8,128)(2,1)S(1)}, bf16[128,512]{1,0:T(8,128)(2,1)S(1)}, u32[]{:S(2)}, u32[]{:S(2)}) collective-permute-start(bf16[128,512]{1,0:T(8,128)(2,1)S(1)} %get-tuple-element.144), channel_id=1, source_target_pairs={{0,16},{8,24},{16,0},{24,8},{1,17},{9,25},{17,1},{25,9},{2,18},{10... | collective-permute-start | bytes 393224 | tf_op jit(solution)/shard_map/ppermute | solution.py:190
  178.1 8.2 %collective-permute-done.44.refs_2_ = bf16[128,512]{1,0:T(8,128)(2,1)S(1)} collective-permute-done((bf16[128,512]{1,0:T(8,128)(2,1)S(1)}, bf16[128,512]{1,0:T(8,128)(2,1)S(1)}, u32[]{:S(2)}, u32[]{:S(2)}) %collective-permute-start.44) | collective-permute-done | bytes 131104 | tf_op jit(solution)/shard_map/ppermute | solution.py:190
  190.7 3.3 %collective-permute-done.46 = bf16[128,1024]{1,0:T(8,128)(2,1)S(1)} collective-permute-done((bf16[128,1024]{1,0:T(8,128)(2,1)S(1)}, bf16[128,1024]{1,0:T(8,128)(2,1)S(1)}, u32[]{:S(2)}, u32[]{:S(2)}) %collective-permute-start.46) | collective-permute-done | bytes 262176 | tf_op jit(solution)/shard_map/ppermute | solution.py:534
  (106 shorter events, 63.1 us)
Async XLA Ops:
  5.6 12.3 %collective-permute-start.1 = (bf16[144,512]{1,0:T(8,128)(2,1)S(1)}, bf16[144,512]{1,0:T(8,128)(2,1)S(1)}, u32[]{:S(2)}, u32[]{:S(2)}) collective-permute-start(bf16[144,512]{1,0:T(8,128)(2,1)S(1)} %get-tuple-element.81), channel_id=1, source_target_pairs={{0,16},{8,24},{16,0},{24,8},{1,17},{9,25},{17,1},{25,9},{2,18},{10... | collective-permute-start | bytes 442376 | tf_op jit(solution)/shard_map/ppermute | solution.py:190
  23.2 11.7 %collective-permute-start.3 = (bf16[2,2,64,512]{3,2,1,0:T(8,128)(2,1)S(1)}, bf16[2,2,64,512]{3,2,1,0:T(8,128)(2,1)S(1)}, u32[]{:S(2)}, u32[]{:S(2)}) collective-permute-start(bf16[2,2,64,512]{3,2,1,0:T(8,128)(2,1)S(1)} %get-tuple-element.85), channel_id=1, source_target_pairs={{0,2},{2,0},{4,6},{6,4},{1,3},{3,1},{5,7},{7,5},{8,10},{10,8},{12,... | collective-permute-start | bytes 786440 | tf_op jit(solution)/shard_map/ppermute | solution.py:193
  23.2 11.7 %collective-permute-start.4 = (bf16[2,2,64,512]{3,2,1,0:T(8,128)(2,1)S(1)}, bf16[2,2,64,512]{3,2,1,0:T(8,128)(2,1)S(1)}, u32[]{:S(2)}, u32[]{:S(2)}) collective-permute-start(bf16[2,2,64,512]{3,2,1,0:T(8,128)(2,1)S(1)} %get-tuple-element.86), channel_id=1, source_target_pairs={{0,4},{2,6},{4,0},{6,2},{1,5},{3,7},{5,1},{7,3},{8,12},{10,14},{12... | collective-permute-start | bytes 786440 | tf_op jit(solution)/shard_map/ppermute | solution.py:193
  24.7 12.5 %collective-permute-start.5 = (bf16[2,2,64,512]{3,2,1,0:T(8,128)(2,1)S(1)}, bf16[2,2,64,512]{3,2,1,0:T(8,128)(2,1)S(1)}, u32[]{:S(2)}, u32[]{:S(2)}) collective-permute-start(bf16[2,2,64,512]{3,2,1,0:T(8,128)(2,1)S(1)} %get-tuple-element.87), channel_id=1, source_target_pairs={{0,6},{2,4},{4,2},{6,0},{1,7},{3,5},{5,3},{7,1},{8,14},{10,12},{12... | collective-permute-start | bytes 786440 | tf_op jit(solution)/shard_map/ppermute | solution.py:193
  38.1 16.2 %collective-permute-start.9 = (bf16[512,384]{1,0:T(8,128)(2,1)S(1)}, bf16[512,384]{1,0:T(8,128)(2,1)S(1)}, u32[]{:S(2)}, u32[]{:S(2)}) collective-permute-start(bf16[512,384]{1,0:T(8,128)(2,1)S(1)} %get-tuple-element.93.refs_0_), channel_id=1, source_target_pairs={{0,8},{24,16},{1,9},{25,17},{2,10},{26,18},{3,11},{27,19},{4,12},{... | collective-permute-start | bytes 1179656 | tf_op jit(solution)/shard_map/ppermute | solution.py:196
  42.1 12.3 %collective-permute-start.12 = (bf16[2,2,64,512]{3,2,1,0:T(8,128)(2,1)S(1)}, bf16[2,2,64,512]{3,2,1,0:T(8,128)(2,1)S(1)}, u32[]{:S(2)}, u32[]{:S(2)}) collective-permute-start(bf16[2,2,64,512]{3,2,1,0:T(8,128)(2,1)S(1)} %get-tuple-element.98), channel_id=1, source_target_pairs={{0,6},{2,4},{4,2},{6,0},{1,7},{3,5},{5,3},{7,1},{8,14},{10,12},{12... | collective-permute-start | bytes 786440 | tf_op jit(solution)/shard_map/ppermute | solution.py:193
  42.4 17.6 %collective-permute-start.14 = (bf16[512,384]{1,0:T(8,128)(2,1)S(1)}, bf16[512,384]{1,0:T(8,128)(2,1)S(1)}, u32[]{:S(2)}, u32[]{:S(2)}) collective-permute-start(bf16[512,384]{1,0:T(8,128)(2,1)S(1)} %get-tuple-element.100.refs_0_), channel_id=1, source_target_pairs={{0,8},{24,16},{1,9},{25,17},{2,10},{26,18},{3,11},{27,19},{4,12},{... | collective-permute-start | bytes 1179656 | tf_op jit(solution)/shard_map/ppermute | solution.py:196
  55.6 19.8 %collective-permute-start.13 = (bf16[512,384]{1,0:T(8,128)(2,1)S(1)}, bf16[512,384]{1,0:T(8,128)(2,1)S(1)}, u32[]{:S(2)}, u32[]{:S(2)}) collective-permute-start(bf16[512,384]{1,0:T(8,128)(2,1)S(1)} %get-tuple-element.99.refs_0_), channel_id=1, source_target_pairs={{0,8},{24,16},{1,9},{25,17},{2,10},{26,18},{3,11},{27,19},{4,12},{... | collective-permute-start | bytes 1179656 | tf_op jit(solution)/shard_map/ppermute | solution.py:196
  60.7 14.8 %collective-permute-start.16 = (bf16[512,384]{1,0:T(8,128)(2,1)S(1)}, bf16[512,384]{1,0:T(8,128)(2,1)S(1)}, u32[]{:S(2)}, u32[]{:S(2)}) collective-permute-start(bf16[512,384]{1,0:T(8,128)(2,1)S(1)} %get-tuple-element.102.refs_2_), channel_id=1, source_target_pairs={{8,16},{16,8},{9,17},{17,9},{10,18},{18,10},{11,19},{19,11},{12,20... | collective-permute-start | bytes 1179656 | tf_op jit(solution)/shard_map/ppermute | solution.py:199
  61.3 21.0 %collective-permute-start.17 = (bf16[512,384]{1,0:T(8,128)(2,1)S(1)}, bf16[512,384]{1,0:T(8,128)(2,1)S(1)}, u32[]{:S(2)}, u32[]{:S(2)}) collective-permute-start(bf16[512,384]{1,0:T(8,128)(2,1)S(1)} %get-tuple-element.103.refs_4_), channel_id=1, source_target_pairs={{8,0},{16,24},{9,1},{17,25},{10,2},{18,26},{11,3},{19,27},{12,4},{... | collective-permute-start | bytes 1179656 | tf_op jit(solution)/shard_map/ppermute | solution.py:202
  62.6 27.0 %collective-permute-start.18 = (bf16[512,384]{1,0:T(8,128)(2,1)S(1)}, bf16[512,384]{1,0:T(8,128)(2,1)S(1)}, u32[]{:S(2)}, u32[]{:S(2)}) collective-permute-start(bf16[512,384]{1,0:T(8,128)(2,1)S(1)} %get-tuple-element.106.refs_0_), channel_id=1, source_target_pairs={{0,8},{24,16},{1,9},{25,17},{2,10},{26,18},{3,11},{27,19},{4,12},{... | collective-permute-start | bytes 1179656 | tf_op jit(solution)/shard_map/ppermute | solution.py:196
  83.8 11.9 %collective-permute-start.20 = (bf16[512,384]{1,0:T(8,128)(2,1)S(1)}, bf16[512,384]{1,0:T(8,128)(2,1)S(1)}, u32[]{:S(2)}, u32[]{:S(2)}) collective-permute-start(bf16[512,384]{1,0:T(8,128)(2,1)S(1)} %get-tuple-element.108.refs_4_), channel_id=1, source_target_pairs={{8,0},{16,24},{9,1},{17,25},{10,2},{18,26},{11,3},{19,27},{12,4},{... | collective-permute-start | bytes 1179656 | tf_op jit(solution)/shard_map/ppermute | solution.py:202
  85.1 18.0 %collective-permute-start.21 = (bf16[512,384]{1,0:T(8,128)(2,1)S(1)}, bf16[512,384]{1,0:T(8,128)(2,1)S(1)}, u32[]{:S(2)}, u32[]{:S(2)}) collective-permute-start(bf16[512,384]{1,0:T(8,128)(2,1)S(1)} %get-tuple-element.110.refs_0_), channel_id=1, source_target_pairs={{0,8},{24,16},{1,9},{25,17},{2,10},{26,18},{3,11},{27,19},{4,12},{... | collective-permute-start | bytes 1179656 | tf_op jit(solution)/shard_map/ppermute | solution.py:196
  98.4 11.9 %collective-permute-start.24 = (bf16[512,384]{1,0:T(8,128)(2,1)S(1)}, bf16[512,384]{1,0:T(8,128)(2,1)S(1)}, u32[]{:S(2)}, u32[]{:S(2)}) collective-permute-start(bf16[512,384]{1,0:T(8,128)(2,1)S(1)} %get-tuple-element.114.refs_0_), channel_id=1, source_target_pairs={{0,8},{24,16},{1,9},{25,17},{2,10},{26,18},{3,11},{27,19},{4,12},{... | collective-permute-start | bytes 1179656 | tf_op jit(solution)/shard_map/ppermute | solution.py:196
  133.8 12.4 %collective-permute-start.29 = (bf16[2,2,64,512]{3,2,1,0:T(8,128)(2,1)S(1)}, bf16[2,2,64,512]{3,2,1,0:T(8,128)(2,1)S(1)}, u32[]{:S(2)}, u32[]{:S(2)}) collective-permute-start(bf16[2,2,64,512]{3,2,1,0:T(8,128)(2,1)S(1)} %get-tuple-element.121), channel_id=1, source_target_pairs={{0,6},{2,4},{4,2},{6,0},{1,7},{3,5},{5,3},{7,1},{8,14},{10,12},{12... | collective-permute-start | bytes 786440 | tf_op jit(solution)/shard_map/ppermute | solution.py:193
  135.3 14.5 %collective-permute-start.33 = (bf16[2,64,512]{2,1,0:T(8,128)(2,1)S(1)}, bf16[2,64,512]{2,1,0:T(8,128)(2,1)S(1)}, u32[]{:S(2)}, u32[]{:S(2)}) collective-permute-start(bf16[2,64,512]{2,1,0:T(8,128)(2,1)S(1)} %get-tuple-element.127), channel_id=1, source_target_pairs={{0,4},{2,6},{4,0},{6,2},{1,5},{3,7},{5,1},{7,3},{8,12},{10,14},{12... | collective-permute-start | bytes 393224 | tf_op jit(solution)/shard_map/ppermute | solution.py:193
  139.8 11.9 %collective-permute-start.34 = (bf16[2,64,512]{2,1,0:T(8,128)(2,1)S(1)}, bf16[2,64,512]{2,1,0:T(8,128)(2,1)S(1)}, u32[]{:S(2)}, u32[]{:S(2)}) collective-permute-start(bf16[2,64,512]{2,1,0:T(8,128)(2,1)S(1)} %get-tuple-element.128), channel_id=1, source_target_pairs={{0,6},{2,4},{4,2},{6,0},{1,7},{3,5},{5,3},{7,1},{8,14},{10,12},{12... | collective-permute-start | bytes 393224 | tf_op jit(solution)/shard_map/ppermute | solution.py:193
  153.4 15.0 %collective-permute-start.37 = (bf16[128,512]{1,0:T(8,128)(2,1)S(1)}, bf16[128,512]{1,0:T(8,128)(2,1)S(1)}, u32[]{:S(2)}, u32[]{:S(2)}) collective-permute-start(bf16[128,512]{1,0:T(8,128)(2,1)S(1)} %get-tuple-element.133), channel_id=1, source_target_pairs={{0,16},{8,24},{16,0},{24,8},{1,17},{9,25},{17,1},{25,9},{2,18},{10... | collective-permute-start | bytes 393224 | tf_op jit(solution)/shard_map/ppermute | solution.py:190
  156.3 12.1 %collective-permute-start.38 = (bf16[128,512]{1,0:T(8,128)(2,1)S(1)}, bf16[128,512]{1,0:T(8,128)(2,1)S(1)}, u32[]{:S(2)}, u32[]{:S(2)}) collective-permute-start(bf16[128,512]{1,0:T(8,128)(2,1)S(1)} %get-tuple-element.134), channel_id=1, source_target_pairs={{0,8},{8,16},{16,24},{24,0},{1,9},{9,17},{17,25},{25,1},{2,10},{10... | collective-permute-start | bytes 393224 | tf_op jit(solution)/shard_map/ppermute | solution.py:190
  156.6 13.5 %collective-permute-start.40 = (bf16[2,64,512]{2,1,0:T(8,128)(2,1)S(1)}, bf16[2,64,512]{2,1,0:T(8,128)(2,1)S(1)}, u32[]{:S(2)}, u32[]{:S(2)}) collective-permute-start(bf16[2,64,512]{2,1,0:T(8,128)(2,1)S(1)} %get-tuple-element.138), channel_id=1, source_target_pairs={{0,2},{2,0},{4,6},{6,4},{1,3},{3,1},{5,7},{7,5},{8,10},{10,8},{12,... | collective-permute-start | bytes 393224 | tf_op jit(solution)/shard_map/ppermute | solution.py:193
  156.6 13.5 %collective-permute-start.41 = (bf16[2,64,512]{2,1,0:T(8,128)(2,1)S(1)}, bf16[2,64,512]{2,1,0:T(8,128)(2,1)S(1)}, u32[]{:S(2)}, u32[]{:S(2)}) collective-permute-start(bf16[2,64,512]{2,1,0:T(8,128)(2,1)S(1)} %get-tuple-element.139), channel_id=1, source_target_pairs={{0,4},{2,6},{4,0},{6,2},{1,5},{3,7},{5,1},{7,3},{8,12},{10,14},{12... | collective-permute-start | bytes 393224 | tf_op jit(solution)/shard_map/ppermute | solution.py:193
  168.5 21.4 %collective-permute-start.39 = (bf16[128,1024]{1,0:T(8,128)(2,1)S(1)}, bf16[128,1024]{1,0:T(8,128)(2,1)S(1)}, u32[]{:S(2)}, u32[]{:S(2)}) collective-permute-start(bf16[128,1024]{1,0:T(8,128)(2,1)S(1)} %get-tuple-element.136), channel_id=1, source_target_pairs={{0,1},{1,0},{2,3},{3,2},{4,5},{5,4},{6,7},{7,6},{8,9},{9,8},{10,11... | collective-permute-start | bytes 786440 | tf_op jit(solution)/shard_map/ppermute | solution.py:534
  170.4 15.9 %collective-permute-start.44 = (bf16[128,512]{1,0:T(8,128)(2,1)S(1)}, bf16[128,512]{1,0:T(8,128)(2,1)S(1)}, u32[]{:S(2)}, u32[]{:S(2)}) collective-permute-start(bf16[128,512]{1,0:T(8,128)(2,1)S(1)} %get-tuple-element.144), channel_id=1, source_target_pairs={{0,16},{8,24},{16,0},{24,8},{1,17},{9,25},{17,1},{25,9},{2,18},{10... | collective-permute-start | bytes 393224 | tf_op jit(solution)/shard_map/ppermute | solution.py:190
  174.4 12.0 %collective-permute-start.45 = (bf16[128,512]{1,0:T(8,128)(2,1)S(1)}, bf16[128,512]{1,0:T(8,128)(2,1)S(1)}, u32[]{:S(2)}, u32[]{:S(2)}) collective-permute-start(bf16[128,512]{1,0:T(8,128)(2,1)S(1)} %get-tuple-element.145), channel_id=1, source_target_pairs={{0,8},{8,16},{16,24},{24,0},{1,9},{9,17},{17,25},{25,1},{2,10},{10... | collective-permute-start | bytes 393224 | tf_op jit(solution)/shard_map/ppermute | solution.py:190
  (29 other events, 278.8 us)

commit v5 on v4

--- a/solution.py
+++ b/solution.py
@@ -192,14 +192,10 @@
     def swap(value, bits):
         return lax.ppermute(value, "expert", [(j, j ^ bits) for j in range(owners)])
 
-    def near_hop(value):
-        return lax.ppermute(value, "dp", [(0, 1), (3, 2)])
-
-    def far_hop(value):
-        return lax.ppermute(value, "dp", [(1, 2), (2, 1)])
-
-    def back_hop(value):
-        return lax.ppermute(value, "dp", [(1, 0), (2, 3)])
+    inward, outward = [(0, 1), (3, 2)], [(1, 0), (2, 3)]
+
+    def line_hop(value, pairs):
+        return lax.ppermute(value, "dp", pairs)
 
     def group_at(step):
         return lax.rem(lax.axis_index("dp") + step + groups, groups)
@@ -247,44 +243,47 @@
 
     message = arr((2, local, pair_rows, width))
 
+    def weigh_body(x_ref, cot_ref, score_ref, *outs):
+        d_refs, (line_ref, mix_ref, weighted_ref) = outs[:groups], outs[groups:]
+        line_ref[...] = x_ref[...]
+        score = score_ref[...]
+        mix = score[:, 0:1] / jnp.sum(score, axis=1, keepdims=True)
+        mix_ref[...] = jnp.broadcast_to(mix, mix_ref.shape)
+        weighted_ref[...] = (mix * cot_ref[...].astype(F32)).astype(BF16)
+        for step in range(groups):
+            d_refs[step][...] = weighted_ref[:, columns_at(step)]
+
+    got = call(
+        weigh_body,
+        [arr((toks, width))] * groups + [arr((toks + extra, width)), arr((toks, 128), F32)],
+        [x_got[1], cotangent, scores],
+        scratch=[pltpu.VMEM((toks, model_width), BF16)],
+    )
+    d_pack, (x_first, mix_wide) = got[:groups], got[groups:]
+    d_got = [d_pack[0]] + [shift(d_pack[step], step) for step in range(1, groups)]
+
     def dispatch_x_body(*refs):
-        x_refs, cot_ref, score_ref = refs[:groups], refs[groups], refs[groups + 1]
-        outs = refs[groups + 2 :]
-        send_refs, d_refs = outs[:owners], outs[owners : owners + groups]
-        slot_ref, mix_ref, weighted_ref = outs[owners + groups :]
+        x_refs, send_refs, slot_ref = refs[:groups], refs[groups:-1], refs[-1]
         for step in range(groups):
             group = group_at(-step)
             slot = slots_row(x_refs[step][toks : toks + extra, 0:toks][0:1].astype(F32))
             slot_ref[pl.ds(group * 8, 8), :] = jnp.broadcast_to(slot, (8, toks))
             send_rows(picker(slot), x_refs[step][0:toks, :], group, send_refs)
-        score = score_ref[...]
-        mix = score[:, 0:1] / jnp.sum(score, axis=1, keepdims=True)
-        mix_ref[...] = jnp.broadcast_to(mix, mix_ref.shape)
-        weighted_ref[...] = (mix * cot_ref[...].astype(F32)).astype(BF16)
-        for step in range(groups):
-            d_refs[step][...] = weighted_ref[:, columns_at(step)]
 
     got = call(
         dispatch_x_body,
-        [message] * owners
-        + [arr((toks, width))] * groups
-        + [arr((groups * 8, toks), jnp.int32), arr((toks, 128), F32)],
-        [*x_got, cotangent, scores],
-        scratch=[pltpu.VMEM((toks, model_width), BF16)],
+        [message] * owners + [arr((groups * 8, toks), jnp.int32)],
+        [x_got[0], x_first, *x_got[2:]],
         flops=2 * groups * slot_total * toks * width,
     )
-    x_send, d_pack = got[:owners], got[owners : owners + groups]
-    slots, mix_wide = got[owners + groups :]
+    x_send, slots = got[:owners], got[owners]
     rows_x = [x_send[0]] + [swap(x_send[bits], bits) for bits in range(1, owners)]
-    d_got = [d_pack[0]] + [shift(d_pack[step], step) for step in range(1, groups)]
 
     full = pl.BlockSpec(memory_space=pltpu.VMEM)
-    piece = arr((half_rows, units))
-    piece_flops = 2 * half_rows * units * width
+    piece = arr((block, units))
+    piece_flops = 2 * block * units * width
     dispatch_flops = 2 * groups * slot_total * toks * width
     packed = arr((2, local, block, width))
-    half_packed = pl.BlockSpec((1, local, block, width), lambda *_: (0, 0, 0, 0))
-    other_packed = pl.BlockSpec((1, local, block, width), lambda *_: (1, 0, 0, 0))
 
     def pack_rows(out_ref, refs):
         for half in range(2):
@@ -293,102 +292,117 @@
                     at = slice(bits * pair_rows, (bits + 1) * pair_rows)
                     out_ref[half, i, at, :] = refs[bits][half, i]
 
-    def part_into(out_ref, rows_ref, w_ref, product, half=0):
-        for i in range(local):
-            out_ref[i * block : (i + 1) * block, :] = product(rows_ref[half, i], w_ref[i]).astype(
-                BF16
-            )
+    halves, experts = range(2), range(local)
+    order = [(kind, half, i) for half in halves for i in experts for kind in "gu"]
+    order += [("b", half, i) for half in halves for i in experts]
+    weight_of = {"g": w_gate, "u": w_up, "b": w_down}
+    part, pair, total, final, near, far = {}, {}, {}, {}, {}, {}
 
     def first_body(*refs):
-        x_refs, gate_ref, up_ref = refs[:owners], refs[owners], refs[owners + 1]
+        x_refs, w_refs = refs[:owners], refs[owners : owners + 2]
         d_refs, slot_ref = refs[owners + 2 : owners + 2 + groups], refs[owners + 2 + groups]
         outs = refs[owners + 3 + groups :]
         pack_rows(outs[2], x_refs)
-        part_into(outs[0], outs[2], gate_ref, mm)
-        part_into(outs[1], outs[2], up_ref, mm)
+        for out, w_ref in zip(outs[:2], w_refs):
+            out[...] = mm(outs[2][0, 0], w_ref[0]).astype(BF16)
         for step in range(groups):
             group = group_at(-step)
             slot = slot_ref[pl.ds(group * 8, 8), :][0:1]
             send_rows(picker(slot), d_refs[step][...], group, outs[3:])
 
-    part = {}
     got = call(
         first_body,
         [piece, piece, packed] + [message] * owners,
         [*rows_x, w_gate, w_up, *d_got, slots],
         flops=2 * piece_flops + dispatch_flops,
     )
-    part["g0"], part["u0"], packed_x = got[:3]
+    part[0], part[1], packed_x = got[:3]
     d_send = got[3:]
-
-    order = ["g0", "u0", "g1", "u1", "b0", "b1"]
-    near, far, back, pair, total, final = {}, {}, {}, {}, {}, {}
-    near["g0"], near["u0"] = near_hop(part["g0"]), near_hop(part["u0"])
+    near[0], near[1] = line_hop(part[0], inward), line_hop(part[1], inward)
     rows_d = [d_send[0]] + [swap(d_send[bits], bits) for bits in range(1, owners)]
 
     def at_end():
         place = lax.axis_index("dp")
         return (place == 0) | (place == groups - 1)
 
-    def slot_call(number, rows=None, half=0, weight=None, product=None, unpacked=None):
-        take = order[number] if number < len(order) else None
-        last = order[number - 1] if 0 < number <= len(order) else None
-        done = order[number - 2] if 1 < number else None
-        ins, outs = [], []
-        for name, left, right in ((take, part, near), (last, pair, far), (done, total, back)):
-            if name:
-                ins += [left[name], right[name]]
-                outs.append(piece)
+    def plus(left_ref, right_ref):
+        return (left_ref[...].astype(F32) + right_ref[...].astype(F32)).astype(BF16)
+
+    count = len(order)
+
+    def slot_call(t, rows=None, unpacked=None):
+        take, cross, done = t < count, 0 <= t - 2 < count, 0 <= t - 4 < count
+        ahead = t + 2 < count
+        ins, specs, outs = [near[t]], [full], []
+        if take:
+            ins.append(part[t])
+            outs.append(piece)
+        if cross:
+            ins += [pair[t - 2], far[t - 2]]
+            outs.append(piece)
+        if done:
+            ins.append(total[t - 4])
+            outs.append(piece)
         specs = [full] * len(ins)
-        if rows is not None:
-            ins += [rows, weight]
-            specs += [other_packed if half else half_packed, full]
+        if ahead:
+            kind, half, i = order[t + 2]
+            ins += [rows, weight_of[kind]]
+            specs += [
+                pl.BlockSpec((1, 1, block, width), lambda *_: (half, i, 0, 0)),
+                pl.BlockSpec((1, *weight_of[kind].shape[1:]), lambda *_: (i, 0, 0)),
+            ]
+            outs.append(piece)
+        if ahead and cross:
             outs.append(piece)
         if unpacked is not None:
             ins += unpacked
             specs += [full] * owners
             outs.append(packed)
-        count = len(ins)
+        ins_count = len(ins)
 
         def body(*refs):
-            at, to = 0, count
-            for name in (take, last):
-                if name:
-                    both = refs[at][...].astype(F32) + refs[at + 1][...].astype(F32)
-                    refs[to][...] = both.astype(BF16)
-                    at, to = at + 2, to + 1
+            left, right = list(refs[:ins_count]), list(refs[ins_count:])
+            got_ref = left.pop(0)
+            total_ref = None
+            if take:
+                right.pop(0)[...] = plus(left.pop(0), got_ref)
+            if cross:
+                total_ref = right.pop(0)
+                total_ref[...] = plus(left.pop(0), left.pop(0))
             if done:
-                refs[to][...] = jnp.where(at_end(), refs[at + 1][...], refs[at][...])
-                at, to = at + 2, to + 1
-            if rows is not None:
-                part_into(refs[to], refs[at], refs[at + 1], product)
-                at, to = at + 2, to + 1
+                right.pop(0)[...] = jnp.where(at_end(), got_ref[...], left.pop(0)[...])
+            if ahead:
+                rows_ref, w_ref, part_ref = left.pop(0), left.pop(0), right.pop(0)
+                product = mm_nt if kind == "b" else mm
+                part_ref[...] = product(rows_ref[0, 0], w_ref[0]).astype(BF16)
+                if cross:
+                    right.pop(0)[...] = jnp.where(at_end(), part_ref[...], total_ref[...])
             if unpacked is not None:
-                pack_rows(refs[to], refs[at : at + owners])
-
-        got = list(
-            call(body, outs, ins, specs=specs, flops=piece_flops if rows is not None else 0)
-        )
+                pack_rows(right.pop(0), left)
+
+        got = list(call(body, outs, ins, specs=specs, flops=piece_flops if ahead else 0))
         if take:
-            pair[take] = got.pop(0)
-            far[take] = far_hop(pair[take])
-        if last:
-            total[last] = got.pop(0)
-            back[last] = back_hop(total[last])
+            pair[t] = got.pop(0)
+            far[t] = line_hop(pair[t], [(1, 2), (2, 1)])
+        if cross:
+            total[t - 2] = got.pop(0)
         if done:
-            final[done] = got.pop(0)
-        if rows is not None:
-            name = order[number + 2]
-            part[name] = got.pop(0)
-            near[name] = near_hop(part[name])
+            final[order[t - 4]] = got.pop(0)
+        if ahead:
+            part[t + 2] = got.pop(0)
+        if ahead and cross:
+            near[t + 2] = line_hop(got.pop(0), inward + outward)
+        elif ahead:
+            near[t + 2] = line_hop(part[t + 2], inward)
+        elif cross:
+            near[t + 2] = line_hop(total[t - 2], outward)
         return got
 
-    (packed_d,) = slot_call(0, packed_x, 1, w_gate, mm, unpacked=rows_d)
-    slot_call(1, packed_x, 1, w_up, mm)
-    slot_call(2, packed_d, 0, w_down, mm_nt)
-    slot_call(3, packed_d, 1, w_down, mm_nt)
-    slot_call(4)
-    slot_call(5)
+    for t in range(3):
+        slot_call(t, packed_x)
+    (packed_d,) = slot_call(3, packed_x, unpacked=rows_d)
+    for t in range(4, count):
+        slot_call(t, packed_x if t + 2 < 2 * 2 * local else packed_d)
 
     def spread(refs, half, i, value):
         for bits in range(owners):
@@ -398,26 +412,30 @@
             else:
                 refs[bits][half, i] = rows
 
+    acts = arr((half_rows, units))
+
     def out_body(*refs):
-        w_ref, outs = refs[4], refs[5:]
+        w_ref, outs = refs[4 * local], refs[4 * local + 1 :]
         hidden_refs, out_refs = outs[:2], outs[2:]
-        for half in range(2):
-            gate, up = (refs[2 * half + n][...].astype(F32) for n in range(2))
-            hidden_refs[half][...] = (gate * jax.nn.sigmoid(gate) * up).astype(BF16)
-            for i in range(local):
-                rows = hidden_refs[half][i * block : (i + 1) * block, :]
+        for half in halves:
+            for i in experts:
+                at = 2 * (half * local + i)
+                gate, up = refs[at][...].astype(F32), refs[at + 1][...].astype(F32)
+                rows = (gate * jax.nn.sigmoid(gate) * up).astype(BF16)
+                hidden_refs[half][i * block : (i + 1) * block, :] = rows
                 spread(out_refs, half, i, mm(rows, w_ref[i]).astype(BF16))
 
     got = call(
         out_body,
-        [piece, piece] + [message] * owners,
-        [final["g0"], final["u0"], final["g1"], final["u1"], w_down],
-        flops=2 * piece_flops,
+        [acts, acts] + [message] * owners,
+        [final[name] for name in order[: 4 * local]] + [w_down],
+        flops=2 * local * piece_flops,
     )
     hidden, out_send = got[:2], got[2:]
     out_got = [out_send[0]] + [swap(out_send[bits], bits) for bits in range(1, owners)]
 
-    slot_call(6)
+    for t in range(count, count + 4):
+        slot_call(t)
 
     half_message = arr((local, pair_rows, width))
 
@@ -432,31 +450,25 @@
         return mm_tn(pick, jnp.concatenate(rows, axis=0)).astype(BF16)
 
     def in_call(half):
-        ins = [final[f"g{half}"], final[f"u{half}"]]
-        ins += [final["b0"]] if half == 0 else [total["b1"], back["b1"]]
-        ins += [w_gate, w_up]
+        ins = [final[kind, half, i] for i in experts for kind in "gub"] + [w_gate, w_up]
         count = len(ins)
 
         def body(*refs):
-            gate, up = refs[0][...].astype(F32), refs[1][...].astype(F32)
-            grad = refs[2][...]
-            if half == 1:
-                grad = jnp.where(at_end(), refs[3][...], grad)
-            grad = grad.astype(F32)
             gate_w, up_w = refs[count - 2], refs[count - 1]
             act_refs, in_refs = refs[count : count + 2], refs[count + 2 :]
-            sigma = jax.nn.sigmoid(gate)
-            act_refs[0][...] = (grad * up * sigma * (1.0 + gate * (1.0 - sigma))).astype(BF16)
-            act_refs[1][...] = (grad * (gate * sigma)).astype(BF16)
-            for i in range(local):
+            for i in experts:
+                gate, up, grad = (refs[3 * i + n][...].astype(F32) for n in range(3))
                 rows = slice(i * block, (i + 1) * block)
-                into = mm_nt(act_refs[0][rows, :], gate_w[i]) + mm_nt(
-                    act_refs[1][rows, :], up_w[i]
-                )
+                sigma = jax.nn.sigmoid(gate)
+                act_gate = (grad * up * sigma * (1.0 + gate * (1.0 - sigma))).astype(BF16)
+                act_up = (grad * (gate * sigma)).astype(BF16)
+                act_refs[0][rows, :] = act_gate
+                act_refs[1][rows, :] = act_up
+                into = mm_nt(act_gate, gate_w[i]) + mm_nt(act_up, up_w[i])
                 spread(in_refs, None, i, into.astype(BF16))
 
         got = call(
-            body, [piece, piece] + [half_message] * owners, ins, flops=2 * piece_flops
+            body, [acts, acts] + [half_message] * owners, ins, flops=4 * piece_flops
         )
         sent = got[2:]
         return got[:2], [sent[0]] + [swap(sent[bits], bits) for bits in range(1, owners)]
@@ -549,7 +561,7 @@
                     part_sum = term if part_sum is None else part_sum + term
                 refs[-1][i] = part_sum
 
-        return call(body, [arr(shape, F32)], [rows, *acts], flops=2 * piece_flops)[0]
+        return call(body, [arr(shape, F32)], [rows, *acts], flops=4 * piece_flops)[0]
 
     grad_gate = weight_grad(packed_x, [acts0[0], acts1[0]], w_gate.shape, True)
     grad_up = weight_grad(packed_x, [acts0[1], acts1[1]], w_up.shape, True)

time: 195 us -> 169 us (0.87)
  waiting for transfers between devices: 97.2 us -> 54.9 us
  starting transfers between devices: 77.7 us -> 92.3 us
    ppermute x18 -> x28, waiting for transfers between devices: 38.3 us -> 17.9 us  [line_hop(): return lax.ppermute(value, 'dp', pairs)]
    ppermute x15, waiting for transfers between devices: 24.1 us -> 12 us  [swap(): return lax.ppermute(value, 'expert', [(j, j ^ bits) for j in range(owners)])]
    ppermute x12, waiting for transfers between devices: 31.4 us -> 21 us  [shift(): lax.ppermute(value, 'dp', [(j, (j + step) % groups) for j in range(groups)])]
    ppermute x18 -> x28, starting transfers between devices: 41.8 us -> 51.6 us  [line_hop(): return lax.ppermute(value, 'dp', pairs)]
    ppermute x12, starting transfers between devices: 22.8 us -> 28.5 us  [shift(): lax.ppermute(value, 'dp', [(j, (j + step) % groups) for j in range(groups)])]
    pallas_call x20 -> x30, Pallas kernels: 13.5 us -> 14.6 us  [call(): pl.pallas_call(body, out_shape=outs, grid=() if specs is None else (1,),...]
  transfers between devices with their start and end apart: 47 -> 57, of which waited for: 22 -> 22; matrix products, arithmetic and copies ran while one was open for 1% -> 1% of each run, Pallas kernels for 6% -> 8%
where the time goes in v5:
time: 169 us; the launch traced here: 168 us
  starting transfers between devices  92.3 us (55%)
  waiting for transfers between devices  54.9 us (32%)
  Pallas kernels  14.6 us (9%)
  local copies, waits for them, and re-layouts  3.75 us (2%)
    ppermute x28, starting transfers between devices, line_hop(): return lax.ppermute(value, 'dp', pairs)  51.6 us
    ppermute x12, starting transfers between devices, shift(): lax.ppermute(value, 'dp', [(j, (j + step) % groups) for j in range(groups)])  28.5 us
    ppermute x12, waiting for transfers between devices, shift(): lax.ppermute(value, 'dp', [(j, (j + step) % groups) for j in range(groups)])  21 us
    ppermute x28, waiting for transfers between devices, line_hop(): return lax.ppermute(value, 'dp', pairs)  17.9 us
    pallas_call x30, Pallas kernels, call(): pl.pallas_call(body, out_shape=outs, grid=() if specs is None else (1,),...  14.6 us
    ppermute x15, waiting for transfers between devices, swap(): return lax.ppermute(value, 'expert', [(j, j ^ bits) for j in range(owners)])  12 us
    ppermute x15, starting transfers between devices, swap(): return lax.ppermute(value, 'expert', [(j, j ^ bits) for j in range(owners)])  10 us
    ppermute x2, waiting for transfers between devices, assemble(): other = lax.ppermute(give, 'tensor', [(0, 1), (1, 0)])  3.98 us
  transfers between devices with their start and end apart: 57, of which 22 were waited for; matrix products, arithmetic and copies ran while one was open for 1% of the time, Pallas kernels for 8%

profile of v5, /device:TPU:0, one launch (start us, length us, event | category | flops | bytes accessed | tf_op | source)
XLA Modules:
  0.0 168.3 jit_solution(16209882054779428613)
XLA Ops:
  2.5 3.1 %collective-permute-start = (bf16[144,512]{1,0:T(8,128)(2,1)S(1)}, bf16[144,512]{1,0:T(8,128)(2,1)S(1)}, u32[]{:S(2)}, u32[]{:S(2)}) collective-permute-start(bf16[144,512]{1,0:T(8,128)(2,1)S(1)} %get-tuple-element.111), channel_id=1, source_target_pairs={{0,8},{8,16},{16,24},{24,0},{1,9},{9,17},{17,25},{25,1},{2,10},{10... | collective-permute-start | bytes 442376 | tf_op jit(solution)/shard_map/ppermute | solution.py:190
  5.6 2.6 %collective-permute-start.1 = (bf16[144,512]{1,0:T(8,128)(2,1)S(1)}, bf16[144,512]{1,0:T(8,128)(2,1)S(1)}, u32[]{:S(2)}, u32[]{:S(2)}) collective-permute-start(bf16[144,512]{1,0:T(8,128)(2,1)S(1)} %get-tuple-element.115), channel_id=1, source_target_pairs={{0,16},{8,24},{16,0},{24,8},{1,17},{9,25},{17,1},{25,9},{2,18},{10... | collective-permute-start | bytes 442376 | tf_op jit(solution)/shard_map/ppermute | solution.py:190
  13.7 5.3 %collective-permute-start.6 = (bf16[128,512]{1,0:T(8,128)(2,1)S(1)}, bf16[128,512]{1,0:T(8,128)(2,1)S(1)}, u32[]{:S(2)}, u32[]{:S(2)}) collective-permute-start(bf16[128,512]{1,0:T(8,128)(2,1)S(1)} %get-tuple-element.122), channel_id=1, source_target_pairs={{0,8},{8,16},{16,24},{24,0},{1,9},{9,17},{17,25},{25,1},{2,10},{10... | collective-permute-start | bytes 393224 | tf_op jit(solution)/shard_map/ppermute | solution.py:190
  21.5 4.3 %collective-permute-start.7 = (bf16[128,512]{1,0:T(8,128)(2,1)S(1)}, bf16[128,512]{1,0:T(8,128)(2,1)S(1)}, u32[]{:S(2)}, u32[]{:S(2)}) collective-permute-start(bf16[128,512]{1,0:T(8,128)(2,1)S(1)} %get-tuple-element.123), channel_id=1, source_target_pairs={{0,16},{8,24},{16,0},{24,8},{1,17},{9,25},{17,1},{25,9},{2,18},{10... | collective-permute-start | bytes 393224 | tf_op jit(solution)/shard_map/ppermute | solution.py:190
  25.8 3.4 %collective-permute-start.8 = (bf16[128,512]{1,0:T(8,128)(2,1)S(1)}, bf16[128,512]{1,0:T(8,128)(2,1)S(1)}, u32[]{:S(2)}, u32[]{:S(2)}) collective-permute-start(bf16[128,512]{1,0:T(8,128)(2,1)S(1)} %get-tuple-element.124), channel_id=1, source_target_pairs={{0,24},{8,0},{16,8},{24,16},{1,25},{9,1},{17,9},{25,17},{2,26},{10... | collective-permute-start | bytes 393224 | tf_op jit(solution)/shard_map/ppermute | solution.py:190
  34.2 7.2 %collective-permute-start.9 = (bf16[256,384]{1,0:T(8,128)(2,1)S(1)}, bf16[256,384]{1,0:T(8,128)(2,1)S(1)}, u32[]{:S(2)}, u32[]{:S(2)}) collective-permute-start(bf16[256,384]{1,0:T(8,128)(2,1)S(1)} %get-tuple-element.126.refs_1_), channel_id=1, source_target_pairs={{0,8},{24,16},{1,9},{25,17},{2,10},{26,18},{3,11},{27,19},{4,12},{... | collective-permute-start | bytes 589832 | tf_op jit(solution)/shard_map/ppermute | solution.py:198
  42.7 3.9 %collective-permute-done.9.refs_0_ = bf16[256,384]{1,0:T(8,128)(2,1)S(1)} collective-permute-done((bf16[256,384]{1,0:T(8,128)(2,1)S(1)}, bf16[256,384]{1,0:T(8,128)(2,1)S(1)}, u32[]{:S(2)}, u32[]{:S(2)}) %collective-permute-start.9) | collective-permute-done | bytes 196640 | tf_op jit(solution)/shard_map/ppermute | solution.py:198
  47.0 4.4 %collective-permute-start.10 = (bf16[256,384]{1,0:T(8,128)(2,1)S(1)}, bf16[256,384]{1,0:T(8,128)(2,1)S(1)}, u32[]{:S(2)}, u32[]{:S(2)}) collective-permute-start(bf16[256,384]{1,0:T(8,128)(2,1)S(1)} %get-tuple-element.128.refs_1_), channel_id=1, source_target_pairs={{0,8},{24,16},{1,9},{25,17},{2,10},{26,18},{3,11},{27,19},{4,12},{... | collective-permute-start | bytes 589832 | tf_op jit(solution)/shard_map/ppermute | solution.py:198
  54.6 4.4 %collective-permute-start.15 = (bf16[256,384]{1,0:T(8,128)(2,1)S(1)}, bf16[256,384]{1,0:T(8,128)(2,1)S(1)}, u32[]{:S(2)}, u32[]{:S(2)}) collective-permute-start(bf16[256,384]{1,0:T(8,128)(2,1)S(1)} %get-tuple-element.136.refs_1_), channel_id=1, source_target_pairs={{0,8},{24,16},{1,9},{25,17},{2,10},{26,18},{3,11},{27,19},{4,12},{... | collective-permute-start | bytes 589832 | tf_op jit(solution)/shard_map/ppermute | solution.py:198
  62.0 4.0 %collective-permute-done.19.refs_9_ = bf16[2,2,64,512]{3,2,1,0:T(8,128)(2,1)S(1)} collective-permute-done((bf16[2,2,64,512]{3,2,1,0:T(8,128)(2,1)S(1)}, bf16[2,2,64,512]{3,2,1,0:T(8,128)(2,1)S(1)}, u32[]{:S(2)}, u32[]{:S(2)}) %collective-permute-start.19) | collective-permute-done | bytes 262176 | tf_op jit(solution)/shard_map/ppermute | solution.py:193
  68.2 3.3 %collective-permute-start.22 = (bf16[256,384]{1,0:T(8,128)(2,1)S(1)}, bf16[256,384]{1,0:T(8,128)(2,1)S(1)}, u32[]{:S(2)}, u32[]{:S(2)}) collective-permute-start(bf16[256,384]{1,0:T(8,128)(2,1)S(1)} %get-tuple-element.147), channel_id=1, source_target_pairs={{0,8},{24,16},{8,0},{16,24},{1,9},{25,17},{9,1},{17,25},{2,10},{26... | collective-permute-start | bytes 589832 | tf_op jit(solution)/shard_map/ppermute | solution.py:198
  74.6 3.7 %collective-permute-start.24 = (bf16[256,384]{1,0:T(8,128)(2,1)S(1)}, bf16[256,384]{1,0:T(8,128)(2,1)S(1)}, u32[]{:S(2)}, u32[]{:S(2)}) collective-permute-start(bf16[256,384]{1,0:T(8,128)(2,1)S(1)} %get-tuple-element.153), channel_id=1, source_target_pairs={{0,8},{24,16},{8,0},{16,24},{1,9},{25,17},{9,1},{17,25},{2,10},{26... | collective-permute-start | bytes 589832 | tf_op jit(solution)/shard_map/ppermute | solution.py:198
  83.0 3.4 %collective-permute-start.28 = (bf16[256,384]{1,0:T(8,128)(2,1)S(1)}, bf16[256,384]{1,0:T(8,128)(2,1)S(1)}, u32[]{:S(2)}, u32[]{:S(2)}) collective-permute-start(bf16[256,384]{1,0:T(8,128)(2,1)S(1)} %get-tuple-element.163), channel_id=1, source_target_pairs={{0,8},{24,16},{8,0},{16,24},{1,9},{25,17},{9,1},{17,25},{2,10},{26... | collective-permute-start | bytes 589832 | tf_op jit(solution)/shard_map/ppermute | solution.py:198
  87.5 3.6 %collective-permute-start.30 = (bf16[256,384]{1,0:T(8,128)(2,1)S(1)}, bf16[256,384]{1,0:T(8,128)(2,1)S(1)}, u32[]{:S(2)}, u32[]{:S(2)}) collective-permute-start(bf16[256,384]{1,0:T(8,128)(2,1)S(1)} %get-tuple-element.168), channel_id=1, source_target_pairs={{0,8},{24,16},{8,0},{16,24},{1,9},{25,17},{9,1},{17,25},{2,10},{26... | collective-permute-start | bytes 589832 | tf_op jit(solution)/shard_map/ppermute | solution.py:198
  92.2 3.1 %collective-permute-start.32 = (bf16[256,384]{1,0:T(8,128)(2,1)S(1)}, bf16[256,384]{1,0:T(8,128)(2,1)S(1)}, u32[]{:S(2)}, u32[]{:S(2)}) collective-permute-start(bf16[256,384]{1,0:T(8,128)(2,1)S(1)} %get-tuple-element.173), channel_id=1, source_target_pairs={{0,8},{24,16},{8,0},{16,24},{1,9},{25,17},{9,1},{17,25},{2,10},{26... | collective-permute-start | bytes 589832 | tf_op jit(solution)/shard_map/ppermute | solution.py:198
  102.2 3.7 %collective-permute-done.37.refs_0_ = bf16[256,384]{1,0:T(8,128)(2,1)S(1)} collective-permute-done((bf16[256,384]{1,0:T(8,128)(2,1)S(1)}, bf16[256,384]{1,0:T(8,128)(2,1)S(1)}, u32[]{:S(2)}, u32[]{:S(2)}) %collective-permute-start.37) | collective-permute-done | bytes 196640 | tf_op jit(solution)/shard_map/ppermute | solution.py:198
  107.3 2.6 %collective-permute-done.39.refs_0_ = bf16[256,384]{1,0:T(8,128)(2,1)S(1)} collective-permute-done((bf16[256,384]{1,0:T(8,128)(2,1)S(1)}, bf16[256,384]{1,0:T(8,128)(2,1)S(1)}, u32[]{:S(2)}, u32[]{:S(2)}) %collective-permute-start.39) | collective-permute-done | bytes 196640 | tf_op jit(solution)/shard_map/ppermute | solution.py:198
  114.4 2.9 %collective-permute-done.44.refs_0_ = bf16[256,384]{1,0:T(8,128)(2,1)S(1)} collective-permute-done((bf16[256,384]{1,0:T(8,128)(2,1)S(1)}, bf16[256,384]{1,0:T(8,128)(2,1)S(1)}, u32[]{:S(2)}, u32[]{:S(2)}) %collective-permute-start.44) | collective-permute-done | bytes 196640 | tf_op jit(solution)/shard_map/ppermute | solution.py:198
  121.2 3.7 %collective-permute-done.36.refs_3_ = bf16[2,2,64,512]{3,2,1,0:T(8,128)(2,1)S(1)} collective-permute-done((bf16[2,2,64,512]{3,2,1,0:T(8,128)(2,1)S(1)}, bf16[2,2,64,512]{3,2,1,0:T(8,128)(2,1)S(1)}, u32[]{:S(2)}, u32[]{:S(2)}) %collective-permute-start.36) | collective-permute-done | bytes 262176 | tf_op jit(solution)/shard_map/ppermute | solution.py:193
  125.0 2.6 %collective-permute-done.42.refs_6_ = bf16[2,64,512]{2,1,0:T(8,128)(2,1)S(1)} collective-permute-done((bf16[2,64,512]{2,1,0:T(8,128)(2,1)S(1)}, bf16[2,64,512]{2,1,0:T(8,128)(2,1)S(1)}, u32[]{:S(2)}, u32[]{:S(2)}) %collective-permute-start.42) | collective-permute-done | bytes 131104 | tf_op jit(solution)/shard_map/ppermute | solution.py:193
  130.6 3.2 %collective-permute-start.47 = (bf16[128,512]{1,0:T(8,128)(2,1)S(1)}, bf16[128,512]{1,0:T(8,128)(2,1)S(1)}, u32[]{:S(2)}, u32[]{:S(2)}) collective-permute-start(bf16[128,512]{1,0:T(8,128)(2,1)S(1)} %get-tuple-element.197), channel_id=1, source_target_pairs={{0,16},{8,24},{16,0},{24,8},{1,17},{9,25},{17,1},{25,9},{2,18},{10... | collective-permute-start | bytes 393224 | tf_op jit(solution)/shard_map/ppermute | solution.py:190
  137.2 9.3 %collective-permute-done.47.refs_2_ = bf16[128,512]{1,0:T(8,128)(2,1)S(1)} collective-permute-done((bf16[128,512]{1,0:T(8,128)(2,1)S(1)}, bf16[128,512]{1,0:T(8,128)(2,1)S(1)}, u32[]{:S(2)}, u32[]{:S(2)}) %collective-permute-start.47) | collective-permute-done | bytes 131104 | tf_op jit(solution)/shard_map/ppermute | solution.py:190
  155.3 5.0 %collective-permute-done.54.refs_2_ = bf16[128,512]{1,0:T(8,128)(2,1)S(1)} collective-permute-done((bf16[128,512]{1,0:T(8,128)(2,1)S(1)}, bf16[128,512]{1,0:T(8,128)(2,1)S(1)}, u32[]{:S(2)}, u32[]{:S(2)}) %collective-permute-start.54) | collective-permute-done | bytes 131104 | tf_op jit(solution)/shard_map/ppermute | solution.py:190
  163.6 4.0 %collective-permute-done.56 = bf16[128,1024]{1,0:T(8,128)(2,1)S(1)} collective-permute-done((bf16[128,1024]{1,0:T(8,128)(2,1)S(1)}, bf16[128,1024]{1,0:T(8,128)(2,1)S(1)}, u32[]{:S(2)}, u32[]{:S(2)}) %collective-permute-start.56) | collective-permute-done | bytes 262176 | tf_op jit(solution)/shard_map/ppermute | solution.py:546
  (136 shorter events, 70.6 us)
Async XLA Ops:
  5.6 13.4 %collective-permute-start.1 = (bf16[144,512]{1,0:T(8,128)(2,1)S(1)}, bf16[144,512]{1,0:T(8,128)(2,1)S(1)}, u32[]{:S(2)}, u32[]{:S(2)}) collective-permute-start(bf16[144,512]{1,0:T(8,128)(2,1)S(1)} %get-tuple-element.115), channel_id=1, source_target_pairs={{0,16},{8,24},{16,0},{24,8},{1,17},{9,25},{17,1},{25,9},{2,18},{10... | collective-permute-start | bytes 442376 | tf_op jit(solution)/shard_map/ppermute | solution.py:190
  8.2 10.8 %collective-permute-start.2 = (bf16[144,512]{1,0:T(8,128)(2,1)S(1)}, bf16[144,512]{1,0:T(8,128)(2,1)S(1)}, u32[]{:S(2)}, u32[]{:S(2)}) collective-permute-start(bf16[144,512]{1,0:T(8,128)(2,1)S(1)} %get-tuple-element.116), channel_id=1, source_target_pairs={{0,24},{8,0},{16,8},{24,16},{1,25},{9,1},{17,9},{25,17},{2,26},{10... | collective-permute-start | bytes 442376 | tf_op jit(solution)/shard_map/ppermute | solution.py:190
  13.7 12.1 %collective-permute-start.6 = (bf16[128,512]{1,0:T(8,128)(2,1)S(1)}, bf16[128,512]{1,0:T(8,128)(2,1)S(1)}, u32[]{:S(2)}, u32[]{:S(2)}) collective-permute-start(bf16[128,512]{1,0:T(8,128)(2,1)S(1)} %get-tuple-element.122), channel_id=1, source_target_pairs={{0,8},{8,16},{16,24},{24,0},{1,9},{9,17},{17,25},{25,1},{2,10},{10... | collective-permute-start | bytes 393224 | tf_op jit(solution)/shard_map/ppermute | solution.py:190
  19.5 13.0 %collective-permute-start.3 = (bf16[2,2,64,512]{3,2,1,0:T(8,128)(2,1)S(1)}, bf16[2,2,64,512]{3,2,1,0:T(8,128)(2,1)S(1)}, u32[]{:S(2)}, u32[]{:S(2)}) collective-permute-start(bf16[2,2,64,512]{3,2,1,0:T(8,128)(2,1)S(1)} %get-tuple-element.118), channel_id=1, source_target_pairs={{0,2},{2,0},{4,6},{6,4},{1,3},{3,1},{5,7},{7,5},{8,10},{10,8},{12,... | collective-permute-start | bytes 786440 | tf_op jit(solution)/shard_map/ppermute | solution.py:193
  19.6 13.0 %collective-permute-start.4 = (bf16[2,2,64,512]{3,2,1,0:T(8,128)(2,1)S(1)}, bf16[2,2,64,512]{3,2,1,0:T(8,128)(2,1)S(1)}, u32[]{:S(2)}, u32[]{:S(2)}) collective-permute-start(bf16[2,2,64,512]{3,2,1,0:T(8,128)(2,1)S(1)} %get-tuple-element.119), channel_id=1, source_target_pairs={{0,4},{2,6},{4,0},{6,2},{1,5},{3,7},{5,1},{7,3},{8,12},{10,14},{12... | collective-permute-start | bytes 786440 | tf_op jit(solution)/shard_map/ppermute | solution.py:193
  21.2 12.3 %collective-permute-start.5 = (bf16[2,2,64,512]{3,2,1,0:T(8,128)(2,1)S(1)}, bf16[2,2,64,512]{3,2,1,0:T(8,128)(2,1)S(1)}, u32[]{:S(2)}, u32[]{:S(2)}) collective-permute-start(bf16[2,2,64,512]{3,2,1,0:T(8,128)(2,1)S(1)} %get-tuple-element.120), channel_id=1, source_target_pairs={{0,6},{2,4},{4,2},{6,0},{1,7},{3,5},{5,3},{7,1},{8,14},{10,12},{12... | collective-permute-start | bytes 786440 | tf_op jit(solution)/shard_map/ppermute | solution.py:193
  34.2 12.4 %collective-permute-start.9 = (bf16[256,384]{1,0:T(8,128)(2,1)S(1)}, bf16[256,384]{1,0:T(8,128)(2,1)S(1)}, u32[]{:S(2)}, u32[]{:S(2)}) collective-permute-start(bf16[256,384]{1,0:T(8,128)(2,1)S(1)} %get-tuple-element.126.refs_1_), channel_id=1, source_target_pairs={{0,8},{24,16},{1,9},{25,17},{2,10},{26,18},{3,11},{27,19},{4,12},{... | collective-permute-start | bytes 589832 | tf_op jit(solution)/shard_map/ppermute | solution.py:198
  41.4 12.3 %collective-permute-start.14 = (bf16[256,384]{1,0:T(8,128)(2,1)S(1)}, bf16[256,384]{1,0:T(8,128)(2,1)S(1)}, u32[]{:S(2)}, u32[]{:S(2)}) collective-permute-start(bf16[256,384]{1,0:T(8,128)(2,1)S(1)} %get-tuple-element.135.refs_1_), channel_id=1, source_target_pairs={{0,8},{24,16},{1,9},{25,17},{2,10},{26,18},{3,11},{27,19},{4,12},{... | collective-permute-start | bytes 589832 | tf_op jit(solution)/shard_map/ppermute | solution.py:198
  53.7 12.3 %collective-permute-start.19 = (bf16[2,2,64,512]{3,2,1,0:T(8,128)(2,1)S(1)}, bf16[2,2,64,512]{3,2,1,0:T(8,128)(2,1)S(1)}, u32[]{:S(2)}, u32[]{:S(2)}) collective-permute-start(bf16[2,2,64,512]{3,2,1,0:T(8,128)(2,1)S(1)} %get-tuple-element.141), channel_id=1, source_target_pairs={{0,6},{2,4},{4,2},{6,0},{1,7},{3,5},{5,3},{7,1},{8,14},{10,12},{12... | collective-permute-start | bytes 786440 | tf_op jit(solution)/shard_map/ppermute | solution.py:193
  54.6 11.5 %collective-permute-start.15 = (bf16[256,384]{1,0:T(8,128)(2,1)S(1)}, bf16[256,384]{1,0:T(8,128)(2,1)S(1)}, u32[]{:S(2)}, u32[]{:S(2)}) collective-permute-start(bf16[256,384]{1,0:T(8,128)(2,1)S(1)} %get-tuple-element.136.refs_1_), channel_id=1, source_target_pairs={{0,8},{24,16},{1,9},{25,17},{2,10},{26,18},{3,11},{27,19},{4,12},{... | collective-permute-start | bytes 589832 | tf_op jit(solution)/shard_map/ppermute | solution.py:198
  68.2 10.8 %collective-permute-start.22 = (bf16[256,384]{1,0:T(8,128)(2,1)S(1)}, bf16[256,384]{1,0:T(8,128)(2,1)S(1)}, u32[]{:S(2)}, u32[]{:S(2)}) collective-permute-start(bf16[256,384]{1,0:T(8,128)(2,1)S(1)} %get-tuple-element.147), channel_id=1, source_target_pairs={{0,8},{24,16},{8,0},{16,24},{1,9},{25,17},{9,1},{17,25},{2,10},{26... | collective-permute-start | bytes 589832 | tf_op jit(solution)/shard_map/ppermute | solution.py:198
  99.4 10.5 %collective-permute-start.39 = (bf16[256,384]{1,0:T(8,128)(2,1)S(1)}, bf16[256,384]{1,0:T(8,128)(2,1)S(1)}, u32[]{:S(2)}, u32[]{:S(2)}) collective-permute-start(bf16[256,384]{1,0:T(8,128)(2,1)S(1)} %get-tuple-element.185.refs_3_), channel_id=1, source_target_pairs={{8,0},{16,24},{9,1},{17,25},{10,2},{18,26},{11,3},{19,27},{12,4},{... | collective-permute-start | bytes 589832 | tf_op jit(solution)/shard_map/ppermute | solution.py:198
  102.1 11.6 %collective-permute-start.34 = (bf16[2,2,64,512]{3,2,1,0:T(8,128)(2,1)S(1)}, bf16[2,2,64,512]{3,2,1,0:T(8,128)(2,1)S(1)}, u32[]{:S(2)}, u32[]{:S(2)}) collective-permute-start(bf16[2,2,64,512]{3,2,1,0:T(8,128)(2,1)S(1)} %get-tuple-element.179), channel_id=1, source_target_pairs={{0,2},{2,0},{4,6},{6,4},{1,3},{3,1},{5,7},{7,5},{8,10},{10,8},{12,... | collective-permute-start | bytes 786440 | tf_op jit(solution)/shard_map/ppermute | solution.py:193
  106.0 11.3 %collective-permute-start.44 = (bf16[256,384]{1,0:T(8,128)(2,1)S(1)}, bf16[256,384]{1,0:T(8,128)(2,1)S(1)}, u32[]{:S(2)}, u32[]{:S(2)}) collective-permute-start(bf16[256,384]{1,0:T(8,128)(2,1)S(1)} %get-tuple-element.192.refs_1_), channel_id=1, source_target_pairs={{8,0},{16,24},{9,1},{17,25},{10,2},{18,26},{11,3},{19,27},{12,4},{... | collective-permute-start | bytes 589832 | tf_op jit(solution)/shard_map/ppermute | solution.py:198
  112.8 12.1 %collective-permute-start.36 = (bf16[2,2,64,512]{3,2,1,0:T(8,128)(2,1)S(1)}, bf16[2,2,64,512]{3,2,1,0:T(8,128)(2,1)S(1)}, u32[]{:S(2)}, u32[]{:S(2)}) collective-permute-start(bf16[2,2,64,512]{3,2,1,0:T(8,128)(2,1)S(1)} %get-tuple-element.181), channel_id=1, source_target_pairs={{0,6},{2,4},{4,2},{6,0},{1,7},{3,5},{5,3},{7,1},{8,14},{10,12},{12... | collective-permute-start | bytes 786440 | tf_op jit(solution)/shard_map/ppermute | solution.py:193
  113.7 11.3 %collective-permute-start.41 = (bf16[2,64,512]{2,1,0:T(8,128)(2,1)S(1)}, bf16[2,64,512]{2,1,0:T(8,128)(2,1)S(1)}, u32[]{:S(2)}, u32[]{:S(2)}) collective-permute-start(bf16[2,64,512]{2,1,0:T(8,128)(2,1)S(1)} %get-tuple-element.189), channel_id=1, source_target_pairs={{0,2},{2,0},{4,6},{6,4},{1,3},{3,1},{5,7},{7,5},{8,10},{10,8},{12,... | collective-permute-start | bytes 393224 | tf_op jit(solution)/shard_map/ppermute | solution.py:193
  130.6 15.8 %collective-permute-start.47 = (bf16[128,512]{1,0:T(8,128)(2,1)S(1)}, bf16[128,512]{1,0:T(8,128)(2,1)S(1)}, u32[]{:S(2)}, u32[]{:S(2)}) collective-permute-start(bf16[128,512]{1,0:T(8,128)(2,1)S(1)} %get-tuple-element.197), channel_id=1, source_target_pairs={{0,16},{8,24},{16,0},{24,8},{1,17},{9,25},{17,1},{25,9},{2,18},{10... | collective-permute-start | bytes 393224 | tf_op jit(solution)/shard_map/ppermute | solution.py:190
  133.8 12.7 %collective-permute-start.48 = (bf16[128,512]{1,0:T(8,128)(2,1)S(1)}, bf16[128,512]{1,0:T(8,128)(2,1)S(1)}, u32[]{:S(2)}, u32[]{:S(2)}) collective-permute-start(bf16[128,512]{1,0:T(8,128)(2,1)S(1)} %get-tuple-element.198), channel_id=1, source_target_pairs={{0,8},{8,16},{16,24},{24,0},{1,9},{9,17},{17,25},{25,1},{2,10},{10... | collective-permute-start | bytes 393224 | tf_op jit(solution)/shard_map/ppermute | solution.py:190
  134.8 13.3 %collective-permute-start.50 = (bf16[2,64,512]{2,1,0:T(8,128)(2,1)S(1)}, bf16[2,64,512]{2,1,0:T(8,128)(2,1)S(1)}, u32[]{:S(2)}, u32[]{:S(2)}) collective-permute-start(bf16[2,64,512]{2,1,0:T(8,128)(2,1)S(1)} %get-tuple-element.202), channel_id=1, source_target_pairs={{0,2},{2,0},{4,6},{6,4},{1,3},{3,1},{5,7},{7,5},{8,10},{10,8},{12,... | collective-permute-start | bytes 393224 | tf_op jit(solution)/shard_map/ppermute | solution.py:193
  134.8 13.3 %collective-permute-start.51 = (bf16[2,64,512]{2,1,0:T(8,128)(2,1)S(1)}, bf16[2,64,512]{2,1,0:T(8,128)(2,1)S(1)}, u32[]{:S(2)}, u32[]{:S(2)}) collective-permute-start(bf16[2,64,512]{2,1,0:T(8,128)(2,1)S(1)} %get-tuple-element.203), channel_id=1, source_target_pairs={{0,4},{2,6},{4,0},{6,2},{1,5},{3,7},{5,1},{7,3},{8,12},{10,14},{12... | collective-permute-start | bytes 393224 | tf_op jit(solution)/shard_map/ppermute | solution.py:193
  136.5 11.6 %collective-permute-start.52 = (bf16[2,64,512]{2,1,0:T(8,128)(2,1)S(1)}, bf16[2,64,512]{2,1,0:T(8,128)(2,1)S(1)}, u32[]{:S(2)}, u32[]{:S(2)}) collective-permute-start(bf16[2,64,512]{2,1,0:T(8,128)(2,1)S(1)} %get-tuple-element.204), channel_id=1, source_target_pairs={{0,6},{2,4},{4,2},{6,0},{1,7},{3,5},{5,3},{7,1},{8,14},{10,12},{12... | collective-permute-start | bytes 393224 | tf_op jit(solution)/shard_map/ppermute | solution.py:193
  146.5 16.2 %collective-permute-start.49 = (bf16[128,1024]{1,0:T(8,128)(2,1)S(1)}, bf16[128,1024]{1,0:T(8,128)(2,1)S(1)}, u32[]{:S(2)}, u32[]{:S(2)}) collective-permute-start(bf16[128,1024]{1,0:T(8,128)(2,1)S(1)} %get-tuple-element.200), channel_id=1, source_target_pairs={{0,1},{1,0},{2,3},{3,2},{4,5},{5,4},{6,7},{7,6},{8,9},{9,8},{10,11... | collective-permute-start | bytes 786440 | tf_op jit(solution)/shard_map/ppermute | solution.py:546
  148.5 11.7 %collective-permute-start.54 = (bf16[128,512]{1,0:T(8,128)(2,1)S(1)}, bf16[128,512]{1,0:T(8,128)(2,1)S(1)}, u32[]{:S(2)}, u32[]{:S(2)}) collective-permute-start(bf16[128,512]{1,0:T(8,128)(2,1)S(1)} %get-tuple-element.208), channel_id=1, source_target_pairs={{0,16},{8,24},{16,0},{24,8},{1,17},{9,25},{17,1},{25,9},{2,18},{10... | collective-permute-start | bytes 393224 | tf_op jit(solution)/shard_map/ppermute | solution.py:190
  148.6 11.7 %collective-permute-start.55 = (bf16[128,512]{1,0:T(8,128)(2,1)S(1)}, bf16[128,512]{1,0:T(8,128)(2,1)S(1)}, u32[]{:S(2)}, u32[]{:S(2)}) collective-permute-start(bf16[128,512]{1,0:T(8,128)(2,1)S(1)} %get-tuple-element.209), channel_id=1, source_target_pairs={{0,8},{8,16},{16,24},{24,0},{1,9},{9,17},{17,25},{25,1},{2,10},{10... | collective-permute-start | bytes 393224 | tf_op jit(solution)/shard_map/ppermute | solution.py:190
  (39 other events, 332.1 us)

commit v6 on v5

--- a/solution.py
+++ b/solution.py
@@ -243,40 +243,34 @@
 
     message = arr((2, local, pair_rows, width))
 
-    def weigh_body(x_ref, cot_ref, score_ref, *outs):
-        d_refs, (line_ref, mix_ref, weighted_ref) = outs[:groups], outs[groups:]
-        line_ref[...] = x_ref[...]
+    def weigh_body(cot_ref, score_ref, weighted_ref, mix_ref):
         score = score_ref[...]
         mix = score[:, 0:1] / jnp.sum(score, axis=1, keepdims=True)
         mix_ref[...] = jnp.broadcast_to(mix, mix_ref.shape)
         weighted_ref[...] = (mix * cot_ref[...].astype(F32)).astype(BF16)
-        for step in range(groups):
-            d_refs[step][...] = weighted_ref[:, columns_at(step)]
-
-    got = call(
-        weigh_body,
-        [arr((toks, width))] * groups + [arr((toks + extra, width)), arr((toks, 128), F32)],
-        [x_got[1], cotangent, scores],
-        scratch=[pltpu.VMEM((toks, model_width), BF16)],
-    )
-    d_pack, (x_first, mix_wide) = got[:groups], got[groups:]
-    d_got = [d_pack[0]] + [shift(d_pack[step], step) for step in range(1, groups)]
+
+    weighted, mix_wide = call(
+        weigh_body, [arr((toks, model_width)), arr((toks, 128), F32)], [cotangent, scores]
+    )
 
     def dispatch_x_body(*refs):
-        x_refs, send_refs, slot_ref = refs[:groups], refs[groups:-1], refs[-1]
+        x_refs, weighted_ref, outs = refs[:groups], refs[groups], refs[groups + 1 :]
+        send_refs, slot_ref, d_refs = outs[:owners], outs[owners], outs[owners + 1 :]
         for step in range(groups):
             group = group_at(-step)
             slot = slots_row(x_refs[step][toks : toks + extra, 0:toks][0:1].astype(F32))
             slot_ref[pl.ds(group * 8, 8), :] = jnp.broadcast_to(slot, (8, toks))
             send_rows(picker(slot), x_refs[step][0:toks, :], group, send_refs)
+            d_refs[step][...] = weighted_ref[:, columns_at(step)]
 
     got = call(
         dispatch_x_body,
-        [message] * owners + [arr((groups * 8, toks), jnp.int32)],
-        [x_got[0], x_first, *x_got[2:]],
+        [message] * owners + [arr((groups * 8, toks), jnp.int32)] + [arr((toks, width))] * groups,
+        [*x_got, weighted],
         flops=2 * groups * slot_total * toks * width,
     )
-    x_send, slots = got[:owners], got[owners]
+    x_send, slots, d_pack = got[:owners], got[owners], got[owners + 1 :]
+    d_got = [d_pack[0]] + [shift(d_pack[step], step) for step in range(1, groups)]
     rows_x = [x_send[0]] + [swap(x_send[bits], bits) for bits in range(1, owners)]
 
     full = pl.BlockSpec(memory_space=pltpu.VMEM)
@@ -293,33 +287,34 @@
                     out_ref[half, i, at, :] = refs[bits][half, i]
 
     halves, experts = range(2), range(local)
-    order = [(kind, half, i) for half in halves for i in experts for kind in "gu"]
-    order += [("b", half, i) for half in halves for i in experts]
+    assert local == 2
+    order = [(kind, 0, i) for i in experts for kind in "gu"]
+    order += [("g", 1, 0), ("u", 1, 0), ("b", 0, 0), ("b", 0, 1)]
+    order += [("g", 1, 1), ("u", 1, 1), ("b", 1, 0), ("b", 1, 1)]
     weight_of = {"g": w_gate, "u": w_up, "b": w_down}
     part, pair, total, final, near, far = {}, {}, {}, {}, {}, {}
 
     def first_body(*refs):
-        x_refs, w_refs = refs[:owners], refs[owners : owners + 2]
-        d_refs, slot_ref = refs[owners + 2 : owners + 2 + groups], refs[owners + 2 + groups]
-        outs = refs[owners + 3 + groups :]
+        x_refs, w_refs, outs = refs[:owners], refs[owners : owners + 2], refs[owners + 4 :]
+        outs[3][...], outs[4][...] = refs[owners + 2][...], refs[owners + 3][...]
         pack_rows(outs[2], x_refs)
         for out, w_ref in zip(outs[:2], w_refs):
             out[...] = mm(outs[2][0, 0], w_ref[0]).astype(BF16)
+
+    part[0], part[1], packed_x, d_got[1], d_got[3] = call(
+        first_body,
+        [piece, piece, packed] + [arr((toks, width))] * 2,
+        [*rows_x, w_gate, w_up, d_got[1], d_got[3]],
+        flops=2 * piece_flops,
+    )
+    near[0], near[1] = line_hop(part[0], inward), line_hop(part[1], inward)
+
+    def dispatch_d_body(*refs):
+        d_refs, slot_ref, out_refs = refs[:groups], refs[groups], refs[groups + 1 :]
         for step in range(groups):
             group = group_at(-step)
             slot = slot_ref[pl.ds(group * 8, 8), :][0:1]
-            send_rows(picker(slot), d_refs[step][...], group, outs[3:])
-
-    got = call(
-        first_body,
-        [piece, piece, packed] + [message] * owners,
-        [*rows_x, w_gate, w_up, *d_got, slots],
-        flops=2 * piece_flops + dispatch_flops,
-    )
-    part[0], part[1], packed_x = got[:3]
-    d_send = got[3:]
-    near[0], near[1] = line_hop(part[0], inward), line_hop(part[1], inward)
-    rows_d = [d_send[0]] + [swap(d_send[bits], bits) for bits in range(1, owners)]
+            send_rows(picker(slot), d_refs[step][...], group, out_refs)
 
     def at_end():
         place = lax.axis_index("dp")
@@ -330,7 +325,7 @@
 
     count = len(order)
 
-    def slot_call(t, rows=None, unpacked=None):
+    def slot_call(t, unpacked=None, also=None):
         take, cross, done = t < count, 0 <= t - 2 < count, 0 <= t - 4 < count
         ahead = t + 2 < count
         ins, specs, outs = [near[t]], [full], []
@@ -346,7 +341,7 @@
         specs = [full] * len(ins)
         if ahead:
             kind, half, i = order[t + 2]
-            ins += [rows, weight_of[kind]]
+            ins += [packed_d if kind == "b" else packed_x, weight_of[kind]]
             specs += [
                 pl.BlockSpec((1, 1, block, width), lambda *_: (half, i, 0, 0)),
                 pl.BlockSpec((1, *weight_of[kind].shape[1:]), lambda *_: (i, 0, 0)),
@@ -358,6 +353,10 @@
             ins += unpacked
             specs += [full] * owners
             outs.append(packed)
+        if also is not None:
+            ins += also[1]
+            specs += [full] * len(also[1])
+            outs += also[2]
         ins_count = len(ins)
 
         def body(*refs):
@@ -370,7 +369,8 @@
                 total_ref = right.pop(0)
                 total_ref[...] = plus(left.pop(0), left.pop(0))
             if done:
-                right.pop(0)[...] = jnp.where(at_end(), got_ref[...], left.pop(0)[...])
+                final_ref = right.pop(0)
+                final_ref[...] = jnp.where(at_end(), got_ref[...], left.pop(0)[...])
             if ahead:
                 rows_ref, w_ref, part_ref = left.pop(0), left.pop(0), right.pop(0)
                 product = mm_nt if kind == "b" else mm
@@ -379,6 +379,8 @@
                     right.pop(0)[...] = jnp.where(at_end(), part_ref[...], total_ref[...])
             if unpacked is not None:
                 pack_rows(right.pop(0), left)
+            if also is not None:
+                also[0](*left, *right, *([total_ref, final_ref] if done else []))
 
         got = list(call(body, outs, ins, specs=specs, flops=piece_flops if ahead else 0))
         if take:
@@ -394,50 +396,135 @@
             near[t + 2] = line_hop(got.pop(0), inward + outward)
         elif ahead:
             near[t + 2] = line_hop(part[t + 2], inward)
-        elif cross:
-            near[t + 2] = line_hop(total[t - 2], outward)
         return got
 
-    for t in range(3):
-        slot_call(t, packed_x)
-    (packed_d,) = slot_call(3, packed_x, unpacked=rows_d)
-    for t in range(4, count):
-        slot_call(t, packed_x if t + 2 < 2 * 2 * local else packed_d)
-
-    def spread(refs, half, i, value):
+    d_send = slot_call(0, also=(dispatch_d_body, [*d_got, slots], [message] * owners))
+    rows_d = [d_send[0]] + [swap(d_send[bits], bits) for bits in range(1, owners)]
+    slot_call(1)
+    slot_call(2)
+    (packed_d,) = slot_call(3, unpacked=rows_d)
+    for t in range(4, 7):
+        slot_call(t)
+
+    acts, half_message = arr((half_rows, units)), arr((local, pair_rows, width))
+
+    def spread(refs, i, value):
         for bits in range(owners):
-            rows = value[bits * pair_rows : (bits + 1) * pair_rows]
-            if half is None:
-                refs[bits][i] = rows
-            else:
-                refs[bits][half, i] = rows
-
-    acts = arr((half_rows, units))
-
-    def out_body(*refs):
-        w_ref, outs = refs[4 * local], refs[4 * local + 1 :]
-        hidden_refs, out_refs = outs[:2], outs[2:]
-        for half in halves:
-            for i in experts:
-                at = 2 * (half * local + i)
-                gate, up = refs[at][...].astype(F32), refs[at + 1][...].astype(F32)
-                rows = (gate * jax.nn.sigmoid(gate) * up).astype(BF16)
-                hidden_refs[half][i * block : (i + 1) * block, :] = rows
-                spread(out_refs, half, i, mm(rows, w_ref[i]).astype(BF16))
+            refs[bits][i] = value[bits * pair_rows : (bits + 1) * pair_rows]
+
+    assert local == 2
+    acts, two_pieces = arr((half_rows, units)), arr((2, block, units))
+
+    def out_rows(refs, w_ref, hidden_ref, out_refs):
+        for i in experts:
+            gate, up = refs[2 * i][...].astype(F32), refs[2 * i + 1][...].astype(F32)
+            rows = (gate * jax.nn.sigmoid(gate) * up).astype(BF16)
+            hidden_ref[i * block : (i + 1) * block, :] = rows
+            spread(out_refs, i, mm(rows, w_ref[i]).astype(BF16))
+
+    def even_out_body(*refs):
+        known, (w_ref, hidden_ref), out_refs = refs[:3], refs[3:5], refs[5 : 5 + owners]
+        out_rows([*known, refs[-1]], w_ref, hidden_ref, out_refs)
+
+    def sent_over(messages):
+        return [messages[0]] + [swap(messages[bits], bits) for bits in range(1, owners)]
+
+    def several(refs, *counts):
+        taken, at = [], 0
+        for n in counts:
+            taken.append(refs[at : at + n])
+            at += n
+        return taken
+
+    def chosen(total_piece, back_piece):
+        return jnp.where(at_end(), back_piece, total_piece)
+
+    def into_rows(gu, grads, w_refs, act_refs, in_refs):
+        for i in experts:
+            gate, up, grad = (v.astype(F32) for v in (gu[2 * i], gu[2 * i + 1], grads[i]))
+            rows = slice(i * block, (i + 1) * block)
+            sigma = jax.nn.sigmoid(gate)
+            act_gate = (grad * up * sigma * (1.0 + gate * (1.0 - sigma))).astype(BF16)
+            act_up = (grad * (gate * sigma)).astype(BF16)
+            act_refs[0][rows, :] = act_gate
+            act_refs[1][rows, :] = act_up
+            into = mm_nt(act_gate, w_refs[0][i]) + mm_nt(act_up, w_refs[1][i])
+            spread(in_refs, i, into.astype(BF16))
+
+    assert count == 12
+    got = slot_call(
+        7,
+        also=(
+            even_out_body,
+            [final[name] for name in order[:3]] + [w_down],
+            [acts] + [half_message] * owners,
+        ),
+    )
+    hidden_even, out_even = got[0], sent_over(got[1:])
+    for t in range(8, 10):
+        slot_call(t)
+    slot_call(10, also=(lambda *refs: None, out_even[1:], []))
+
+    two_pieces = arr((2, block, units))
+    even_names = [name for name in order[:4]]
+
+    def in_even_body(*refs):
+        known, (b_ref, before_ref), w_refs, act_refs, in_refs, (two_ref, total_ref, final_ref) = (
+            several(refs, 4, 2, 2, 2, owners, 3)
+        )
+        two_ref[0], two_ref[1] = before_ref[...], total_ref[...]
+        grads = [b_ref[...], final_ref[...]]
+        into_rows([r[...] for r in known], grads, w_refs, act_refs, in_refs)
+
+    got = slot_call(
+        11,
+        also=(
+            in_even_body,
+            [final[name] for name in even_names] + [final["b", 0, 0], total[8], w_gate, w_up],
+            [acts, acts] + [half_message] * owners + [two_pieces],
+        ),
+    )
+    acts0, in_got0, two_total = got[:2], sent_over(got[2:-1]), got[-1]
+    two_back = line_hop(two_total, outward)
+
+    def cross_body(*refs):
+        for n in range(2):
+            refs[4][n] = plus(refs[2 * n], refs[2 * n + 1])
+
+    (odd_total,) = call(cross_body, [two_pieces], [pair[10], far[10], pair[11], far[11]])
+    odd_back = line_hop(odd_total, outward)
+
+    def odd_out_body(*refs):
+        known, (total_ref, back_ref, w_ref, hidden_ref), out_refs, last_refs = several(
+            refs, 2, 4, owners, 2
+        )
+        for n in range(2):
+            last_refs[n][...] = chosen(total_ref[n], back_ref[n])
+        out_rows([*known, *last_refs], w_ref, hidden_ref, out_refs)
 
     got = call(
-        out_body,
-        [acts, acts] + [message] * owners,
-        [final[name] for name in order[: 4 * local]] + [w_down],
+        odd_out_body,
+        [acts] + [half_message] * owners + [piece] * 2,
+        [final["g", 1, 0], final["u", 1, 0], two_total, two_back, w_down],
         flops=2 * local * piece_flops,
     )
-    hidden, out_send = got[:2], got[2:]
-    out_got = [out_send[0]] + [swap(out_send[bits], bits) for bits in range(1, owners)]
-
-    for t in range(count, count + 4):
-        slot_call(t)
-
-    half_message = arr((local, pair_rows, width))
+    hidden, out_odd, gu_last = [hidden_even, got[0]], sent_over(got[1:-2]), got[-2:]
+
+    def last_body(*refs):
+        known, (total_ref, back_ref), w_refs, _, act_refs, in_refs = several(
+            refs, 4, 2, 2, owners, 2, owners
+        )
+        grads = [chosen(total_ref[i], back_ref[i]) for i in experts]
+        into_rows([r[...] for r in known], grads, w_refs, act_refs, in_refs)
+
+    got = call(
+        last_body,
+        [acts, acts] + [half_message] * owners,
+        [final["g", 1, 0], final["u", 1, 0], *gu_last, odd_total, odd_back, w_gate, w_up]
+        + [*in_got0[1:], out_odd[1]],
+        flops=4 * local * piece_flops,
+    )
+    acts1, in_got1 = got[:2], sent_over(got[2:])
 
     def combined(slot_ref, group, block_of):
         place = group // 2 * cap
@@ -449,85 +536,53 @@
         pick = picker(slot_ref[group * 8 : group * 8 + 1, :])
         return mm_tn(pick, jnp.concatenate(rows, axis=0)).astype(BF16)
 
-    def in_call(half):
-        ins = [final[kind, half, i] for i in experts for kind in "gub"] + [w_gate, w_up]
-        count = len(ins)
-
-        def body(*refs):
-            gate_w, up_w = refs[count - 2], refs[count - 1]
-            act_refs, in_refs = refs[count : count + 2], refs[count + 2 :]
-            for i in experts:
-                gate, up, grad = (refs[3 * i + n][...].astype(F32) for n in range(3))
-                rows = slice(i * block, (i + 1) * block)
-                sigma = jax.nn.sigmoid(gate)
-                act_gate = (grad * up * sigma * (1.0 + gate * (1.0 - sigma))).astype(BF16)
-                act_up = (grad * (gate * sigma)).astype(BF16)
-                act_refs[0][rows, :] = act_gate
-                act_refs[1][rows, :] = act_up
-                into = mm_nt(act_gate, gate_w[i]) + mm_nt(act_up, up_w[i])
-                spread(in_refs, None, i, into.astype(BF16))
-
-        got = call(
-            body, [acts, acts] + [half_message] * owners, ins, flops=4 * piece_flops
+    def out_tokens_body(*refs):
+        even_refs, odd_refs, (slot_ref, _), tok_refs, (sum_ref,) = several(
+            refs, owners, owners, 2, groups, 1
         )
-        sent = got[2:]
-        return got[:2], [sent[0]] + [swap(sent[bits], bits) for bits in range(1, owners)]
-
-    acts0, in_got0 = in_call(0)
-    acts1, in_got1 = in_call(1)
-
-    def tokens_body(*refs):
-        o_refs, i_refs, slot_ref = refs[:owners], refs[owners : 2 * owners], refs[2 * owners]
-        outs = refs[2 * owners + 2 :]
-        sum_ref = refs[-1]
         for group in range(groups):
+            o_refs = odd_refs if group % 2 else even_refs
             sum_ref[group] = combined(
-                slot_ref, group, lambda bits, i, rows: o_refs[bits][group % 2, i, rows, :]
+                slot_ref, group, lambda bits, i, rows: o_refs[bits][i, rows, :]
             )
-        for group in range(0, groups, 2):
-            outs[groups][group // 2] = combined(
+        for step in range(groups):
+            tok_refs[step][...] = sum_ref[group_at(-step)]
+
+    whole_rows = [pltpu.VMEM((groups, toks, width), BF16)]
+    out_tok = call(
+        out_tokens_body,
+        [arr((toks, width))] * groups,
+        [*out_even, *out_odd, slots, acts1[0]],
+        scratch=whole_rows,
+        flops=dispatch_flops,
+    )
+    out_chunk = [out_tok[0]] + [shift(out_tok[step], -step) for step in range(1, groups)]
+
+    def in_tokens_body(*refs):
+        even_refs, odd_refs, (slot_ref,), tok_refs, (sum_ref,) = several(
+            refs, owners, owners, 1, groups, 1
+        )
+        for group in range(groups):
+            i_refs = odd_refs if group % 2 else even_refs
+            sum_ref[group] = combined(
                 slot_ref, group, lambda bits, i, rows: i_refs[bits][i, rows, :]
             )
         for step in range(groups):
-            outs[step][...] = sum_ref[group_at(-step)]
-
-    got = call(
-        tokens_body,
-        [arr((toks, width))] * groups + [arr((groups // 2, toks, width))],
-        [*out_got, *in_got0, slots, acts1[0]],
-        scratch=[pltpu.VMEM((groups, toks, width), BF16)],
-        flops=2 * dispatch_flops,
-    )
-    out_tok, in_even = got[:groups], got[groups]
-    out_chunk = [out_tok[0]] + [shift(out_tok[step], -step) for step in range(1, groups)]
-
-    def in_tokens_body(*refs):
-        i_refs, even_ref, slot_ref = refs[:owners], refs[owners], refs[owners + 1]
-        sum_ref = refs[-1]
-        for group in range(groups):
-            if group % 2 == 0:
-                sum_ref[group] = even_ref[group // 2]
-            else:
-                sum_ref[group] = combined(
-                    slot_ref, group, lambda bits, i, rows: i_refs[bits][i, rows, :]
-                )
-        for step in range(groups):
-            refs[owners + 2 + step][...] = sum_ref[group_at(-step)]
+            tok_refs[step][...] = sum_ref[group_at(-step)]
 
     in_tok = call(
         in_tokens_body,
         [arr((toks, width))] * groups,
-        [*in_got1, in_even, slots],
-        scratch=[pltpu.VMEM((groups, toks, width), BF16)],
+        [*in_got0, *in_got1, slots],
+        scratch=whole_rows,
         flops=dispatch_flops,
     )
     in_chunk = [in_tok[0]] + [shift(in_tok[step], -step) for step in range(1, groups)]
 
     per_part = groups // 2
-    part_width = per_part * width
 
     def assemble_body(*refs):
-        chunk_refs, give_ref, keep_ref, whole_ref = refs[:groups], *refs[groups:]
+        chunk_refs, (give_ref, keep_ref, whole_ref) = several(refs, groups, 3)
         for step in range(groups):
             whole_ref[group_at(step)] = chunk_refs[step][...]
         mine = lax.axis_index("tensor")
@@ -536,18 +591,15 @@
             give_ref[:, at] = whole_ref[(1 - mine) * per_part + j]
             keep_ref[:, at] = whole_ref[mine * per_part + j]
 
-    def assemble(chunks):
+    def across(chunks):
         give, keep = call(
-            assemble_body,
-            [arr((toks, part_width))] * 2,
-            chunks,
-            scratch=[pltpu.VMEM((groups, toks, width), BF16)],
+            assemble_body, [arr((toks, per_part * width))] * 2, chunks, scratch=whole_rows
         )
         other = lax.ppermute(give, "tensor", [(0, 1), (1, 0)])
         return keep.astype(F32) + other.astype(F32)
 
-    output = (mix_wide[:, 0:1] * assemble(out_chunk)).astype(BF16)
-    grad_tokens = assemble(in_chunk).astype(BF16)
+    output = (mix_wide[:, 0:1] * across(out_chunk)).astype(BF16)
+    grad_tokens = across(in_chunk).astype(BF16)
 
     def weight_grad(rows, acts, shape, rows_first):
         def body(*refs):

time: 169 us -> 176 us (1.041)
  waiting for transfers between devices: 54.9 us -> 70.5 us
  starting transfers between devices: 92.3 us -> 83.1 us
    ppermute x12, waiting for transfers between devices: 21 us -> 35.8 us  [shift(): lax.ppermute(value, 'dp', [(j, (j + step) % groups) for j in range(groups)])]
    ppermute x12, starting transfers between devices: 28.5 us -> 19.3 us  [shift(): lax.ppermute(value, 'dp', [(j, (j + step) % groups) for j in range(groups)])]
    ppermute x28 -> x26, waiting for transfers between devices: 17.9 us -> 23.6 us  [line_hop(): return lax.ppermute(value, 'dp', pairs)]
    ppermute x15 -> x18, waiting for transfers between devices: 12 us -> 6.96 us  [swap(): return lax.ppermute(value, 'expert', [(j, j ^ bits) for j in range(owners)])]
    pallas_call x30 -> x26, Pallas kernels: 14.6 us -> 15.3 us  [call(): pl.pallas_call(body, out_shape=outs, grid=() if specs is None else (1,),...]
    ppermute x28 -> x26, starting transfers between devices: 51.6 us -> 51.7 us  [line_hop(): return lax.ppermute(value, 'dp', pairs)]
    ppermute x15 -> x18, starting transfers between devices: 10 us -> 9.9 us  [swap(): return lax.ppermute(value, 'expert', [(j, j ^ bits) for j in range(owners)])]
  transfers between devices with their start and end apart: 57 -> 58, of which waited for: 22 -> 17; matrix products, arithmetic and copies ran while one was open for 1% -> 1% of each run, Pallas kernels for 8% -> 8%
where the time goes in v6:
time: 176 us; the launch traced here: 175 us
  starting transfers between devices  83.1 us (47%)
  waiting for transfers between devices  70.5 us (40%)
  Pallas kernels  15.3 us (9%)
  local copies, waits for them, and re-layouts  3.75 us (2%)
    ppermute x26, starting transfers between devices, line_hop(): return lax.ppermute(value, 'dp', pairs)  51.7 us
    ppermute x12, waiting for transfers between devices, shift(): lax.ppermute(value, 'dp', [(j, (j + step) % groups) for j in range(groups)])  35.8 us
    ppermute x26, waiting for transfers between devices, line_hop(): return lax.ppermute(value, 'dp', pairs)  23.6 us
    ppermute x12, starting transfers between devices, shift(): lax.ppermute(value, 'dp', [(j, (j + step) % groups) for j in range(groups)])  19.3 us
    pallas_call x26, Pallas kernels, call(): pl.pallas_call(body, out_shape=outs, grid=() if specs is None else (1,),...  15.3 us
    ppermute x18, starting transfers between devices, swap(): return lax.ppermute(value, 'expert', [(j, j ^ bits) for j in range(owners)])  9.9 us
    ppermute x18, waiting for transfers between devices, swap(): return lax.ppermute(value, 'expert', [(j, j ^ bits) for j in range(owners)])  6.96 us
    ppermute x2, waiting for transfers between devices, across(): other = lax.ppermute(give, 'tensor', [(0, 1), (1, 0)])  4.18 us
  transfers between devices with their start and end apart: 58, of which 17 were waited for; matrix products, arithmetic and copies ran while one was open for 1% of the time, Pallas kernels for 8%

profile of v6, /device:TPU:0, one launch (start us, length us, event | category | flops | bytes accessed | tf_op | source)
XLA Modules:
  0.0 175.5 jit_solution(4476188569752575155)
XLA Ops:
  2.5 3.1 %collective-permute-start = (bf16[144,512]{1,0:T(8,128)(2,1)S(1)}, bf16[144,512]{1,0:T(8,128)(2,1)S(1)}, u32[]{:S(2)}, u32[]{:S(2)}) collective-permute-start(bf16[144,512]{1,0:T(8,128)(2,1)S(1)} %get-tuple-element.115), channel_id=1, source_target_pairs={{0,8},{8,16},{16,24},{24,0},{1,9},{9,17},{17,25},{25,1},{2,10},{10... | collective-permute-start | bytes 442376 | tf_op jit(solution)/shard_map/ppermute | solution.py:190
  5.6 2.6 %collective-permute-start.1 = (bf16[144,512]{1,0:T(8,128)(2,1)S(1)}, bf16[144,512]{1,0:T(8,128)(2,1)S(1)}, u32[]{:S(2)}, u32[]{:S(2)}) collective-permute-start(bf16[144,512]{1,0:T(8,128)(2,1)S(1)} %get-tuple-element.116), channel_id=1, source_target_pairs={{0,16},{8,24},{16,0},{24,8},{1,17},{9,25},{17,1},{25,9},{2,18},{10... | collective-permute-start | bytes 442376 | tf_op jit(solution)/shard_map/ppermute | solution.py:190
  12.4 5.5 %collective-permute-done.1.refs_2_ = bf16[144,512]{1,0:T(8,128)(2,1)S(1)} collective-permute-done((bf16[144,512]{1,0:T(8,128)(2,1)S(1)}, bf16[144,512]{1,0:T(8,128)(2,1)S(1)}, u32[]{:S(2)}, u32[]{:S(2)}) %collective-permute-start.1) | collective-permute-done | bytes 147488 | tf_op jit(solution)/shard_map/ppermute | solution.py:190
  20.3 3.6 %collective-permute-start.6 = (bf16[128,512]{1,0:T(8,128)(2,1)S(1)}, bf16[128,512]{1,0:T(8,128)(2,1)S(1)}, u32[]{:S(2)}, u32[]{:S(2)}) collective-permute-start(bf16[128,512]{1,0:T(8,128)(2,1)S(1)} %get-tuple-element.123), channel_id=1, source_target_pairs={{0,8},{8,16},{16,24},{24,0},{1,9},{9,17},{17,25},{25,1},{2,10},{10... | collective-permute-start | bytes 393224 | tf_op jit(solution)/shard_map/ppermute | solution.py:190
  25.0 4.4 %collective-permute-done.6.refs_6_ = bf16[128,512]{1,0:T(8,128)(2,1)S(1)} collective-permute-done((bf16[128,512]{1,0:T(8,128)(2,1)S(1)}, bf16[128,512]{1,0:T(8,128)(2,1)S(1)}, u32[]{:S(2)}, u32[]{:S(2)}) %collective-permute-start.6) | collective-permute-done | bytes 131104 | tf_op jit(solution)/shard_map/ppermute | solution.py:190
  29.4 2.4 %collective-permute-done.7.refs_7_ = bf16[128,512]{1,0:T(8,128)(2,1)S(1)} collective-permute-done((bf16[128,512]{1,0:T(8,128)(2,1)S(1)}, bf16[128,512]{1,0:T(8,128)(2,1)S(1)}, u32[]{:S(2)}, u32[]{:S(2)}) %collective-permute-start.7) | collective-permute-done | bytes 131104 | tf_op jit(solution)/shard_map/ppermute | solution.py:190
  32.8 5.5 %collective-permute-start.11 = (bf16[256,384]{1,0:T(8,128)(2,1)S(1)}, bf16[256,384]{1,0:T(8,128)(2,1)S(1)}, u32[]{:S(2)}, u32[]{:S(2)}) collective-permute-start(bf16[256,384]{1,0:T(8,128)(2,1)S(1)} %get-tuple-element.129.refs_1_), channel_id=1, source_target_pairs={{0,8},{24,16},{1,9},{25,17},{2,10},{26,18},{3,11},{27,19},{4,12},{... | collective-permute-start | bytes 589832 | tf_op jit(solution)/shard_map/ppermute | solution.py:198
  38.5 2.9 %collective-permute-start.8 = (bf16[256,384]{1,0:T(8,128)(2,1)S(1)}, bf16[256,384]{1,0:T(8,128)(2,1)S(1)}, u32[]{:S(2)}, u32[]{:S(2)}) collective-permute-start(bf16[256,384]{1,0:T(8,128)(2,1)S(1)} %get-tuple-element.125.refs_1_), channel_id=1, source_target_pairs={{0,8},{24,16},{1,9},{25,17},{2,10},{26,18},{3,11},{27,19},{4,12},{... | collective-permute-start | bytes 589832 | tf_op jit(solution)/shard_map/ppermute | solution.py:198
  41.4 6.2 %collective-permute-done.12.refs_6_ = bf16[128,512]{1,0:T(8,128)(2,1)S(1)} collective-permute-done((bf16[128,512]{1,0:T(8,128)(2,1)S(1)}, bf16[128,512]{1,0:T(8,128)(2,1)S(1)}, u32[]{:S(2)}, u32[]{:S(2)}) %collective-permute-start.12) | collective-permute-done | bytes 131104 | tf_op jit(solution)/shard_map/ppermute | solution.py:190
  54.2 4.4 %collective-permute-start.9 = (bf16[256,384]{1,0:T(8,128)(2,1)S(1)}, bf16[256,384]{1,0:T(8,128)(2,1)S(1)}, u32[]{:S(2)}, u32[]{:S(2)}) collective-permute-start(bf16[256,384]{1,0:T(8,128)(2,1)S(1)} %get-tuple-element.127.refs_1_), channel_id=1, source_target_pairs={{0,8},{24,16},{1,9},{25,17},{2,10},{26,18},{3,11},{27,19},{4,12},{... | collective-permute-start | bytes 589832 | tf_op jit(solution)/shard_map/ppermute | solution.py:198
  59.7 3.4 %collective-permute-done.9.refs_0_ = bf16[256,384]{1,0:T(8,128)(2,1)S(1)} collective-permute-done((bf16[256,384]{1,0:T(8,128)(2,1)S(1)}, bf16[256,384]{1,0:T(8,128)(2,1)S(1)}, u32[]{:S(2)}, u32[]{:S(2)}) %collective-permute-start.9) | collective-permute-done | bytes 196640 | tf_op jit(solution)/shard_map/ppermute | solution.py:198
  63.1 2.5 %collective-permute-start.22 = (bf16[256,384]{1,0:T(8,128)(2,1)S(1)}, bf16[256,384]{1,0:T(8,128)(2,1)S(1)}, u32[]{:S(2)}, u32[]{:S(2)}) collective-permute-start(bf16[256,384]{1,0:T(8,128)(2,1)S(1)} %get-tuple-element.150), channel_id=1, source_target_pairs={{0,8},{24,16},{8,0},{16,24},{1,9},{25,17},{9,1},{17,25},{2,10},{26... | collective-permute-start | bytes 589832 | tf_op jit(solution)/shard_map/ppermute | solution.py:198
  66.7 3.2 %collective-permute-start.16 = (bf16[256,384]{1,0:T(8,128)(2,1)S(1)}, bf16[256,384]{1,0:T(8,128)(2,1)S(1)}, u32[]{:S(2)}, u32[]{:S(2)}) collective-permute-start(bf16[256,384]{1,0:T(8,128)(2,1)S(1)} %get-tuple-element.139), channel_id=1, source_target_pairs={{0,8},{24,16},{8,0},{16,24},{1,9},{25,17},{9,1},{17,25},{2,10},{26... | collective-permute-start | bytes 589832 | tf_op jit(solution)/shard_map/ppermute | solution.py:198
  70.9 5.7 %collective-permute-start.24 = (bf16[256,384]{1,0:T(8,128)(2,1)S(1)}, bf16[256,384]{1,0:T(8,128)(2,1)S(1)}, u32[]{:S(2)}, u32[]{:S(2)}) collective-permute-start(bf16[256,384]{1,0:T(8,128)(2,1)S(1)} %get-tuple-element.156), channel_id=1, source_target_pairs={{0,8},{24,16},{8,0},{16,24},{1,9},{25,17},{9,1},{17,25},{2,10},{26... | collective-permute-start | bytes 589832 | tf_op jit(solution)/shard_map/ppermute | solution.py:198
  77.8 2.5 %collective-permute-start.18 = (bf16[256,384]{1,0:T(8,128)(2,1)S(1)}, bf16[256,384]{1,0:T(8,128)(2,1)S(1)}, u32[]{:S(2)}, u32[]{:S(2)}) collective-permute-start(bf16[256,384]{1,0:T(8,128)(2,1)S(1)} %get-tuple-element.144), channel_id=1, source_target_pairs={{0,8},{24,16},{8,0},{16,24},{1,9},{25,17},{9,1},{17,25},{2,10},{26... | collective-permute-start | bytes 589832 | tf_op jit(solution)/shard_map/ppermute | solution.py:198
  82.0 4.3 %collective-permute-start.29 = (bf16[256,384]{1,0:T(8,128)(2,1)S(1)}, bf16[256,384]{1,0:T(8,128)(2,1)S(1)}, u32[]{:S(2)}, u32[]{:S(2)}) collective-permute-start(bf16[256,384]{1,0:T(8,128)(2,1)S(1)} %get-tuple-element.165), channel_id=1, source_target_pairs={{0,8},{24,16},{8,0},{16,24},{1,9},{25,17},{9,1},{17,25},{2,10},{26... | collective-permute-start | bytes 589832 | tf_op jit(solution)/shard_map/ppermute | solution.py:198
  87.7 3.1 %collective-permute-start.31 = (bf16[256,384]{1,0:T(8,128)(2,1)S(1)}, bf16[256,384]{1,0:T(8,128)(2,1)S(1)}, u32[]{:S(2)}, u32[]{:S(2)}) collective-permute-start(bf16[256,384]{1,0:T(8,128)(2,1)S(1)} %get-tuple-element.170), channel_id=1, source_target_pairs={{0,8},{24,16},{8,0},{16,24},{1,9},{25,17},{9,1},{17,25},{2,10},{26... | collective-permute-start | bytes 589832 | tf_op jit(solution)/shard_map/ppermute | solution.py:198
  93.5 2.5 %collective-permute-start.35 = (bf16[256,384]{1,0:T(8,128)(2,1)S(1)}, bf16[256,384]{1,0:T(8,128)(2,1)S(1)}, u32[]{:S(2)}, u32[]{:S(2)}) collective-permute-start(bf16[256,384]{1,0:T(8,128)(2,1)S(1)} %get-tuple-element.180), channel_id=1, source_target_pairs={{0,8},{24,16},{8,0},{16,24},{1,9},{25,17},{9,1},{17,25},{2,10},{26... | collective-permute-start | bytes 589832 | tf_op jit(solution)/shard_map/ppermute | solution.py:198
  100.1 5.7 %collective-permute-done.28.refs_7_.refs_3_ = bf16[2,64,512]{2,1,0:T(8,128)(2,1)S(1)} collective-permute-done((bf16[2,64,512]{2,1,0:T(8,128)(2,1)S(1)}, bf16[2,64,512]{2,1,0:T(8,128)(2,1)S(1)}, u32[]{:S(2)}, u32[]{:S(2)}) %collective-permute-start.28) | collective-permute-done | bytes 131104 | tf_op jit(solution)/shard_map/ppermute | solution.py:193
  113.7 13.9 %collective-permute-done.37.refs_3_ = bf16[2,256,384]{2,1,0:T(8,128)(2,1)S(1)} collective-permute-done((bf16[2,256,384]{2,1,0:T(8,128)(2,1)S(1)}, bf16[2,256,384]{2,1,0:T(8,128)(2,1)S(1)}, u32[]{:S(2)}, u32[]{:S(2)}) %collective-permute-start.37) | collective-permute-done | bytes 393248 | tf_op jit(solution)/shard_map/ppermute | solution.py:198
  130.0 4.8 %collective-permute-done.43.refs_5_ = bf16[2,256,384]{2,1,0:T(8,128)(2,1)S(1)} collective-permute-done((bf16[2,256,384]{2,1,0:T(8,128)(2,1)S(1)}, bf16[2,256,384]{2,1,0:T(8,128)(2,1)S(1)}, u32[]{:S(2)}, u32[]{:S(2)}) %collective-permute-start.43) | collective-permute-done | bytes 393248 | tf_op jit(solution)/shard_map/ppermute | solution.py:198
  142.8 8.3 %collective-permute-done.48.refs_2_ = bf16[128,512]{1,0:T(8,128)(2,1)S(1)} collective-permute-done((bf16[128,512]{1,0:T(8,128)(2,1)S(1)}, bf16[128,512]{1,0:T(8,128)(2,1)S(1)}, u32[]{:S(2)}, u32[]{:S(2)}) %collective-permute-start.48) | collective-permute-done | bytes 131104 | tf_op jit(solution)/shard_map/ppermute | solution.py:190
  161.1 6.1 %collective-permute-done.55.refs_2_ = bf16[128,512]{1,0:T(8,128)(2,1)S(1)} collective-permute-done((bf16[128,512]{1,0:T(8,128)(2,1)S(1)}, bf16[128,512]{1,0:T(8,128)(2,1)S(1)}, u32[]{:S(2)}, u32[]{:S(2)}) %collective-permute-start.55) | collective-permute-done | bytes 131104 | tf_op jit(solution)/shard_map/ppermute | solution.py:190
  170.5 4.2 %collective-permute-done.57 = bf16[128,1024]{1,0:T(8,128)(2,1)S(1)} collective-permute-done((bf16[128,1024]{1,0:T(8,128)(2,1)S(1)}, bf16[128,1024]{1,0:T(8,128)(2,1)S(1)}, u32[]{:S(2)}, u32[]{:S(2)}) %collective-permute-start.57) | collective-permute-done | bytes 262176 | tf_op jit(solution)/shard_map/ppermute | solution.py:598
  (134 shorter events, 63.4 us)
Async XLA Ops:
  5.6 12.3 %collective-permute-start.1 = (bf16[144,512]{1,0:T(8,128)(2,1)S(1)}, bf16[144,512]{1,0:T(8,128)(2,1)S(1)}, u32[]{:S(2)}, u32[]{:S(2)}) collective-permute-start(bf16[144,512]{1,0:T(8,128)(2,1)S(1)} %get-tuple-element.116), channel_id=1, source_target_pairs={{0,16},{8,24},{16,0},{24,8},{1,17},{9,25},{17,1},{25,9},{2,18},{10... | collective-permute-start | bytes 442376 | tf_op jit(solution)/shard_map/ppermute | solution.py:190
  18.4 13.5 %collective-permute-start.3 = (bf16[2,2,64,512]{3,2,1,0:T(8,128)(2,1)S(1)}, bf16[2,2,64,512]{3,2,1,0:T(8,128)(2,1)S(1)}, u32[]{:S(2)}, u32[]{:S(2)}) collective-permute-start(bf16[2,2,64,512]{3,2,1,0:T(8,128)(2,1)S(1)} %get-tuple-element.120), channel_id=1, source_target_pairs={{0,2},{2,0},{4,6},{6,4},{1,3},{3,1},{5,7},{7,5},{8,10},{10,8},{12,... | collective-permute-start | bytes 786440 | tf_op jit(solution)/shard_map/ppermute | solution.py:193
  18.5 13.4 %collective-permute-start.4 = (bf16[2,2,64,512]{3,2,1,0:T(8,128)(2,1)S(1)}, bf16[2,2,64,512]{3,2,1,0:T(8,128)(2,1)S(1)}, u32[]{:S(2)}, u32[]{:S(2)}) collective-permute-start(bf16[2,2,64,512]{3,2,1,0:T(8,128)(2,1)S(1)} %get-tuple-element.121), channel_id=1, source_target_pairs={{0,4},{2,6},{4,0},{6,2},{1,5},{3,7},{5,1},{7,3},{8,12},{10,14},{12... | collective-permute-start | bytes 786440 | tf_op jit(solution)/shard_map/ppermute | solution.py:193
  20.0 12.3 %collective-permute-start.5 = (bf16[2,2,64,512]{3,2,1,0:T(8,128)(2,1)S(1)}, bf16[2,2,64,512]{3,2,1,0:T(8,128)(2,1)S(1)}, u32[]{:S(2)}, u32[]{:S(2)}) collective-permute-start(bf16[2,2,64,512]{3,2,1,0:T(8,128)(2,1)S(1)} %get-tuple-element.122), channel_id=1, source_target_pairs={{0,6},{2,4},{4,2},{6,0},{1,7},{3,5},{5,3},{7,1},{8,14},{10,12},{12... | collective-permute-start | bytes 786440 | tf_op jit(solution)/shard_map/ppermute | solution.py:193
  32.8 14.7 %collective-permute-start.11 = (bf16[256,384]{1,0:T(8,128)(2,1)S(1)}, bf16[256,384]{1,0:T(8,128)(2,1)S(1)}, u32[]{:S(2)}, u32[]{:S(2)}) collective-permute-start(bf16[256,384]{1,0:T(8,128)(2,1)S(1)} %get-tuple-element.129.refs_1_), channel_id=1, source_target_pairs={{0,8},{24,16},{1,9},{25,17},{2,10},{26,18},{3,11},{27,19},{4,12},{... | collective-permute-start | bytes 589832 | tf_op jit(solution)/shard_map/ppermute | solution.py:198
  38.5 14.3 %collective-permute-start.8 = (bf16[256,384]{1,0:T(8,128)(2,1)S(1)}, bf16[256,384]{1,0:T(8,128)(2,1)S(1)}, u32[]{:S(2)}, u32[]{:S(2)}) collective-permute-start(bf16[256,384]{1,0:T(8,128)(2,1)S(1)} %get-tuple-element.125.refs_1_), channel_id=1, source_target_pairs={{0,8},{24,16},{1,9},{25,17},{2,10},{26,18},{3,11},{27,19},{4,12},{... | collective-permute-start | bytes 589832 | tf_op jit(solution)/shard_map/ppermute | solution.py:198
  51.1 15.1 %collective-permute-start.13 = (bf16[2,2,64,512]{3,2,1,0:T(8,128)(2,1)S(1)}, bf16[2,2,64,512]{3,2,1,0:T(8,128)(2,1)S(1)}, u32[]{:S(2)}, u32[]{:S(2)}) collective-permute-start(bf16[2,2,64,512]{3,2,1,0:T(8,128)(2,1)S(1)} %get-tuple-element.136), channel_id=1, source_target_pairs={{0,2},{2,0},{4,6},{6,4},{1,3},{3,1},{5,7},{7,5},{8,10},{10,8},{12,... | collective-permute-start | bytes 786440 | tf_op jit(solution)/shard_map/ppermute | solution.py:193
  51.2 15.0 %collective-permute-start.14 = (bf16[2,2,64,512]{3,2,1,0:T(8,128)(2,1)S(1)}, bf16[2,2,64,512]{3,2,1,0:T(8,128)(2,1)S(1)}, u32[]{:S(2)}, u32[]{:S(2)}) collective-permute-start(bf16[2,2,64,512]{3,2,1,0:T(8,128)(2,1)S(1)} %get-tuple-element.137), channel_id=1, source_target_pairs={{0,4},{2,6},{4,0},{6,2},{1,5},{3,7},{5,1},{7,3},{8,12},{10,14},{12... | collective-permute-start | bytes 786440 | tf_op jit(solution)/shard_map/ppermute | solution.py:193
  52.7 13.5 %collective-permute-start.15 = (bf16[2,2,64,512]{3,2,1,0:T(8,128)(2,1)S(1)}, bf16[2,2,64,512]{3,2,1,0:T(8,128)(2,1)S(1)}, u32[]{:S(2)}, u32[]{:S(2)}) collective-permute-start(bf16[2,2,64,512]{3,2,1,0:T(8,128)(2,1)S(1)} %get-tuple-element.138), channel_id=1, source_target_pairs={{0,6},{2,4},{4,2},{6,0},{1,7},{3,5},{5,3},{7,1},{8,14},{10,12},{12... | collective-permute-start | bytes 786440 | tf_op jit(solution)/shard_map/ppermute | solution.py:193
  66.7 10.7 %collective-permute-start.16 = (bf16[256,384]{1,0:T(8,128)(2,1)S(1)}, bf16[256,384]{1,0:T(8,128)(2,1)S(1)}, u32[]{:S(2)}, u32[]{:S(2)}) collective-permute-start(bf16[256,384]{1,0:T(8,128)(2,1)S(1)} %get-tuple-element.139), channel_id=1, source_target_pairs={{0,8},{24,16},{8,0},{16,24},{1,9},{25,17},{9,1},{17,25},{2,10},{26... | collective-permute-start | bytes 589832 | tf_op jit(solution)/shard_map/ppermute | solution.py:198
  70.9 10.7 %collective-permute-start.24 = (bf16[256,384]{1,0:T(8,128)(2,1)S(1)}, bf16[256,384]{1,0:T(8,128)(2,1)S(1)}, u32[]{:S(2)}, u32[]{:S(2)}) collective-permute-start(bf16[256,384]{1,0:T(8,128)(2,1)S(1)} %get-tuple-element.156), channel_id=1, source_target_pairs={{0,8},{24,16},{8,0},{16,24},{1,9},{25,17},{9,1},{17,25},{2,10},{26... | collective-permute-start | bytes 589832 | tf_op jit(solution)/shard_map/ppermute | solution.py:198
  93.5 12.3 %collective-permute-start.35 = (bf16[256,384]{1,0:T(8,128)(2,1)S(1)}, bf16[256,384]{1,0:T(8,128)(2,1)S(1)}, u32[]{:S(2)}, u32[]{:S(2)}) collective-permute-start(bf16[256,384]{1,0:T(8,128)(2,1)S(1)} %get-tuple-element.180), channel_id=1, source_target_pairs={{0,8},{24,16},{8,0},{16,24},{1,9},{25,17},{9,1},{17,25},{2,10},{26... | collective-permute-start | bytes 589832 | tf_op jit(solution)/shard_map/ppermute | solution.py:198
  109.0 18.5 %collective-permute-start.37 = (bf16[2,256,384]{2,1,0:T(8,128)(2,1)S(1)}, bf16[2,256,384]{2,1,0:T(8,128)(2,1)S(1)}, u32[]{:S(2)}, u32[]{:S(2)}) collective-permute-start(bf16[2,256,384]{2,1,0:T(8,128)(2,1)S(1)} %get-tuple-element.186.refs_2_), channel_id=1, source_target_pairs={{8,0},{16,24},{9,1},{17,25},{10,2},{18,26},{11,3},{19,27},{12,4},{... | collective-permute-start | bytes 1179656 | tf_op jit(solution)/shard_map/ppermute | solution.py:198
  110.5 24.4 %collective-permute-start.43 = (bf16[2,256,384]{2,1,0:T(8,128)(2,1)S(1)}, bf16[2,256,384]{2,1,0:T(8,128)(2,1)S(1)}, u32[]{:S(2)}, u32[]{:S(2)}) collective-permute-start(bf16[2,256,384]{2,1,0:T(8,128)(2,1)S(1)} %shard_map.127.refs_4_), channel_id=1, source_target_pairs={{8,0},{16,24},{9,1},{17,25},{10,2},{18,26},{11,3},{19,27},{12,4},{... | collective-permute-start | bytes 1179656 | tf_op jit(solution)/shard_map/ppermute | solution.py:198
  111.8 16.4 %collective-permute-start.44 = (bf16[2,64,512]{2,1,0:T(8,128)(2,1)S(1)}, bf16[2,64,512]{2,1,0:T(8,128)(2,1)S(1)}, u32[]{:S(2)}, u32[]{:S(2)}) collective-permute-start(bf16[2,64,512]{2,1,0:T(8,128)(2,1)S(1)} %get-tuple-element.195), channel_id=1, source_target_pairs={{0,2},{2,0},{4,6},{6,4},{1,3},{3,1},{5,7},{7,5},{8,10},{10,8},{12,... | collective-permute-start | bytes 393224 | tf_op jit(solution)/shard_map/ppermute | solution.py:193
  111.9 17.0 %collective-permute-start.45 = (bf16[2,64,512]{2,1,0:T(8,128)(2,1)S(1)}, bf16[2,64,512]{2,1,0:T(8,128)(2,1)S(1)}, u32[]{:S(2)}, u32[]{:S(2)}) collective-permute-start(bf16[2,64,512]{2,1,0:T(8,128)(2,1)S(1)} %get-tuple-element.196), channel_id=1, source_target_pairs={{0,4},{2,6},{4,0},{6,2},{1,5},{3,7},{5,1},{7,3},{8,12},{10,14},{12... | collective-permute-start | bytes 393224 | tf_op jit(solution)/shard_map/ppermute | solution.py:193
  112.5 17.5 %collective-permute-start.46 = (bf16[2,64,512]{2,1,0:T(8,128)(2,1)S(1)}, bf16[2,64,512]{2,1,0:T(8,128)(2,1)S(1)}, u32[]{:S(2)}, u32[]{:S(2)}) collective-permute-start(bf16[2,64,512]{2,1,0:T(8,128)(2,1)S(1)} %get-tuple-element.197), channel_id=1, source_target_pairs={{0,6},{2,4},{4,2},{6,0},{1,7},{3,5},{5,3},{7,1},{8,14},{10,12},{12... | collective-permute-start | bytes 393224 | tf_op jit(solution)/shard_map/ppermute | solution.py:193
  138.2 12.9 %collective-permute-start.48 = (bf16[128,512]{1,0:T(8,128)(2,1)S(1)}, bf16[128,512]{1,0:T(8,128)(2,1)S(1)}, u32[]{:S(2)}, u32[]{:S(2)}) collective-permute-start(bf16[128,512]{1,0:T(8,128)(2,1)S(1)} %get-tuple-element.201), channel_id=1, source_target_pairs={{0,16},{8,24},{16,0},{24,8},{1,17},{9,25},{17,1},{25,9},{2,18},{10... | collective-permute-start | bytes 393224 | tf_op jit(solution)/shard_map/ppermute | solution.py:190
  139.1 12.1 %collective-permute-start.49 = (bf16[128,512]{1,0:T(8,128)(2,1)S(1)}, bf16[128,512]{1,0:T(8,128)(2,1)S(1)}, u32[]{:S(2)}, u32[]{:S(2)}) collective-permute-start(bf16[128,512]{1,0:T(8,128)(2,1)S(1)} %get-tuple-element.202), channel_id=1, source_target_pairs={{0,8},{8,16},{16,24},{24,0},{1,9},{9,17},{17,25},{25,1},{2,10},{10... | collective-permute-start | bytes 393224 | tf_op jit(solution)/shard_map/ppermute | solution.py:190
  140.2 12.6 %collective-permute-start.51 = (bf16[2,64,512]{2,1,0:T(8,128)(2,1)S(1)}, bf16[2,64,512]{2,1,0:T(8,128)(2,1)S(1)}, u32[]{:S(2)}, u32[]{:S(2)}) collective-permute-start(bf16[2,64,512]{2,1,0:T(8,128)(2,1)S(1)} %get-tuple-element.207), channel_id=1, source_target_pairs={{0,2},{2,0},{4,6},{6,4},{1,3},{3,1},{5,7},{7,5},{8,10},{10,8},{12,... | collective-permute-start | bytes 393224 | tf_op jit(solution)/shard_map/ppermute | solution.py:193
  140.2 12.6 %collective-permute-start.52 = (bf16[2,64,512]{2,1,0:T(8,128)(2,1)S(1)}, bf16[2,64,512]{2,1,0:T(8,128)(2,1)S(1)}, u32[]{:S(2)}, u32[]{:S(2)}) collective-permute-start(bf16[2,64,512]{2,1,0:T(8,128)(2,1)S(1)} %get-tuple-element.208), channel_id=1, source_target_pairs={{0,4},{2,6},{4,0},{6,2},{1,5},{3,7},{5,1},{7,3},{8,12},{10,14},{12... | collective-permute-start | bytes 393224 | tf_op jit(solution)/shard_map/ppermute | solution.py:193
  151.2 18.5 %collective-permute-start.50 = (bf16[128,1024]{1,0:T(8,128)(2,1)S(1)}, bf16[128,1024]{1,0:T(8,128)(2,1)S(1)}, u32[]{:S(2)}, u32[]{:S(2)}) collective-permute-start(bf16[128,1024]{1,0:T(8,128)(2,1)S(1)} %get-tuple-element.204), channel_id=1, source_target_pairs={{0,1},{1,0},{2,3},{3,2},{4,5},{5,4},{6,7},{7,6},{8,9},{9,8},{10,11... | collective-permute-start | bytes 786440 | tf_op jit(solution)/shard_map/ppermute | solution.py:598
  153.5 13.6 %collective-permute-start.55 = (bf16[128,512]{1,0:T(8,128)(2,1)S(1)}, bf16[128,512]{1,0:T(8,128)(2,1)S(1)}, u32[]{:S(2)}, u32[]{:S(2)}) collective-permute-start(bf16[128,512]{1,0:T(8,128)(2,1)S(1)} %get-tuple-element.212), channel_id=1, source_target_pairs={{0,16},{8,24},{16,0},{24,8},{1,17},{9,25},{17,1},{25,9},{2,18},{10... | collective-permute-start | bytes 393224 | tf_op jit(solution)/shard_map/ppermute | solution.py:190
  155.4 11.8 %collective-permute-start.56 = (bf16[128,512]{1,0:T(8,128)(2,1)S(1)}, bf16[128,512]{1,0:T(8,128)(2,1)S(1)}, u32[]{:S(2)}, u32[]{:S(2)}) collective-permute-start(bf16[128,512]{1,0:T(8,128)(2,1)S(1)} %get-tuple-element.213), channel_id=1, source_target_pairs={{0,8},{8,16},{16,24},{24,0},{1,9},{9,17},{17,25},{25,1},{2,10},{10... | collective-permute-start | bytes 393224 | tf_op jit(solution)/shard_map/ppermute | solution.py:190
  (40 other events, 321.3 us)

commit v7 on v5

--- a/solution.py
+++ b/solution.py
@@ -216,7 +216,7 @@
     x_pack = call(
         pack_body, [arr((toks + extra, width))] * groups, [tokens, routes.reshape(1, toks)]
     )
-    x_got = [x_pack[0]] + [shift(x_pack[step], step) for step in range(1, groups)]
+    x_near = {step: shift(x_pack[step], step) for step in (1, 3)}
 
     def slots_row(line):
         first = lax.broadcasted_iota(jnp.int32, (toks, toks), 0)
@@ -232,52 +232,71 @@
         row = lax.broadcasted_iota(jnp.int32, (slot_total, toks), 0)
         return jnp.where(row == jnp.broadcast_to(slot, (slot_total, toks)), 1.0, 0.0).astype(BF16)
 
-    def send_rows(pick, rows, group, out_refs):
+    def send_rows(pick, rows, group, out_refs, halved=False):
         sent = mm(pick, rows).astype(BF16)
         parity, place = lax.rem(group, 2), lax.div(group, 2)
         rows_at = pl.ds(pl.multiple_of(place * cap, cap), cap)
         for bits in range(owners):
             for i in range(local):
                 at = bits * held + i * cap
-                out_refs[bits][parity, i, rows_at, :] = sent[at : at + cap]
+                if halved:
+                    out_refs[bits][i, rows_at, :] = sent[at : at + cap]
+                else:
+                    out_refs[bits][parity, i, rows_at, :] = sent[at : at + cap]
+
+    def dispatch_x(x_ref, step, slot_ref, out_refs):
+        group = group_at(-step)
+        slot = slots_row(x_ref[toks : toks + extra, 0:toks][0:1].astype(F32))
+        slot_ref[pl.ds(group * 8, 8), :] = jnp.broadcast_to(slot, (8, toks))
+        send_rows(picker(slot), x_ref[0:toks, :], group, out_refs, halved=True)
 
     message = arr((2, local, pair_rows, width))
-
-    def weigh_body(x_ref, cot_ref, score_ref, *outs):
-        d_refs, (line_ref, mix_ref, weighted_ref) = outs[:groups], outs[groups:]
-        line_ref[...] = x_ref[...]
+    half_message = arr((local, pair_rows, width))
+    slot_rows = arr((groups * 8, toks), jnp.int32)
+
+    def weigh_body(cot_ref, score_ref, weighted_ref, mix_ref):
         score = score_ref[...]
         mix = score[:, 0:1] / jnp.sum(score, axis=1, keepdims=True)
         mix_ref[...] = jnp.broadcast_to(mix, mix_ref.shape)
         weighted_ref[...] = (mix * cot_ref[...].astype(F32)).astype(BF16)
+
+    weighted, mix_wide = call(
+        weigh_body, [arr((toks, model_width)), arr((toks, 128), F32)], [cotangent, scores]
+    )
+
+    def other_half_body(one_ref, three_ref, kept_ref, *outs):
+        send_refs, slot_ref, passed_ref = outs[:owners], outs[owners], outs[owners + 1]
+        slot_ref[...] = jnp.zeros(slot_ref.shape, jnp.int32)
+        dispatch_x(one_ref, 1, slot_ref, send_refs)
+        dispatch_x(three_ref, 3, slot_ref, send_refs)
+        passed_ref[...] = kept_ref[...]
+
+    got = call(
+        other_half_body,
+        [half_message] * owners + [slot_rows, arr((toks + extra, width))],
+        [x_near[1], x_near[3], x_pack[2]],
+        flops=groups * slot_total * toks * width,
+    )
+    other_send, other_slots, x_far = got[:owners], got[owners], shift(got[owners + 1], 2)
+    other_x = [other_send[0]] + [swap(other_send[bits], bits) for bits in range(1, owners)]
+
+    def own_half_body(own_ref, far_ref, before_ref, weighted_ref, _, *outs):
+        send_refs, slot_ref, d_refs = outs[:owners], outs[owners], outs[owners + 1 :]
+        slot_ref[...] = before_ref[...]
+        dispatch_x(own_ref, 0, slot_ref, send_refs)
+        dispatch_x(far_ref, 2, slot_ref, send_refs)
         for step in range(groups):
             d_refs[step][...] = weighted_ref[:, columns_at(step)]
 
     got = call(
-        weigh_body,
-        [arr((toks, width))] * groups + [arr((toks + extra, width)), arr((toks, 128), F32)],
-        [x_got[1], cotangent, scores],
-        scratch=[pltpu.VMEM((toks, model_width), BF16)],
-    )
-    d_pack, (x_first, mix_wide) = got[:groups], got[groups:]
+        own_half_body,
+        [half_message] * owners + [slot_rows] + [arr((toks, width))] * groups,
+        [x_pack[0], x_far, other_slots, weighted, other_x[1]],
+        flops=groups * slot_total * toks * width,
+    )
+    own_send, slots, d_pack = got[:owners], got[owners], got[owners + 1 :]
+    own_x = [own_send[0]] + [swap(own_send[bits], bits) for bits in range(1, owners)]
     d_got = [d_pack[0]] + [shift(d_pack[step], step) for step in range(1, groups)]
-
-    def dispatch_x_body(*refs):
-        x_refs, send_refs, slot_ref = refs[:groups], refs[groups:-1], refs[-1]
-        for step in range(groups):
-            group = group_at(-step)
-            slot = slots_row(x_refs[step][toks : toks + extra, 0:toks][0:1].astype(F32))
-            slot_ref[pl.ds(group * 8, 8), :] = jnp.broadcast_to(slot, (8, toks))
-            send_rows(picker(slot), x_refs[step][0:toks, :], group, send_refs)
-
-    got = call(
-        dispatch_x_body,
-        [message] * owners + [arr((groups * 8, toks), jnp.int32)],
-        [x_got[0], x_first, *x_got[2:]],
-        flops=2 * groups * slot_total * toks * width,
-    )
-    x_send, slots = got[:owners], got[owners]
-    rows_x = [x_send[0]] + [swap(x_send[bits], bits) for bits in range(1, owners)]
 
     full = pl.BlockSpec(memory_space=pltpu.VMEM)
     piece = arr((block, units))
@@ -299,27 +318,32 @@
     part, pair, total, final, near, far = {}, {}, {}, {}, {}, {}
 
     def first_body(*refs):
-        x_refs, w_refs = refs[:owners], refs[owners : owners + 2]
-        d_refs, slot_ref = refs[owners + 2 : owners + 2 + groups], refs[owners + 2 + groups]
-        outs = refs[owners + 3 + groups :]
-        pack_rows(outs[2], x_refs)
+        own_refs, other_refs, rest = refs[:owners], refs[owners : 2 * owners], refs[2 * owners :]
+        w_refs, d_refs, outs = rest[:2], rest[2:4], rest[4:]
+        outs[3][...], outs[4][...] = d_refs[0][...], d_refs[1][...]
+        parity = lax.rem(lax.axis_index("dp"), 2)
+        for half, half_refs in ((parity, own_refs), (1 - parity, other_refs)):
+            for i in experts:
+                for bits in range(owners):
+                    at = slice(bits * pair_rows, (bits + 1) * pair_rows)
+                    outs[2][half, i, at, :] = half_refs[bits][i]
         for out, w_ref in zip(outs[:2], w_refs):
             out[...] = mm(outs[2][0, 0], w_ref[0]).astype(BF16)
+
+    part[0], part[1], packed_x, d_got[1], d_got[3] = call(
+        first_body,
+        [piece, piece, packed] + [arr((toks, width))] * 2,
+        [*own_x, *other_x, w_gate, w_up, d_got[1], d_got[3]],
+        flops=2 * piece_flops,
+    )
+    near[0], near[1] = line_hop(part[0], inward), line_hop(part[1], inward)
+
+    def dispatch_d_body(*refs):
+        d_refs, slot_ref, out_refs = refs[:groups], refs[groups], refs[groups + 1 :]
         for step in range(groups):
             group = group_at(-step)
             slot = slot_ref[pl.ds(group * 8, 8), :][0:1]
-            send_rows(picker(slot), d_refs[step][...], group, outs[3:])
-
-    got = call(
-        first_body,
-        [piece, piece, packed] + [message] * owners,
-        [*rows_x, w_gate, w_up, *d_got, slots],
-        flops=2 * piece_flops + dispatch_flops,
-    )
-    part[0], part[1], packed_x = got[:3]
-    d_send = got[3:]
-    near[0], near[1] = line_hop(part[0], inward), line_hop(part[1], inward)
-    rows_d = [d_send[0]] + [swap(d_send[bits], bits) for bits in range(1, owners)]
+            send_rows(picker(slot), d_refs[step][...], group, out_refs)
 
     def at_end():
         place = lax.axis_index("dp")
@@ -330,7 +354,7 @@
 
     count = len(order)
 
-    def slot_call(t, rows=None, unpacked=None):
+    def slot_call(t, rows=None, unpacked=None, also=None):
         take, cross, done = t < count, 0 <= t - 2 < count, 0 <= t - 4 < count
         ahead = t + 2 < count
         ins, specs, outs = [near[t]], [full], []
@@ -358,6 +382,10 @@
             ins += unpacked
             specs += [full] * owners
             outs.append(packed)
+        if also is not None:
+            ins += also[1]
+            specs += [full] * len(also[1])
+            outs += also[2]
         ins_count = len(ins)
 
         def body(*refs):
@@ -370,7 +398,8 @@
                 total_ref = right.pop(0)
                 total_ref[...] = plus(left.pop(0), left.pop(0))
             if done:
-                right.pop(0)[...] = jnp.where(at_end(), got_ref[...], left.pop(0)[...])
+                final_ref = right.pop(0)
+                final_ref[...] = jnp.where(at_end(), got_ref[...], left.pop(0)[...])
             if ahead:
                 rows_ref, w_ref, part_ref = left.pop(0), left.pop(0), right.pop(0)
                 product = mm_nt if kind == "b" else mm
@@ -379,6 +408,8 @@
                     right.pop(0)[...] = jnp.where(at_end(), part_ref[...], total_ref[...])
             if unpacked is not None:
                 pack_rows(right.pop(0), left)
+            if also is not None:
+                also[0](*left, *right, *([total_ref, final_ref] if done else []))
 
         got = list(call(body, outs, ins, specs=specs, flops=piece_flops if ahead else 0))
         if take:
@@ -394,15 +425,17 @@
             near[t + 2] = line_hop(got.pop(0), inward + outward)
         elif ahead:
             near[t + 2] = line_hop(part[t + 2], inward)
-        elif cross:
-            near[t + 2] = line_hop(total[t - 2], outward)
         return got
 
-    for t in range(3):
+    d_send = slot_call(
+        0, packed_x, also=(dispatch_d_body, [*d_got, slots], [message] * owners)
+    )
+    rows_d = [d_send[0]] + [swap(d_send[bits], bits) for bits in range(1, owners)]
+    for t in range(1, 5):
         slot_call(t, packed_x)
-    (packed_d,) = slot_call(3, packed_x, unpacked=rows_d)
-    for t in range(4, count):
-        slot_call(t, packed_x if t + 2 < 2 * 2 * local else packed_d)
+    (packed_d,) = slot_call(5, packed_x, unpacked=rows_d)
+    for t in range(6, count - 1):
+        slot_call(t, packed_d)
 
     def spread(refs, half, i, value):
         for bits in range(owners):
@@ -412,32 +445,72 @@
             else:
                 refs[bits][half, i] = rows
 
-    acts = arr((half_rows, units))
+    assert local == 2
+    acts, two_pieces = arr((half_rows, units)), arr((2, block, units))
+
+    last_done = order[4 * local - 1]
 
     def out_body(*refs):
-        w_ref, outs = refs[4 * local], refs[4 * local + 1 :]
-        hidden_refs, out_refs = outs[:2], outs[2:]
+        w_ref, outs = refs[4 * local - 1], refs[4 * local + 1 :]
+        hidden_refs, (give_ref, keep_ref), (two_ref, total_ref, final_ref) = (
+            outs[:2],
+            outs[2:-3],
+            outs[-3:],
+        )
+        mine = lax.axis_index("tensor")
+        two_ref[0], two_ref[1] = refs[4 * local][...], total_ref[...]
+        pieces = [*refs[: 4 * local - 1], final_ref]
         for half in halves:
             for i in experts:
                 at = 2 * (half * local + i)
-                gate, up = refs[at][...].astype(F32), refs[at + 1][...].astype(F32)
+                gate, up = pieces[at][...].astype(F32), pieces[at + 1][...].astype(F32)
                 rows = (gate * jax.nn.sigmoid(gate) * up).astype(BF16)
                 hidden_refs[half][i * block : (i + 1) * block, :] = rows
-                spread(out_refs, half, i, mm(rows, w_ref[i]).astype(BF16))
-
-    got = call(
-        out_body,
-        [acts, acts] + [message] * owners,
-        [final[name] for name in order[: 4 * local]] + [w_down],
-        flops=2 * local * piece_flops,
-    )
-    hidden, out_send = got[:2], got[2:]
-    out_got = [out_send[0]] + [swap(out_send[bits], bits) for bits in range(1, owners)]
-
-    for t in range(count, count + 4):
-        slot_call(t)
-
-    half_message = arr((local, pair_rows, width))
+                result = mm(rows, w_ref[i]).astype(BF16)
+                left, right = result[:, :part_cols], result[:, part_cols:]
+                give_ref[half, i] = jnp.where(mine == 0, right, left)
+                keep_ref[half, i] = jnp.where(mine == 0, left, right)
+
+    part_cols = width // 2
+    part_rows = arr((2, local, block, part_cols))
+    assert order[count - 1 - 4] == last_done
+    got = slot_call(
+        count - 1,
+        also=(
+            out_body,
+            [final[name] for name in order[: 4 * local - 1]] + [w_down, total[count - 4]],
+            [acts, acts] + [part_rows] * 2 + [two_pieces],
+        ),
+    )
+    hidden, out_send, even_total = got[:2], got[2:-1], got[-1]
+    even_back = line_hop(even_total, outward)
+    part_message = arr((2, local, pair_rows, part_cols))
+
+    def across(value):
+        return lax.ppermute(value, "tensor", [(0, 1), (1, 0)])
+
+    def part_body(keep_ref, got_ref, *out_refs):
+        for half in halves:
+            for i in experts:
+                for bits in range(owners):
+                    at = slice(bits * pair_rows, (bits + 1) * pair_rows)
+                    out_refs[bits][half, i] = (
+                        keep_ref[half, i, at, :].astype(F32) + got_ref[half, i, at, :].astype(F32)
+                    ).astype(BF16)
+
+    out_sum = call(part_body, [part_message] * owners, [out_send[1], across(out_send[0])])
+    out_got = [out_sum[0]] + [swap(out_sum[bits], bits) for bits in range(1, owners)]
+
+    def cross_body(*refs):
+        for n in range(2):
+            refs[4][n] = plus(refs[2 * n], refs[2 * n + 1])
+
+    (odd_total,) = call(
+        cross_body,
+        [two_pieces],
+        [pair[count - 2], far[count - 2], pair[count - 1], far[count - 1]],
+    )
+    odd_back = line_hop(odd_total, outward)
 
     def combined(slot_ref, group, block_of):
         place = group // 2 * cap
@@ -449,105 +522,141 @@
         pick = picker(slot_ref[group * 8 : group * 8 + 1, :])
         return mm_tn(pick, jnp.concatenate(rows, axis=0)).astype(BF16)
 
-    def in_call(half):
-        ins = [final[kind, half, i] for i in experts for kind in "gub"] + [w_gate, w_up]
-        count = len(ins)
-
-        def body(*refs):
-            gate_w, up_w = refs[count - 2], refs[count - 1]
-            act_refs, in_refs = refs[count : count + 2], refs[count + 2 :]
-            for i in experts:
-                gate, up, grad = (refs[3 * i + n][...].astype(F32) for n in range(3))
-                rows = slice(i * block, (i + 1) * block)
-                sigma = jax.nn.sigmoid(gate)
-                act_gate = (grad * up * sigma * (1.0 + gate * (1.0 - sigma))).astype(BF16)
-                act_up = (grad * (gate * sigma)).astype(BF16)
-                act_refs[0][rows, :] = act_gate
-                act_refs[1][rows, :] = act_up
-                into = mm_nt(act_gate, gate_w[i]) + mm_nt(act_up, up_w[i])
-                spread(in_refs, None, i, into.astype(BF16))
-
-        got = call(
-            body, [acts, acts] + [half_message] * owners, ins, flops=4 * piece_flops
-        )
-        sent = got[2:]
-        return got[:2], [sent[0]] + [swap(sent[bits], bits) for bits in range(1, owners)]
-
-    acts0, in_got0 = in_call(0)
-    acts1, in_got1 = in_call(1)
-
-    def tokens_body(*refs):
-        o_refs, i_refs, slot_ref = refs[:owners], refs[owners : 2 * owners], refs[2 * owners]
-        outs = refs[2 * owners + 2 :]
-        sum_ref = refs[-1]
+    def into_rows(refs, grad_refs, gate_w, up_w, act_refs, in_refs):
+        for i in experts:
+            gate, up = refs[2 * i][...].astype(F32), refs[2 * i + 1][...].astype(F32)
+            grad = jnp.where(at_end(), grad_refs[1][i], grad_refs[0][i]).astype(F32)
+            rows = slice(i * block, (i + 1) * block)
+            sigma = jax.nn.sigmoid(gate)
+            act_gate = (grad * up * sigma * (1.0 + gate * (1.0 - sigma))).astype(BF16)
+            act_up = (grad * (gate * sigma)).astype(BF16)
+            act_refs[0][rows, :] = act_gate
+            act_refs[1][rows, :] = act_up
+            into = mm_nt(act_gate, gate_w[i]) + mm_nt(act_up, up_w[i])
+            spread(in_refs, None, i, into.astype(BF16))
+
+    def gate_up(half):
+        return [final[kind, half, i] for i in experts for kind in "gu"]
+
+    def in_even_body(*refs):
+        left = list(refs)
+
+        def several(n):
+            taken = left[:n]
+            del left[:n]
+            return taken
+
+        gu_refs, grad_refs, w_refs = several(2 * local), several(2), several(2)
+        o_refs, (slot_ref,) = several(owners), several(1)
+        act_refs, in_refs, tok_refs, (sum_ref,) = *(several(n) for n in (2, owners, groups)), left
+        into_rows(gu_refs, grad_refs, *w_refs, act_refs, in_refs)
         for group in range(groups):
             sum_ref[group] = combined(
                 slot_ref, group, lambda bits, i, rows: o_refs[bits][group % 2, i, rows, :]
             )
-        for group in range(0, groups, 2):
-            outs[groups][group // 2] = combined(
-                slot_ref, group, lambda bits, i, rows: i_refs[bits][i, rows, :]
-            )
         for step in range(groups):
-            outs[step][...] = sum_ref[group_at(-step)]
+            tok_refs[step][...] = sum_ref[group_at(-step)]
 
     got = call(
-        tokens_body,
-        [arr((toks, width))] * groups + [arr((groups // 2, toks, width))],
-        [*out_got, *in_got0, slots, acts1[0]],
-        scratch=[pltpu.VMEM((groups, toks, width), BF16)],
-        flops=2 * dispatch_flops,
-    )
-    out_tok, in_even = got[:groups], got[groups]
+        in_even_body,
+        [acts, acts] + [half_message] * owners + [arr((toks, part_cols))] * groups,
+        [*gate_up(0), even_total, even_back, w_gate, w_up, *out_got, slots],
+        scratch=[pltpu.VMEM((groups, toks, part_cols), BF16)],
+        flops=4 * local * piece_flops + dispatch_flops,
+    )
+    acts0, out_tok = got[:2], got[2 + owners :]
+    in_got0 = [got[2]] + [swap(got[2 + bits], bits) for bits in range(1, owners)]
     out_chunk = [out_tok[0]] + [shift(out_tok[step], -step) for step in range(1, groups)]
 
-    def in_tokens_body(*refs):
-        i_refs, even_ref, slot_ref = refs[:owners], refs[owners], refs[owners + 1]
-        sum_ref = refs[-1]
-        for group in range(groups):
-            if group % 2 == 0:
-                sum_ref[group] = even_ref[group // 2]
-            else:
-                sum_ref[group] = combined(
-                    slot_ref, group, lambda bits, i, rows: i_refs[bits][i, rows, :]
-                )
-        for step in range(groups):
-            refs[owners + 2 + step][...] = sum_ref[group_at(-step)]
-
-    in_tok = call(
-        in_tokens_body,
-        [arr((toks, width))] * groups,
-        [*in_got1, in_even, slots],
-        scratch=[pltpu.VMEM((groups, toks, width), BF16)],
-        flops=dispatch_flops,
-    )
-    in_chunk = [in_tok[0]] + [shift(in_tok[step], -step) for step in range(1, groups)]
+    def last_body(*refs):
+        left = list(refs)
+
+        def several(n):
+            taken = left[:n]
+            del left[:n]
+            return taken
+
+        gu_refs, grad_refs = several(2 * local), several(2)
+        (gate_w, up_w), _ = several(2), several(1)
+        act_refs, in_refs = several(2), several(owners)
+        into_rows(gu_refs, grad_refs, gate_w, up_w, act_refs, in_refs)
+
+    got = call(
+        last_body,
+        [acts, acts] + [half_message] * owners,
+        [
+            *gate_up(1),
+            *(odd_total, odd_back, w_gate, w_up),
+            in_got0[1],
+        ],
+        flops=4 * local * piece_flops,
+    )
+    acts1 = got[:2]
+    in_got1 = [got[2]] + [swap(got[2 + bits], bits) for bits in range(1, owners)]
 
     per_part = groups // 2
     part_width = per_part * width
 
-    def assemble_body(*refs):
-        chunk_refs, give_ref, keep_ref, whole_ref = refs[:groups], *refs[groups:]
+    def assemble(chunk_refs, give_ref, keep_ref, whole_ref):
+        cols = chunk_refs[0].shape[1]
         for step in range(groups):
             whole_ref[group_at(step)] = chunk_refs[step][...]
         mine = lax.axis_index("tensor")
         for j in range(per_part):
-            at = slice(j * width, (j + 1) * width)
+            at = slice(j * cols, (j + 1) * cols)
             give_ref[:, at] = whole_ref[(1 - mine) * per_part + j]
             keep_ref[:, at] = whole_ref[mine * per_part + j]
 
-    def assemble(chunks):
-        give, keep = call(
-            assemble_body,
-            [arr((toks, part_width))] * 2,
-            chunks,
-            scratch=[pltpu.VMEM((groups, toks, width), BF16)],
-        )
-        other = lax.ppermute(give, "tensor", [(0, 1), (1, 0)])
-        return keep.astype(F32) + other.astype(F32)
-
-    output = (mix_wide[:, 0:1] * assemble(out_chunk)).astype(BF16)
-    grad_tokens = assemble(in_chunk).astype(BF16)
+    def in_tokens_body(*refs):
+        left = list(refs)
+
+        def several(n):
+            taken = left[:n]
+            del left[:n]
+            return taken
+
+        even_refs, odd_refs, chunk_refs = several(owners), several(owners), several(groups)
+        (slot_ref,), tok_refs, (give_ref, keep_ref, sum_ref, part_ref) = several(1), several(groups), left
+        for group in range(groups):
+            i_refs = odd_refs if group % 2 else even_refs
+            sum_ref[group] = combined(
+                slot_ref, group, lambda bits, i, rows: i_refs[bits][i, rows, :]
+            )
+        for step in range(groups):
+            tok_refs[step][...] = sum_ref[group_at(-step)]
+        assemble(chunk_refs, give_ref, keep_ref, part_ref)
+
+    swapped = [arr((toks, part_width))] * 2
+    whole_rows = [pltpu.VMEM((groups, toks, width), BF16)]
+    got = call(
+        in_tokens_body,
+        [arr((toks, width))] * groups + [arr((toks, per_part * part_cols))] * 2,
+        [*in_got0, *in_got1, *out_chunk, slots],
+        scratch=whole_rows + [pltpu.VMEM((groups, toks, part_cols), BF16)],
+        flops=dispatch_flops,
+    )
+    in_tok, give_out, keep_out = got[:groups], *got[groups:]
+    in_chunk = [in_tok[0]] + [shift(in_tok[step], -step) for step in range(1, groups)]
+
+    def assemble_body(*refs):
+        assemble(refs[:groups], *refs[groups:])
+
+    give_in, keep_in = call(assemble_body, swapped, in_chunk, scratch=whole_rows)
+
+    grad_tokens = (keep_in.astype(F32) + across(give_in).astype(F32)).astype(BF16)
+
+    def output_body(mix_ref, keep_ref, other_ref, out_ref):
+        mine = lax.axis_index("tensor")
+        mix = mix_ref[:, 0:1]
+        for j in range(per_part):
+            at = slice(j * part_cols, (j + 1) * part_cols)
+            for part, ref in ((mine, keep_ref), (1 - mine, other_ref)):
+                start = pl.multiple_of(j * width + part * part_cols, part_cols)
+                out_ref[:, pl.ds(start, part_cols)] = (mix * ref[:, at].astype(F32)).astype(BF16)
+
+    (output,) = call(
+        output_body, [arr((toks, part_width))], [mix_wide, keep_out, across(give_out)]
+    )
 
     def weight_grad(rows, acts, shape, rows_first):
         def body(*refs):

time: 169 us -> 175 us (1.036)
  waiting for transfers between devices: 54.9 us -> 66.6 us
  starting transfers between devices: 92.3 us -> 86.3 us
    ppermute x28 -> x26, waiting for transfers between devices: 17.9 us -> 7.42 us  [line_hop(): return lax.ppermute(value, 'dp', pairs)]
    ppermute x12, waiting for transfers between devices: 21 us -> 30.6 us  [shift(): lax.ppermute(value, 'dp', [(j, (j + step) % groups) for j in range(groups)])]
    ppermute x15 -> x18, waiting for transfers between devices: 12 us -> 18.7 us  [swap(): return lax.ppermute(value, 'expert', [(j, j ^ bits) for j in range(owners)])]
    ppermute x12, starting transfers between devices: 28.5 us -> 22 us  [shift(): lax.ppermute(value, 'dp', [(j, (j + step) % groups) for j in range(groups)])]
    ppermute x2 -> x3, waiting for transfers between devices: 3.98 us -> 9.91 us  [across(): return lax.ppermute(value, 'tensor', [(0, 1), (1, 0)])]
    ppermute x28 -> x26, starting transfers between devices: 51.6 us -> 49.4 us  [line_hop(): return lax.ppermute(value, 'dp', pairs)]
    pallas_call x30 -> x27, Pallas kernels: 14.6 us -> 16 us  [call(): pl.pallas_call(body, out_shape=outs, grid=() if specs is None else (1,),...]
    ppermute x2 -> x3, starting transfers between devices: 2.15 us -> 3.6 us  [across(): return lax.ppermute(value, 'tensor', [(0, 1), (1, 0)])]
  transfers between devices with their start and end apart: 57 -> 59, of which waited for: 22 -> 24; matrix products, arithmetic and copies ran while one was open for 1% -> 0% of each run, Pallas kernels for 8% -> 8%
where the time goes in v7:
time: 175 us
  starting transfers between devices  86.3 us (49%)
  waiting for transfers between devices  66.6 us (38%)
  Pallas kernels  16 us (9%)
  local copies, waits for them, and re-layouts  3.64 us (2%)
    ppermute x26, starting transfers between devices, line_hop(): return lax.ppermute(value, 'dp', pairs)  49.4 us
    ppermute x12, waiting for transfers between devices, shift(): lax.ppermute(value, 'dp', [(j, (j + step) % groups) for j in range(groups)])  30.6 us
    ppermute x12, starting transfers between devices, shift(): lax.ppermute(value, 'dp', [(j, (j + step) % groups) for j in range(groups)])  22 us
    ppermute x18, waiting for transfers between devices, swap(): return lax.ppermute(value, 'expert', [(j, j ^ bits) for j in range(owners)])  18.7 us
    pallas_call x27, Pallas kernels, call(): pl.pallas_call(body, out_shape=outs, grid=() if specs is None else (1,),...  16 us
    ppermute x18, starting transfers between devices, swap(): return lax.ppermute(value, 'expert', [(j, j ^ bits) for j in range(owners)])  11.3 us
    ppermute x3, waiting for transfers between devices, across(): return lax.ppermute(value, 'tensor', [(0, 1), (1, 0)])  9.91 us
    ppermute x26, waiting for transfers between devices, line_hop(): return lax.ppermute(value, 'dp', pairs)  7.42 us
  transfers between devices with their start and end apart: 59, of which 24 were waited for; matrix products, arithmetic and copies ran while one was open for 0% of the time, Pallas kernels for 8%

profile of v7, /device:TPU:0, one launch (start us, length us, event | category | flops | bytes accessed | tf_op | source)
XLA Modules:
  0.0 174.6 jit_solution(12392600457514045784)
XLA Ops:
  2.5 3.1 %collective-permute-start = (bf16[144,512]{1,0:T(8,128)(2,1)S(1)}, bf16[144,512]{1,0:T(8,128)(2,1)S(1)}, u32[]{:S(2)}, u32[]{:S(2)}) collective-permute-start(bf16[144,512]{1,0:T(8,128)(2,1)S(1)} %get-tuple-element.118), channel_id=1, source_target_pairs={{0,8},{8,16},{16,24},{24,0},{1,9},{9,17},{17,25},{25,1},{2,10},{10... | collective-permute-start | bytes 442376 | tf_op jit(solution)/shard_map/ppermute | solution.py:190
  7.7 4.7 %collective-permute-done.one_ref = bf16[144,512]{1,0:T(8,128)(2,1)S(1)} collective-permute-done((bf16[144,512]{1,0:T(8,128)(2,1)S(1)}, bf16[144,512]{1,0:T(8,128)(2,1)S(1)}, u32[]{:S(2)}, u32[]{:S(2)}) %collective-permute-start) | collective-permute-done | bytes 147488 | tf_op jit(solution)/shard_map/ppermute | solution.py:190
  19.8 4.0 %collective-permute-done.2.far_ref = bf16[144,512]{1,0:T(8,128)(2,1)S(1)} collective-permute-done((bf16[144,512]{1,0:T(8,128)(2,1)S(1)}, bf16[144,512]{1,0:T(8,128)(2,1)S(1)}, u32[]{:S(2)}, u32[]{:S(2)}) %collective-permute-start.2) | collective-permute-done | bytes 147488 | tf_op jit(solution)/shard_map/ppermute | solution.py:190
  26.0 3.8 %collective-permute-start.10 = (bf16[128,512]{1,0:T(8,128)(2,1)S(1)}, bf16[128,512]{1,0:T(8,128)(2,1)S(1)}, u32[]{:S(2)}, u32[]{:S(2)}) collective-permute-start(bf16[128,512]{1,0:T(8,128)(2,1)S(1)} %get-tuple-element.133), channel_id=1, source_target_pairs={{0,24},{8,0},{16,8},{24,16},{1,25},{9,1},{17,9},{25,17},{2,26},{10... | collective-permute-start | bytes 393224 | tf_op jit(solution)/shard_map/ppermute | solution.py:190
  35.2 2.7 %collective-permute-start.11 = (bf16[256,384]{1,0:T(8,128)(2,1)S(1)}, bf16[256,384]{1,0:T(8,128)(2,1)S(1)}, u32[]{:S(2)}, u32[]{:S(2)}) collective-permute-start(bf16[256,384]{1,0:T(8,128)(2,1)S(1)} %get-tuple-element.134.refs_1_), channel_id=1, source_target_pairs={{0,8},{24,16},{1,9},{25,17},{2,10},{26,18},{3,11},{27,19},{4,12},{... | collective-permute-start | bytes 589832 | tf_op jit(solution)/shard_map/ppermute | solution.py:198
  38.9 4.6 %collective-permute-start.17 = (bf16[256,384]{1,0:T(8,128)(2,1)S(1)}, bf16[256,384]{1,0:T(8,128)(2,1)S(1)}, u32[]{:S(2)}, u32[]{:S(2)}) collective-permute-start(bf16[256,384]{1,0:T(8,128)(2,1)S(1)} %get-tuple-element.148.refs_1_), channel_id=1, source_target_pairs={{0,8},{24,16},{1,9},{25,17},{2,10},{26,18},{3,11},{27,19},{4,12},{... | collective-permute-start | bytes 589832 | tf_op jit(solution)/shard_map/ppermute | solution.py:198
  43.4 2.5 %collective-permute-done.12.refs_6_ = bf16[128,512]{1,0:T(8,128)(2,1)S(1)} collective-permute-done((bf16[128,512]{1,0:T(8,128)(2,1)S(1)}, bf16[128,512]{1,0:T(8,128)(2,1)S(1)}, u32[]{:S(2)}, u32[]{:S(2)}) %collective-permute-start.12) | collective-permute-done | bytes 131104 | tf_op jit(solution)/shard_map/ppermute | solution.py:190
  46.6 6.0 %collective-permute-start.13 = (bf16[256,384]{1,0:T(8,128)(2,1)S(1)}, bf16[256,384]{1,0:T(8,128)(2,1)S(1)}, u32[]{:S(2)}, u32[]{:S(2)}) collective-permute-start(bf16[256,384]{1,0:T(8,128)(2,1)S(1)} %get-tuple-element.141.refs_1_), channel_id=1, source_target_pairs={{0,8},{24,16},{1,9},{25,17},{2,10},{26,18},{3,11},{27,19},{4,12},{... | collective-permute-start | bytes 589832 | tf_op jit(solution)/shard_map/ppermute | solution.py:198
  58.1 3.7 %collective-permute-start.15 = (bf16[256,384]{1,0:T(8,128)(2,1)S(1)}, bf16[256,384]{1,0:T(8,128)(2,1)S(1)}, u32[]{:S(2)}, u32[]{:S(2)}) collective-permute-start(bf16[256,384]{1,0:T(8,128)(2,1)S(1)} %get-tuple-element.143), channel_id=1, source_target_pairs={{0,8},{24,16},{8,0},{16,24},{1,9},{25,17},{9,1},{17,25},{2,10},{26... | collective-permute-start | bytes 589832 | tf_op jit(solution)/shard_map/ppermute | solution.py:198
  68.6 3.2 %collective-permute-start.25 = (bf16[256,384]{1,0:T(8,128)(2,1)S(1)}, bf16[256,384]{1,0:T(8,128)(2,1)S(1)}, u32[]{:S(2)}, u32[]{:S(2)}) collective-permute-start(bf16[256,384]{1,0:T(8,128)(2,1)S(1)} %get-tuple-element.160), channel_id=1, source_target_pairs={{0,8},{24,16},{8,0},{16,24},{1,9},{25,17},{9,1},{17,25},{2,10},{26... | collective-permute-start | bytes 589832 | tf_op jit(solution)/shard_map/ppermute | solution.py:198
  72.5 4.0 %collective-permute-done.24.refs_10_ = bf16[2,2,64,512]{3,2,1,0:T(8,128)(2,1)S(1)} collective-permute-done((bf16[2,2,64,512]{3,2,1,0:T(8,128)(2,1)S(1)}, bf16[2,2,64,512]{3,2,1,0:T(8,128)(2,1)S(1)}, u32[]{:S(2)}, u32[]{:S(2)}) %collective-permute-start.24) | collective-permute-done | bytes 262176 | tf_op jit(solution)/shard_map/ppermute | solution.py:193
  79.2 3.5 %collective-permute-start.33 = (bf16[256,384]{1,0:T(8,128)(2,1)S(1)}, bf16[256,384]{1,0:T(8,128)(2,1)S(1)}, u32[]{:S(2)}, u32[]{:S(2)}) collective-permute-start(bf16[256,384]{1,0:T(8,128)(2,1)S(1)} %get-tuple-element.179), channel_id=1, source_target_pairs={{0,8},{24,16},{8,0},{16,24},{1,9},{25,17},{9,1},{17,25},{2,10},{26... | collective-permute-start | bytes 589832 | tf_op jit(solution)/shard_map/ppermute | solution.py:198
  84.9 3.7 %collective-permute-start.29 = (bf16[256,384]{1,0:T(8,128)(2,1)S(1)}, bf16[256,384]{1,0:T(8,128)(2,1)S(1)}, u32[]{:S(2)}, u32[]{:S(2)}) collective-permute-start(bf16[256,384]{1,0:T(8,128)(2,1)S(1)} %get-tuple-element.171), channel_id=1, source_target_pairs={{0,8},{24,16},{8,0},{16,24},{1,9},{25,17},{9,1},{17,25},{2,10},{26... | collective-permute-start | bytes 589832 | tf_op jit(solution)/shard_map/ppermute | solution.py:198
  89.7 3.1 %collective-permute-start.35 = (bf16[256,384]{1,0:T(8,128)(2,1)S(1)}, bf16[256,384]{1,0:T(8,128)(2,1)S(1)}, u32[]{:S(2)}, u32[]{:S(2)}) collective-permute-start(bf16[256,384]{1,0:T(8,128)(2,1)S(1)} %get-tuple-element.185), channel_id=1, source_target_pairs={{0,8},{24,16},{8,0},{16,24},{1,9},{25,17},{9,1},{17,25},{2,10},{26... | collective-permute-start | bytes 589832 | tf_op jit(solution)/shard_map/ppermute | solution.py:198
  93.9 2.8 %collective-permute-start.31 = (bf16[256,384]{1,0:T(8,128)(2,1)S(1)}, bf16[256,384]{1,0:T(8,128)(2,1)S(1)}, u32[]{:S(2)}, u32[]{:S(2)}) collective-permute-start(bf16[256,384]{1,0:T(8,128)(2,1)S(1)} %get-tuple-element.175), channel_id=1, source_target_pairs={{0,8},{24,16},{8,0},{16,24},{1,9},{25,17},{9,1},{17,25},{2,10},{26... | collective-permute-start | bytes 589832 | tf_op jit(solution)/shard_map/ppermute | solution.py:198
  97.9 3.5 %collective-permute-done.31.refs_0_ = bf16[256,384]{1,0:T(8,128)(2,1)S(1)} collective-permute-done((bf16[256,384]{1,0:T(8,128)(2,1)S(1)}, bf16[256,384]{1,0:T(8,128)(2,1)S(1)}, u32[]{:S(2)}, u32[]{:S(2)}) %collective-permute-start.31) | collective-permute-done | bytes 196640 | tf_op jit(solution)/shard_map/ppermute | solution.py:198
  108.5 7.2 %collective-permute-done.38.got_ref = bf16[2,2,256,256]{3,2,1,0:T(8,128)(2,1)S(1)} collective-permute-done((bf16[2,2,256,256]{3,2,1,0:T(8,128)(2,1)S(1)}, bf16[2,2,256,256]{3,2,1,0:T(8,128)(2,1)S(1)}, u32[]{:S(2)}, u32[]{:S(2)}) %collective-permute-start.38) | collective-permute-done | bytes 524320 | tf_op jit(solution)/shard_map/ppermute | solution.py:490
  117.7 4.5 %collective-permute-done.40.refs_10_ = bf16[2,2,64,256]{3,2,1,0:T(8,128)(2,1)S(1)} collective-permute-done((bf16[2,2,64,256]{3,2,1,0:T(8,128)(2,1)S(1)}, bf16[2,2,64,256]{3,2,1,0:T(8,128)(2,1)S(1)}, u32[]{:S(2)}, u32[]{:S(2)}) %collective-permute-start.40) | collective-permute-done | bytes 131104 | tf_op jit(solution)/shard_map/ppermute | solution.py:193
  129.9 5.5 %collective-permute-start.52 = (bf16[128,256]{1,0:T(8,128)(2,1)S(1)}, bf16[128,256]{1,0:T(8,128)(2,1)S(1)}, u32[]{:S(2)}, u32[]{:S(2)}) collective-permute-start(bf16[128,256]{1,0:T(8,128)(2,1)S(1)} %get-tuple-element.211), channel_id=1, source_target_pairs={{0,16},{8,24},{16,0},{24,8},{1,17},{9,25},{17,1},{25,9},{2,18},{10... | collective-permute-start | bytes 196616 | tf_op jit(solution)/shard_map/ppermute | solution.py:190
  137.4 4.7 %collective-permute-done.52.refs_10_ = bf16[128,256]{1,0:T(8,128)(2,1)S(1)} collective-permute-done((bf16[128,256]{1,0:T(8,128)(2,1)S(1)}, bf16[128,256]{1,0:T(8,128)(2,1)S(1)}, u32[]{:S(2)}, u32[]{:S(2)}) %collective-permute-start.52) | collective-permute-done | bytes 65568 | tf_op jit(solution)/shard_map/ppermute | solution.py:190
  143.6 4.5 %collective-permute-done.49.refs_6_ = bf16[2,64,512]{2,1,0:T(8,128)(2,1)S(1)} collective-permute-done((bf16[2,64,512]{2,1,0:T(8,128)(2,1)S(1)}, bf16[2,64,512]{2,1,0:T(8,128)(2,1)S(1)}, u32[]{:S(2)}, u32[]{:S(2)}) %collective-permute-start.49) | collective-permute-done | bytes 131104 | tf_op jit(solution)/shard_map/ppermute | solution.py:193
  151.8 5.0 %collective-permute-done.55.refs_1_ = bf16[128,512]{1,0:T(8,128)(2,1)S(1)} collective-permute-done((bf16[128,512]{1,0:T(8,128)(2,1)S(1)}, bf16[128,512]{1,0:T(8,128)(2,1)S(1)}, u32[]{:S(2)}, u32[]{:S(2)}) %collective-permute-start.55) | collective-permute-done | bytes 131104 | tf_op jit(solution)/shard_map/ppermute | solution.py:190
  156.8 5.8 %collective-permute-done.56.refs_2_ = bf16[128,512]{1,0:T(8,128)(2,1)S(1)} collective-permute-done((bf16[128,512]{1,0:T(8,128)(2,1)S(1)}, bf16[128,512]{1,0:T(8,128)(2,1)S(1)}, u32[]{:S(2)}, u32[]{:S(2)}) %collective-permute-start.56) | collective-permute-done | bytes 131104 | tf_op jit(solution)/shard_map/ppermute | solution.py:190
  170.2 2.7 %collective-permute-done.54.other_ref = bf16[128,512]{1,0:T(8,128)(2,1)S(1)} collective-permute-done((bf16[128,512]{1,0:T(8,128)(2,1)S(1)}, bf16[128,512]{1,0:T(8,128)(2,1)S(1)}, u32[]{:S(2)}, u32[]{:S(2)}) %collective-permute-start.54) | collective-permute-done | bytes 131104 | tf_op jit(solution)/shard_map/ppermute | solution.py:490
  (135 shorter events, 75.0 us)
Async XLA Ops:
  2.5 9.8 %collective-permute-start = (bf16[144,512]{1,0:T(8,128)(2,1)S(1)}, bf16[144,512]{1,0:T(8,128)(2,1)S(1)}, u32[]{:S(2)}, u32[]{:S(2)}) collective-permute-start(bf16[144,512]{1,0:T(8,128)(2,1)S(1)} %get-tuple-element.118), channel_id=1, source_target_pairs={{0,8},{8,16},{16,24},{24,0},{1,9},{9,17},{17,25},{25,1},{2,10},{10... | collective-permute-start | bytes 442376 | tf_op jit(solution)/shard_map/ppermute | solution.py:190
  14.4 9.3 %collective-permute-start.2 = (bf16[144,512]{1,0:T(8,128)(2,1)S(1)}, bf16[144,512]{1,0:T(8,128)(2,1)S(1)}, u32[]{:S(2)}, u32[]{:S(2)}) collective-permute-start(bf16[144,512]{1,0:T(8,128)(2,1)S(1)} %get-tuple-element.121), channel_id=1, source_target_pairs={{0,16},{8,24},{16,0},{24,8},{1,17},{9,25},{17,1},{25,9},{2,18},{10... | collective-permute-start | bytes 442376 | tf_op jit(solution)/shard_map/ppermute | solution.py:190
  15.8 10.2 %collective-permute-start.7 = (bf16[2,64,512]{2,1,0:T(8,128)(2,1)S(1)}, bf16[2,64,512]{2,1,0:T(8,128)(2,1)S(1)}, u32[]{:S(2)}, u32[]{:S(2)}) collective-permute-start(bf16[2,64,512]{2,1,0:T(8,128)(2,1)S(1)} %get-tuple-element.130), channel_id=1, source_target_pairs={{0,4},{2,6},{4,0},{6,2},{1,5},{3,7},{5,1},{7,3},{8,12},{10,14},{12... | collective-permute-start | bytes 393224 | tf_op jit(solution)/shard_map/ppermute | solution.py:193
  35.2 10.8 %collective-permute-start.11 = (bf16[256,384]{1,0:T(8,128)(2,1)S(1)}, bf16[256,384]{1,0:T(8,128)(2,1)S(1)}, u32[]{:S(2)}, u32[]{:S(2)}) collective-permute-start(bf16[256,384]{1,0:T(8,128)(2,1)S(1)} %get-tuple-element.134.refs_1_), channel_id=1, source_target_pairs={{0,8},{24,16},{1,9},{25,17},{2,10},{26,18},{3,11},{27,19},{4,12},{... | collective-permute-start | bytes 589832 | tf_op jit(solution)/shard_map/ppermute | solution.py:198
  38.9 14.4 %collective-permute-start.17 = (bf16[256,384]{1,0:T(8,128)(2,1)S(1)}, bf16[256,384]{1,0:T(8,128)(2,1)S(1)}, u32[]{:S(2)}, u32[]{:S(2)}) collective-permute-start(bf16[256,384]{1,0:T(8,128)(2,1)S(1)} %get-tuple-element.148.refs_1_), channel_id=1, source_target_pairs={{0,8},{24,16},{1,9},{25,17},{2,10},{26,18},{3,11},{27,19},{4,12},{... | collective-permute-start | bytes 589832 | tf_op jit(solution)/shard_map/ppermute | solution.py:198
  46.6 11.2 %collective-permute-start.13 = (bf16[256,384]{1,0:T(8,128)(2,1)S(1)}, bf16[256,384]{1,0:T(8,128)(2,1)S(1)}, u32[]{:S(2)}, u32[]{:S(2)}) collective-permute-start(bf16[256,384]{1,0:T(8,128)(2,1)S(1)} %get-tuple-element.141.refs_1_), channel_id=1, source_target_pairs={{0,8},{24,16},{1,9},{25,17},{2,10},{26,18},{3,11},{27,19},{4,12},{... | collective-permute-start | bytes 589832 | tf_op jit(solution)/shard_map/ppermute | solution.py:198
  53.6 9.0 %collective-permute-start.18 = (bf16[256,384]{1,0:T(8,128)(2,1)S(1)}, bf16[256,384]{1,0:T(8,128)(2,1)S(1)}, u32[]{:S(2)}, u32[]{:S(2)}) collective-permute-start(bf16[256,384]{1,0:T(8,128)(2,1)S(1)} %get-tuple-element.149.refs_1_), channel_id=1, source_target_pairs={{0,8},{24,16},{1,9},{25,17},{2,10},{26,18},{3,11},{27,19},{4,12},{... | collective-permute-start | bytes 589832 | tf_op jit(solution)/shard_map/ppermute | solution.py:198
  62.6 9.2 %collective-permute-start.23 = (bf16[2,2,64,512]{3,2,1,0:T(8,128)(2,1)S(1)}, bf16[2,2,64,512]{3,2,1,0:T(8,128)(2,1)S(1)}, u32[]{:S(2)}, u32[]{:S(2)}) collective-permute-start(bf16[2,2,64,512]{3,2,1,0:T(8,128)(2,1)S(1)} %get-tuple-element.157), channel_id=1, source_target_pairs={{0,4},{2,6},{4,0},{6,2},{1,5},{3,7},{5,1},{7,3},{8,12},{10,14},{12... | collective-permute-start | bytes 786440 | tf_op jit(solution)/shard_map/ppermute | solution.py:193
  64.1 12.3 %collective-permute-start.24 = (bf16[2,2,64,512]{3,2,1,0:T(8,128)(2,1)S(1)}, bf16[2,2,64,512]{3,2,1,0:T(8,128)(2,1)S(1)}, u32[]{:S(2)}, u32[]{:S(2)}) collective-permute-start(bf16[2,2,64,512]{3,2,1,0:T(8,128)(2,1)S(1)} %get-tuple-element.158), channel_id=1, source_target_pairs={{0,6},{2,4},{4,2},{6,0},{1,7},{3,5},{5,3},{7,1},{8,14},{10,12},{12... | collective-permute-start | bytes 786440 | tf_op jit(solution)/shard_map/ppermute | solution.py:193
  65.5 11.0 %collective-permute-start.20 = (bf16[256,384]{1,0:T(8,128)(2,1)S(1)}, bf16[256,384]{1,0:T(8,128)(2,1)S(1)}, u32[]{:S(2)}, u32[]{:S(2)}) collective-permute-start(bf16[256,384]{1,0:T(8,128)(2,1)S(1)} %get-tuple-element.151), channel_id=1, source_target_pairs={{0,8},{24,16},{8,0},{16,24},{1,9},{25,17},{9,1},{17,25},{2,10},{26... | collective-permute-start | bytes 589832 | tf_op jit(solution)/shard_map/ppermute | solution.py:198
  68.6 10.2 %collective-permute-start.25 = (bf16[256,384]{1,0:T(8,128)(2,1)S(1)}, bf16[256,384]{1,0:T(8,128)(2,1)S(1)}, u32[]{:S(2)}, u32[]{:S(2)}) collective-permute-start(bf16[256,384]{1,0:T(8,128)(2,1)S(1)} %get-tuple-element.160), channel_id=1, source_target_pairs={{0,8},{24,16},{8,0},{16,24},{1,9},{25,17},{9,1},{17,25},{2,10},{26... | collective-permute-start | bytes 589832 | tf_op jit(solution)/shard_map/ppermute | solution.py:198
  79.2 10.1 %collective-permute-start.33 = (bf16[256,384]{1,0:T(8,128)(2,1)S(1)}, bf16[256,384]{1,0:T(8,128)(2,1)S(1)}, u32[]{:S(2)}, u32[]{:S(2)}) collective-permute-start(bf16[256,384]{1,0:T(8,128)(2,1)S(1)} %get-tuple-element.179), channel_id=1, source_target_pairs={{0,8},{24,16},{8,0},{16,24},{1,9},{25,17},{9,1},{17,25},{2,10},{26... | collective-permute-start | bytes 589832 | tf_op jit(solution)/shard_map/ppermute | solution.py:198
  102.9 12.8 %collective-permute-start.38 = (bf16[2,2,256,256]{3,2,1,0:T(8,128)(2,1)S(1)}, bf16[2,2,256,256]{3,2,1,0:T(8,128)(2,1)S(1)}, u32[]{:S(2)}, u32[]{:S(2)}) collective-permute-start(bf16[2,2,256,256]{3,2,1,0:T(8,128)(2,1)S(1)} %get-tuple-element.193), channel_id=1, source_target_pairs={{0,1},{1,0},{2,3},{3,2},{4,5},{5,4},{6,7},{7,6},{8,9},{9,8},{10,11... | collective-permute-start | bytes 1572872 | tf_op jit(solution)/shard_map/ppermute | solution.py:490
  104.4 13.3 %collective-permute-start.37 = (bf16[2,256,384]{2,1,0:T(8,128)(2,1)S(1)}, bf16[2,256,384]{2,1,0:T(8,128)(2,1)S(1)}, u32[]{:S(2)}, u32[]{:S(2)}) collective-permute-start(bf16[2,256,384]{2,1,0:T(8,128)(2,1)S(1)} %get-tuple-element.191.refs_4_), channel_id=1, source_target_pairs={{8,0},{16,24},{9,1},{17,25},{10,2},{18,26},{11,3},{19,27},{12,4},{... | collective-permute-start | bytes 1179656 | tf_op jit(solution)/shard_map/ppermute | solution.py:198
  107.2 22.7 %collective-permute-start.47 = (bf16[2,256,384]{2,1,0:T(8,128)(2,1)S(1)}, bf16[2,256,384]{2,1,0:T(8,128)(2,1)S(1)}, u32[]{:S(2)}, u32[]{:S(2)}) collective-permute-start(bf16[2,256,384]{2,1,0:T(8,128)(2,1)S(1)} %shard_map.129.refs_4_), channel_id=1, source_target_pairs={{8,0},{16,24},{9,1},{17,25},{10,2},{18,26},{11,3},{19,27},{12,4},{... | collective-permute-start | bytes 1179656 | tf_op jit(solution)/shard_map/ppermute | solution.py:198
  125.1 10.3 %collective-permute-start.42 = (bf16[2,64,512]{2,1,0:T(8,128)(2,1)S(1)}, bf16[2,64,512]{2,1,0:T(8,128)(2,1)S(1)}, u32[]{:S(2)}, u32[]{:S(2)}) collective-permute-start(bf16[2,64,512]{2,1,0:T(8,128)(2,1)S(1)} %get-tuple-element.199), channel_id=1, source_target_pairs={{0,2},{2,0},{4,6},{6,4},{1,3},{3,1},{5,7},{7,5},{8,10},{10,8},{12,... | collective-permute-start | bytes 393224 | tf_op jit(solution)/shard_map/ppermute | solution.py:193
  125.7 17.9 %collective-permute-start.43 = (bf16[2,64,512]{2,1,0:T(8,128)(2,1)S(1)}, bf16[2,64,512]{2,1,0:T(8,128)(2,1)S(1)}, u32[]{:S(2)}, u32[]{:S(2)}) collective-permute-start(bf16[2,64,512]{2,1,0:T(8,128)(2,1)S(1)} %get-tuple-element.200), channel_id=1, source_target_pairs={{0,4},{2,6},{4,0},{6,2},{1,5},{3,7},{5,1},{7,3},{8,12},{10,14},{12... | collective-permute-start | bytes 393224 | tf_op jit(solution)/shard_map/ppermute | solution.py:193
  127.1 16.5 %collective-permute-start.44 = (bf16[2,64,512]{2,1,0:T(8,128)(2,1)S(1)}, bf16[2,64,512]{2,1,0:T(8,128)(2,1)S(1)}, u32[]{:S(2)}, u32[]{:S(2)}) collective-permute-start(bf16[2,64,512]{2,1,0:T(8,128)(2,1)S(1)} %get-tuple-element.201), channel_id=1, source_target_pairs={{0,6},{2,4},{4,2},{6,0},{1,7},{3,5},{5,3},{7,1},{8,14},{10,12},{12... | collective-permute-start | bytes 393224 | tf_op jit(solution)/shard_map/ppermute | solution.py:193
  127.2 10.1 %collective-permute-start.51 = (bf16[128,256]{1,0:T(8,128)(2,1)S(1)}, bf16[128,256]{1,0:T(8,128)(2,1)S(1)}, u32[]{:S(2)}, u32[]{:S(2)}) collective-permute-start(bf16[128,256]{1,0:T(8,128)(2,1)S(1)} %get-tuple-element.210), channel_id=1, source_target_pairs={{0,24},{8,0},{16,8},{24,16},{1,25},{9,1},{17,9},{25,17},{2,26},{10... | collective-permute-start | bytes 196616 | tf_op jit(solution)/shard_map/ppermute | solution.py:190
  129.9 12.2 %collective-permute-start.52 = (bf16[128,256]{1,0:T(8,128)(2,1)S(1)}, bf16[128,256]{1,0:T(8,128)(2,1)S(1)}, u32[]{:S(2)}, u32[]{:S(2)}) collective-permute-start(bf16[128,256]{1,0:T(8,128)(2,1)S(1)} %get-tuple-element.211), channel_id=1, source_target_pairs={{0,16},{8,24},{16,0},{24,8},{1,17},{9,25},{17,1},{25,9},{2,18},{10... | collective-permute-start | bytes 196616 | tf_op jit(solution)/shard_map/ppermute | solution.py:190
  150.6 12.0 %collective-permute-start.56 = (bf16[128,512]{1,0:T(8,128)(2,1)S(1)}, bf16[128,512]{1,0:T(8,128)(2,1)S(1)}, u32[]{:S(2)}, u32[]{:S(2)}) collective-permute-start(bf16[128,512]{1,0:T(8,128)(2,1)S(1)} %get-tuple-element.217), channel_id=1, source_target_pairs={{0,16},{8,24},{16,0},{24,8},{1,17},{9,25},{17,1},{25,9},{2,18},{10... | collective-permute-start | bytes 393224 | tf_op jit(solution)/shard_map/ppermute | solution.py:190
  150.6 12.0 %collective-permute-start.57 = (bf16[128,512]{1,0:T(8,128)(2,1)S(1)}, bf16[128,512]{1,0:T(8,128)(2,1)S(1)}, u32[]{:S(2)}, u32[]{:S(2)}) collective-permute-start(bf16[128,512]{1,0:T(8,128)(2,1)S(1)} %get-tuple-element.218), channel_id=1, source_target_pairs={{0,8},{8,16},{16,24},{24,0},{1,9},{9,17},{17,25},{25,1},{2,10},{10... | collective-permute-start | bytes 393224 | tf_op jit(solution)/shard_map/ppermute | solution.py:190
  162.7 11.1 %collective-permute-start.58 = (bf16[128,1024]{1,0:T(8,128)(2,1)S(1)}, bf16[128,1024]{1,0:T(8,128)(2,1)S(1)}, u32[]{:S(2)}, u32[]{:S(2)}) collective-permute-start(bf16[128,1024]{1,0:T(8,128)(2,1)S(1)} %get-tuple-element.220), channel_id=1, source_target_pairs={{0,1},{1,0},{2,3},{3,2},{4,5},{5,4},{6,7},{7,6},{8,9},{9,8},{10,11... | collective-permute-start | bytes 786440 | tf_op jit(solution)/shard_map/ppermute | solution.py:490
  163.2 9.7 %collective-permute-start.54 = (bf16[128,512]{1,0:T(8,128)(2,1)S(1)}, bf16[128,512]{1,0:T(8,128)(2,1)S(1)}, u32[]{:S(2)}, u32[]{:S(2)}) collective-permute-start(bf16[128,512]{1,0:T(8,128)(2,1)S(1)} %get-tuple-element.214), channel_id=1, source_target_pairs={{0,1},{1,0},{2,3},{3,2},{4,5},{5,4},{6,7},{7,6},{8,9},{9,8},{10,11... | collective-permute-start | bytes 393224 | tf_op jit(solution)/shard_map/ppermute | solution.py:490
  (41 other events, 295.9 us)
